TPU v7x, 32 devices: a whole 2x2x4 slice. The times are simulated.
32 devices in a mesh: fsdp: 16 (over z, y, core), tp: 2 (over x).
Axes of the slice: x: 2, y: 2, z: 4, core: 2. Of those that a mesh axis runs over, the one named last changes fastest.
Arguments:
- tokens: bfloat16 [10240, 1536], P(('fsdp', 'tp')), may hold values from -6 to 6
- seq_lens: int32 [16, 4], P('fsdp'), may hold values from 0 to 512, as said below
- gain_attn: bfloat16 [1536], P('fsdp'), may hold values from 0.5 to 1.5
- gain_mlp: bfloat16 [1536], P('fsdp'), may hold values from 0.5 to 1.5
- w_qkv: bfloat16 [1536, 2048], P('fsdp', 'tp'), may hold values from -0.15625 to 0.15625
- b_qkv: bfloat16 [2, 1024], P('tp', 'fsdp'), may hold values from -3 to 3
- w_out: bfloat16 [1536, 1536], P('tp', 'fsdp'), may hold values from -0.625 to 0.625
- w_gate: bfloat16 [1536, 8960], P('fsdp', 'tp'), may hold values from -0.15625 to 0.15625
- w_up: bfloat16 [1536, 8960], P('fsdp', 'tp'), may hold values from -0.15625 to 0.15625
- w_down: bfloat16 [8960, 1536], P('tp', 'fsdp'), may hold values from -0.0625 to 0.0625
- cotangent: bfloat16 [10240, 1536], P(('fsdp', 'tp')), may hold values from -6 to 6
Outputs:
- out_rows: bfloat16 [10240, 1536], P(('fsdp', 'tp'))
- grad_input: float32 [10240, 1536], P(('fsdp', 'tp'))
- grad_gain_attn: float32 [1536], P(('fsdp', 'tp'))
- grad_gain_mlp: float32 [1536], P(('fsdp', 'tp'))
- grad_w_qkv: float32 [1536, 2048], P('fsdp', 'tp')
- grad_b_qkv: float32 [2, 1024], P('tp', 'fsdp')
- grad_w_out: float32 [1536, 1536], P('tp', 'fsdp')
- grad_w_gate: float32 [1536, 8960], P('fsdp', 'tp')
- grad_w_up: float32 [1536, 8960], P('fsdp', 'tp')
- grad_w_down: float32 [8960, 1536], P('tp', 'fsdp')
Inputs may be any that keep to these rules, and one draw needn't show every extreme that they name: `seq_lens`: in each group the lengths sum to at most 640; the second sequence starts before row 320 of its group and ends after it; the second sequence of some group has exactly 512 tokens.
All inputs are finite; a program needn't handle non-finite values.
Results may differ from a plain program's by a relative error of at most 0.012.
Values may be sent and summed in bfloat16 or wider, within the bound.
No kernel may reach another device: no remote copies, remote signals or barrier semaphores. Data moves between devices by JAX's collectives and lax.ppermute only.
A program may use at most 256 MiB of HBM per device.

v0:
```python
import math

import jax
import jax.numpy as jnp
from jax import lax
from jax.sharding import PartitionSpec as P

HEADS = 12
KV = 2
HD = 128


norm_eps = 1e-06
rope_base = 1000000.0


def group_layout(seq_lens, group_rows):
    places = jnp.arange(group_rows, dtype=jnp.int32)
    slot_ids = jnp.arange(seq_lens.shape[0], dtype=jnp.int32)
    seq_ends = jnp.cumsum(seq_lens)
    seq_starts = seq_ends - seq_lens
    segment = jnp.sum((places[:, None] >= seq_ends[None, :]).astype(jnp.int32), axis=1)
    member = (segment[:, None] == slot_ids[None, :]).astype(jnp.int32)
    position = places - jnp.sum(member * seq_starts[None, :], axis=1)
    allowed = (segment[:, None] == segment[None, :]) & (places[None, :] <= places[:, None])
    valid = (segment < seq_lens.shape[0]).astype(jnp.float32)
    return (position, allowed, valid)


def rope_tables(position):
    half_width = HD // 2
    freqs = jnp.exp(jnp.arange(half_width, dtype=jnp.float32) * (-2.0 * math.log(rope_base) / HD))
    angles = position.astype(jnp.float32)[:, None] * freqs[None, :]
    cosine = jnp.cos(angles)
    sine = jnp.sin(angles)
    return (jnp.concatenate([cosine, cosine], 1), jnp.concatenate([sine, sine], 1))


def rotate(vectors, cosine, sine):
    half_width = vectors.shape[-1] // 2
    turned = jnp.concatenate([-vectors[..., half_width:], vectors[..., :half_width]], -1)
    return vectors * cosine[:, None, :] + turned * sine[:, None, :]


def unrotate(grads, cosine, sine):
    half_width = grads.shape[-1] // 2
    turned = grads * sine[:, None, :]
    return grads * cosine[:, None, :] + jnp.concatenate(
        [turned[..., half_width:], -turned[..., :half_width]], -1
    )


def root_scale(values):
    return lax.rsqrt(jnp.mean(values * values, axis=1, keepdims=True) + norm_eps)


def norm_back(grad_normed, gain, hat_rows, scale_rows):
    scaled = grad_normed * gain[None, :]
    return scale_rows * (scaled - hat_rows * jnp.mean(scaled * hat_rows, axis=1, keepdims=True))


def scaled_scores(query_groups, key_rot, allowed):
    raw_scores = jnp.einsum(
        "qkgd,skd->kgqs", query_groups, key_rot, preferred_element_type=jnp.float32
    ) * HD ** (-0.5)
    return jnp.where(allowed[None, None], raw_scores, -1e30)


def body(
    tokens, seq_lens, gain_attn, gain_mlp, w_qkv, b_qkv, w_out, w_gate, w_up, w_down, cotangent
):
    row_count = tokens.shape[0]
    tp_count = lax.axis_size("tp")
    group_rows = row_count * tp_count
    local_heads = HEADS // tp_count
    local_kv = KV // tp_count
    head_group = HEADS // KV
    query_end = local_heads * HD
    key_end = query_end + local_kv * HD
    full_qkv, full_bias, full_out, full_gate, full_up, full_down, gain_first, gain_second = (
        lax.all_gather(w_qkv, "fsdp", axis=0, tiled=True),
        lax.all_gather(b_qkv, "fsdp", axis=1, tiled=True),
        lax.all_gather(w_out, "fsdp", axis=1, tiled=True),
        lax.all_gather(w_gate, "fsdp", axis=0, tiled=True),
        lax.all_gather(w_up, "fsdp", axis=0, tiled=True),
        lax.all_gather(w_down, "fsdp", axis=1, tiled=True),
        lax.all_gather(gain_attn, "fsdp", axis=0, tiled=True),
        lax.all_gather(gain_mlp, "fsdp", axis=0, tiled=True),
    )
    gain_one = gain_first.astype(jnp.float32)
    gain_two = gain_second.astype(jnp.float32)
    position, allowed, valid = group_layout(seq_lens[0], group_rows)
    local_valid = lax.dynamic_slice_in_dim(valid, lax.axis_index("tp") * row_count, row_count)
    inputs = tokens.astype(jnp.float32)
    scale_one = root_scale(inputs)
    normed_one = (inputs * scale_one * gain_one[None, :]).astype(jnp.bfloat16)
    normed_all = lax.all_gather(normed_one, "tp", axis=0, tiled=True)
    qkv_rows = jnp.dot(normed_all, full_qkv, preferred_element_type=jnp.float32) + full_bias.astype(
        jnp.float32
    )
    cosine, sine = rope_tables(position)
    query_rot = rotate(
        qkv_rows[:, :query_end].reshape(group_rows, local_heads, HD), cosine, sine
    ).astype(jnp.bfloat16)
    query_groups = query_rot.reshape(group_rows, local_kv, head_group, HD)
    key_rot = rotate(
        qkv_rows[:, query_end:key_end].reshape(group_rows, local_kv, HD), cosine, sine
    ).astype(jnp.bfloat16)
    value_rows = qkv_rows[:, key_end:].reshape(group_rows, local_kv, HD).astype(jnp.bfloat16)
    scores = scaled_scores(query_groups, key_rot, allowed)
    top_score = jnp.max(scores, axis=-1, keepdims=True)
    expd = jnp.exp(scores - top_score)
    totals = jnp.sum(expd, axis=-1, keepdims=True)
    probs_low = (expd / totals).astype(jnp.bfloat16)
    log_total = top_score + jnp.log(totals)
    mixed = jnp.einsum("kgqs,skd->qkgd", probs_low, value_rows, preferred_element_type=jnp.float32)
    mixed = mixed.astype(jnp.bfloat16).reshape(group_rows, query_end)
    hidden = inputs + lax.psum_scatter(
        jnp.dot(mixed, full_out, preferred_element_type=jnp.float32),
        "tp",
        scatter_dimension=0,
        tiled=True,
    )
    scale_two = root_scale(hidden)
    normed_two = (hidden * scale_two * gain_two[None, :]).astype(jnp.bfloat16)
    normed_mlp = lax.all_gather(normed_two, "tp", axis=0, tiled=True)
    gate_rows = jnp.dot(normed_mlp, full_gate, preferred_element_type=jnp.float32)
    up_rows = jnp.dot(normed_mlp, full_up, preferred_element_type=jnp.float32)
    sigmoid_gate = jax.nn.sigmoid(gate_rows)
    activated = (gate_rows * sigmoid_gate * up_rows).astype(jnp.bfloat16)
    result = hidden + lax.psum_scatter(
        jnp.dot(activated, full_down, preferred_element_type=jnp.float32).astype(jnp.bfloat16),
        "tp",
        scatter_dimension=0,
        tiled=True,
    ).astype(jnp.float32)
    out_rows = result.astype(jnp.bfloat16)
    out_grad = cotangent * local_valid[:, None].astype(jnp.bfloat16)
    grad_all = lax.all_gather(out_grad, "tp", axis=0, tiled=True)
    back_qkv, back_out, back_gate, back_up, back_down = (
        full_qkv,
        full_out,
        full_gate,
        full_up,
        full_down,
    )
    grad_down = jnp.dot(activated.T, grad_all, preferred_element_type=jnp.float32)
    grad_act = jnp.dot(grad_all, back_down.T, preferred_element_type=jnp.float32)
    grad_gate_rows = (
        grad_act * up_rows * sigmoid_gate * (1.0 + gate_rows * (1.0 - sigmoid_gate))
    ).astype(jnp.bfloat16)
    grad_up_rows = (grad_act * gate_rows * sigmoid_gate).astype(jnp.bfloat16)
    grad_gate = jnp.dot(normed_mlp.T, grad_gate_rows, preferred_element_type=jnp.float32)
    grad_up = jnp.dot(normed_mlp.T, grad_up_rows, preferred_element_type=jnp.float32)
    gate_sum, up_sum, down_sum = (
        lax.psum_scatter(grad_gate, "fsdp", scatter_dimension=0, tiled=True),
        lax.psum_scatter(grad_up, "fsdp", scatter_dimension=0, tiled=True),
        lax.psum_scatter(grad_down, "fsdp", scatter_dimension=1, tiled=True),
    )
    grad_normed_two = lax.psum_scatter(
        jnp.dot(grad_gate_rows, back_gate.T, preferred_element_type=jnp.float32)
        + jnp.dot(grad_up_rows, back_up.T, preferred_element_type=jnp.float32),
        "tp",
        scatter_dimension=0,
        tiled=True,
    )
    hidden_hat = hidden * scale_two
    grad_gain_two = jnp.sum(grad_normed_two * hidden_hat, axis=0)
    grad_hidden = out_grad.astype(jnp.float32) + norm_back(
        grad_normed_two, gain_two, hidden_hat, scale_two
    )
    branch_grad = grad_hidden.astype(jnp.bfloat16)
    branch_all = lax.all_gather(branch_grad, "tp", axis=0, tiled=True)
    grad_out = jnp.dot(mixed.T, branch_all, preferred_element_type=jnp.float32)
    grad_mixed = jnp.dot(branch_all, back_out.T, preferred_element_type=jnp.float32)
    grad_mixed = grad_mixed.astype(jnp.bfloat16).reshape(group_rows, local_kv, head_group, HD)
    probs_again = jnp.exp(scaled_scores(query_groups, key_rot, allowed) - log_total)
    grad_values = jnp.einsum(
        "kgqs,qkgd->skd",
        probs_again.astype(jnp.bfloat16),
        grad_mixed,
        preferred_element_type=jnp.float32,
    )
    grad_probs = jnp.einsum(
        "qkgd,skd->kgqs", grad_mixed, value_rows, preferred_element_type=jnp.float32
    )
    grad_scores = probs_again * (
        grad_probs - jnp.sum(probs_again * grad_probs, axis=-1, keepdims=True)
    )
    grad_scores = grad_scores.astype(jnp.bfloat16)
    grad_query = jnp.einsum(
        "kgqs,skd->qkgd", grad_scores, key_rot, preferred_element_type=jnp.float32
    ) * HD ** (-0.5)
    grad_keys = jnp.einsum(
        "kgqs,qkgd->skd", grad_scores, query_groups, preferred_element_type=jnp.float32
    ) * HD ** (-0.5)
    grad_qkv = jnp.concatenate(
        [
            unrotate(grad_query.reshape(group_rows, local_heads, HD), cosine, sine).reshape(
                group_rows, query_end
            ),
            unrotate(grad_keys, cosine, sine).reshape(group_rows, key_end - query_end),
            grad_values.reshape(group_rows, key_end - query_end),
        ],
        axis=1,
    ).astype(jnp.bfloat16)
    grad_bias = jnp.sum(grad_qkv.astype(jnp.float32), axis=0, keepdims=True)
    grad_qkv_weight = jnp.dot(normed_all.T, grad_qkv, preferred_element_type=jnp.float32)
    qkv_sum, bias_sum, out_sum = (
        lax.psum_scatter(grad_qkv_weight, "fsdp", scatter_dimension=0, tiled=True),
        lax.psum_scatter(grad_bias, "fsdp", scatter_dimension=1, tiled=True),
        lax.psum_scatter(grad_out, "fsdp", scatter_dimension=1, tiled=True),
    )
    grad_normed_one = lax.psum_scatter(
        jnp.dot(grad_qkv, back_qkv.T, preferred_element_type=jnp.float32),
        "tp",
        scatter_dimension=0,
        tiled=True,
    )
    input_hat = inputs * scale_one
    grad_gain_one = jnp.sum(grad_normed_one * input_hat, axis=0)
    grad_inputs = grad_hidden + norm_back(grad_normed_one, gain_one, input_hat, scale_one)
    gain_one_sum, gain_two_sum = (
        lax.psum_scatter(grad_gain_one, ("fsdp", "tp"), scatter_dimension=0, tiled=True),
        lax.psum_scatter(grad_gain_two, ("fsdp", "tp"), scatter_dimension=0, tiled=True),
    )
    return (
        out_rows,
        grad_inputs,
        gain_one_sum,
        gain_two_sum,
        qkv_sum,
        bias_sum,
        out_sum,
        gate_sum,
        up_sum,
        down_sum,
    )


def solution(mesh):
    placed = (
        P(("fsdp", "tp"), None),
        P("fsdp", None),
        P("fsdp"),
        P("fsdp"),
        P("fsdp", "tp"),
        P("tp", "fsdp"),
        P("tp", "fsdp"),
        P("fsdp", "tp"),
        P("fsdp", "tp"),
        P("tp", "fsdp"),
        P(("fsdp", "tp"), None),
    )
    return jax.shard_map(
        body,
        mesh=mesh,
        in_specs=placed,
        out_specs=(
            P(("fsdp", "tp"), None),
            P(("fsdp", "tp"), None),
            P(("fsdp", "tp")),
            P(("fsdp", "tp")),
            P("fsdp", "tp"),
            P("tp", "fsdp"),
            P("tp", "fsdp"),
            P("fsdp", "tp"),
            P("fsdp", "tp"),
            P("tp", "fsdp"),
        ),
        check_vma=False,
    )
```

profile of v0, /device:TPU:0, one launch (start us, length us, event | category | flops | bytes accessed | tf_op | source)
XLA Modules:
  0.0 1968.3 jit_solution(5462378631975796142)
XLA Ops:
  13.8 63.0 %all-reduce.6 = (bf16[1536]{0:T(1024)(128)(2,1)S(1)}, bf16[1024]{0:T(1024)(128)(2,1)S(1)}, bf16[1536]{0:T(1024)(128)(2,1)S(1)}) all-reduce(bf16[1536]{0:T(1024)(128)(2,1)S(1)} %dynamic-update-slice, bf16[1024]{0:T(1024)(128)(2,1)S(1)} %dynamic-update-slice.1, ...), channel_id=1, replica_groups=mesh['fsdp'=16,'tp'=2] {'fsdp'}, use_global_device_ids=true, to_apply=%add | all-reduce | flops 4096 | bytes 16384
  82.7 25.6 %all-gather.10.cloned.1.call-done = bf16[640,1536]{1,0:T(8,128)(2,1)} async-done(((bf16[320,1536]{1,0:T(8,128)(2,1)}), bf16[640,1536]{1,0:T(8,128)(2,1)}) %all-gather.10.cloned.1.call-update) | async-done | bytes 1966096 | tf_op jit(solution)/shard_map/all_gather | solution.py:97
  108.3 47.5 %all-gather.12.cloned.1.call-done = bf16[1536,1024]{1,0:T(8,128)(2,1)} async-done(((bf16[96,1024]{1,0:T(8,128)(2,1)}), bf16[1536,1024]{1,0:T(8,128)(2,1)}) %all-gather.12.cloned.1.call-update) | async-done | bytes 3145744 | tf_op jit(solution)/shard_map/all_gather | solution.py:81
  184.1 15.1 all-gather.14.cloned.1.call-done
  204.5 50.8 %reduce-scatter.13.cloned.1.call-done = f32[320,1536]{1,0:T(8,128)} async-done(((f32[640,1536]{1,0:T(8,128)}), f32[320,1536]{1,0:T(8,128)}) %reduce-scatter.13.cloned.1.call-update) | async-done | bytes 1966096 | tf_op jit(solution)/shard_map/reduce_scatter | solution.py:118
  261.9 28.4 %all-gather.16.cloned.1.call-done = bf16[640,1536]{1,0:T(8,128)(2,1)} async-done(((bf16[320,1536]{1,0:T(8,128)(2,1)}), bf16[640,1536]{1,0:T(8,128)(2,1)}) %all-gather.16.cloned.1.call-update) | async-done | bytes 1966096 | tf_op jit(solution)/shard_map/all_gather | solution.py:126
  290.3 110.6 %all-gather.20.cloned.1.call-done = bf16[1536,4480]{1,0:T(8,128)(2,1)} async-done(((bf16[96,4480]{1,0:T(8,128)(2,1)}), bf16[1536,4480]{1,0:T(8,128)(2,1)}) %all-gather.20.cloned.1.call-update) | async-done | bytes 13762576 | tf_op jit(solution)/shard_map/all_gather | solution.py:85
  400.9 15.8 fusion.60
  416.7 93.1 %all-gather.18.cloned.1.call-done = bf16[1536,4480]{1,0:T(8,128)(2,1)} async-done(((bf16[96,4480]{1,0:T(8,128)(2,1)}), bf16[1536,4480]{1,0:T(8,128)(2,1)}) %all-gather.18.cloned.1.call-update) | async-done | bytes 13762576 | tf_op jit(solution)/shard_map/all_gather | solution.py:84
  509.9 15.5 fusion.59
  525.4 16.5 all-gather.24.cloned.1.call-done
  541.9 110.8 %all-gather.22.cloned.1.call-done = bf16[4480,1536]{0,1:T(8,128)(2,1)} async-done(((bf16[4480,96]{0,1:T(8,128)(2,1)}), bf16[4480,1536]{0,1:T(8,128)(2,1)}) %all-gather.22.cloned.1.call-update) | async-done | bytes 13762576 | tf_op jit(solution)/shard_map/all_gather | solution.py:86
  652.7 22.4 %multiply_convert_fusion = (bf16[640,4480]{1,0:T(8,128)(2,1)}, bf16[640,4480]{1,0:T(8,128)(2,1)S(1)}, bf16[640,4480]{1,0:T(8,128)(2,1)}) fusion(f32[640,4480]{1,0:T(8,128)} %fusion.59, f32[640,4480]{1,0:T(8,128)} %fusion.60, bf16[640,1536]{1,0:T(8,128)(2,1)} %all-gather.24.cloned.1.call-done, bf16[4480,1536]{0,1:T(8,128)(2,1)} %all-gather.22.cloned.1.call-done), kind=kOutput, calls=%fused_computation | convolution fusion | flops 8853913600 | bytes 55869440 | tf_op jit(solution)/shard_map/dot_general | solution.py:148
  675.1 15.9 fusion.61
  691.0 26.6 %convolution_add_fusion = f32[640,1536]{1,0:T(8,128)} fusion(f32[640,1536]{1,0:T(8,128)} %fusion.61, bf16[640,4480]{1,0:T(8,128)(2,1)} %get-tuple-element.21, bf16[1536,4480]{1,0:T(8,128)(2,1)} %all-gather.20.cloned.1.call-done), kind=kOutput, calls=%fused_computation.21 | convolution fusion | flops 8809021440 | bytes 27361280 | tf_op jit(solution)/shard_map/dot_general | solution.py:162
  717.6 50.3 %reduce-scatter.17.cloned.1.call-done = f32[320,1536]{1,0:T(8,128)} async-done(((f32[640,1536]{1,0:T(8,128)}), f32[320,1536]{1,0:T(8,128)}) %reduce-scatter.17.cloned.1.call-update) | async-done | bytes 1966096 | tf_op jit(solution)/shard_map/reduce_scatter | solution.py:160
  771.9 31.7 %all-gather.26.cloned.1.call-done = bf16[640,1536]{1,0:T(8,128)(2,1)} async-done(((bf16[320,1536]{1,0:T(8,128)(2,1)}), bf16[640,1536]{1,0:T(8,128)(2,1)}) %all-gather.26.cloned.1.call-update) | async-done | bytes 1966096 | tf_op jit(solution)/shard_map/all_gather | solution.py:173
  816.2 7.1 fusion
  823.3 10.7 fusion.8
  854.9 15.6 convolution_convert_fusion
  870.6 6.2 fusion.62
  876.8 7.3 fusion.52
  884.2 19.4 fusion.64
  903.7 19.5 fusion.63
  923.2 19.2 fusion.65
  943.9 14.1 reduce-scatter.19.cloned.1.call-done
  960.2 39.8 %all-reduce.5 = (f32[1536]{0:T(1024)S(1)}, f32[1536]{0:T(1024)S(1)}) all-reduce(f32[1536]{0:T(1024)S(1)} %get-tuple-element.12, f32[1536]{0:T(1024)S(1)} %get-tuple-element.10), channel_id=6, replica_groups=mesh['fsdp'=16,'tp'=2] {'fsdp','tp'}, use_global_device_ids=true, to_apply=%region_15.16.clone | all-reduce | flops 3072 | bytes 24576
  1006.8 65.1 %reduce-scatter.23.cloned.1.call-done = f32[768,96]{0,1:T(8,128)} async-done(((f32[768,1536]{0,1:T(8,128)}), f32[768,96]{0,1:T(8,128)}) %reduce-scatter.23.cloned.1.call-update) | async-done | bytes 294928 | tf_op jit(solution)/shard_map/reduce_scatter | solution.py:212
  1071.9 88.7 %reduce-scatter.21.cloned.1.call-done = f32[96,1024]{1,0:T(8,128)} async-done(((f32[1536,1024]{1,0:T(8,128)}), f32[96,1024]{1,0:T(8,128)}) %reduce-scatter.21.cloned.1.call-update) | async-done | bytes 393232 | tf_op jit(solution)/shard_map/reduce_scatter | solution.py:210
  1160.6 267.2 %reduce-scatter.27.cloned.1.call-done = f32[96,4480]{1,0:T(8,128)} async-done(((f32[1536,4480]{1,0:T(8,128)}), f32[96,4480]{1,0:T(8,128)}) %reduce-scatter.27.cloned.1.call-update) | async-done | bytes 1720336 | tf_op jit(solution)/shard_map/reduce_scatter | solution.py:157
  1427.7 266.5 %reduce-scatter.25.cloned.1.call-done = f32[96,4480]{1,0:T(8,128)} async-done(((f32[1536,4480]{1,0:T(8,128)}), f32[96,4480]{1,0:T(8,128)}) %reduce-scatter.25.cloned.1.call-update) | async-done | bytes 1720336 | tf_op jit(solution)/shard_map/reduce_scatter | solution.py:156
  1694.2 267.4 %reduce-scatter.29.cloned.1.call-done = f32[4480,96]{0,1:T(8,128)} async-done(((f32[4480,1536]{0,1:T(8,128)}), f32[4480,96]{0,1:T(8,128)}) %reduce-scatter.29.cloned.1.call-update) | async-done | bytes 1720336 | tf_op jit(solution)/shard_map/reduce_scatter | solution.py:158
  (168 shorter events, 99.0 us)
Async XLA Ops:
  7.2 73.6 %copy-start.26 = (s32[1,4]{1,0:T(1,128)S(1)}, s32[1,4]{1,0:T(1,128)}, u32[]{:S(2)}) copy-start(s32[1,4]{1,0:T(1,128)} %param.12) | copy-start | bytes 52
  7.2 101.1 %all-gather.10.cloned.1.call-start = ((), (), s32[]{:S(2)}) async-start(), calls=%async_computation.10 | async-start | bytes 2949120 | tf_op jit(solution)/shard_map/all_gather | solution.py:97
  11.3 70.2 %copy-start.24 = (f32[320]{0:T(512)}, f32[320]{0:T(512)S(1)}, u32[]{:S(2)}) copy-start(f32[320]{0:T(512)S(1)} %add_rsqrt_fusion.1) | copy-start | bytes 3844
  79.3 76.6 %all-gather.12.cloned.1.call-start = ((), (), s32[]{:S(2)}) async-start(), calls=%async_computation.11 | async-start | bytes 3342336 | tf_op jit(solution)/shard_map/all_gather | solution.py:81
  80.0 119.2 %all-gather.14.cloned.1.call-start = ((), (), s32[]{:S(2)}) async-start(), calls=%async_computation.12 | async-start | bytes 2506752 | tf_op jit(solution)/shard_map/all_gather | solution.py:83
  80.8 174.6 %reduce-scatter.13.cloned.1.call-start = ((), (), s32[]{:S(2)}) async-start(), calls=%async_computation.13 | async-start | bytes 5898240 | tf_op jit(solution)/shard_map/reduce_scatter | solution.py:118
  82.7 79.6 %copy-start.14 = (f32[640,64]{1,0:T(8,128)}, f32[640,64]{1,0:T(8,128)S(1)}, u32[]{:S(2)}) copy-start(f32[640,64]{1,0:T(8,128)S(1)} %get-tuple-element.38) | copy-start | bytes 491524
  82.7 79.6 %copy-start.16 = (f32[640,64]{1,0:T(8,128)}, f32[640,64]{1,0:T(8,128)S(1)}, u32[]{:S(2)}) copy-start(f32[640,64]{1,0:T(8,128)S(1)} %get-tuple-element.37) | copy-start | bytes 491524
  163.1 12.4 copy-start.18
  184.1 15.1 copy-start.27
  204.5 50.9 %copy-start.2 = (bf16[320,1536]{1,0:T(8,128)(2,1)S(1)}, bf16[320,1536]{1,0:T(8,128)(2,1)}, u32[]{:S(2)}) copy-start(bf16[320,1536]{1,0:T(8,128)(2,1)} %param.11) | copy-start | bytes 2949124
  204.5 85.8 %all-gather.16.cloned.1.call-start = ((), (), s32[]{:S(2)}) async-start(), calls=%async_computation.14 | async-start | bytes 2949120 | tf_op jit(solution)/shard_map/all_gather | solution.py:126
  258.5 142.4 %all-gather.20.cloned.1.call-start = ((), (), s32[]{:S(2)}) async-start(), calls=%async_computation.16 | async-start | bytes 14622720 | tf_op jit(solution)/shard_map/all_gather | solution.py:85
  259.1 250.8 %all-gather.18.cloned.1.call-start = ((), (), s32[]{:S(2)}) async-start(), calls=%async_computation.15 | async-start | bytes 14622720 | tf_op jit(solution)/shard_map/all_gather | solution.py:84
  259.8 282.1 %all-gather.24.cloned.1.call-start = ((), (), s32[]{:S(2)}) async-start(), calls=%async_computation.19 | async-start | bytes 2949120 | tf_op jit(solution)/shard_map/all_gather | solution.py:139
  261.1 391.6 %all-gather.22.cloned.1.call-start = ((), (), s32[]{:S(2)}) async-start(), calls=%async_computation.17 | async-start | bytes 14622720 | tf_op jit(solution)/shard_map/all_gather | solution.py:86
  261.8 506.1 %reduce-scatter.17.cloned.1.call-start = ((), (), s32[]{:S(2)}) async-start(), calls=%async_computation.20 | async-start | bytes 5898240 | tf_op jit(solution)/shard_map/reduce_scatter | solution.py:160
  675.1 15.9 copy-start.28
  717.6 86.0 %all-gather.26.cloned.1.call-start = ((), (), s32[]{:S(2)}) async-start(), calls=%async_computation.21 | async-start | bytes 2949120 | tf_op jit(solution)/shard_map/all_gather | solution.py:173
  771.8 170.7 %reduce-scatter.31.cloned.1.call-start = ((), (), s32[]{:S(2)}) async-start(), calls=%async_computation.28 | async-start | bytes 557056
  823.3 10.7 copy-start.11
  823.3 10.7 copy-start.15
  848.8 109.3 %reduce-scatter.19.cloned.1.call-start = ((), (), s32[]{:S(2)}) async-start(), calls=%async_computation.22 | async-start | bytes 5898240 | tf_op jit(solution)/shard_map/reduce_scatter | solution.py:214
  854.9 146.4 %reduce-scatter.15.cloned.1.call-start = ((), (), s32[]{:S(2)}) async-start(), calls=%async_computation.18 | async-start | bytes 2949120 | tf_op jit(solution)/shard_map/reduce_scatter | solution.py:131
  870.5 201.4 %reduce-scatter.23.cloned.1.call-start = ((), (), s32[]{:S(2)}) async-start(), calls=%async_computation.24 | async-start | bytes 5013504 | tf_op jit(solution)/shard_map/reduce_scatter | solution.py:212
  876.8 283.8 %reduce-scatter.21.cloned.1.call-start = ((), (), s32[]{:S(2)}) async-start(), calls=%async_computation.23 | async-start | bytes 6684672 | tf_op jit(solution)/shard_map/reduce_scatter | solution.py:210
  884.1 543.6 %reduce-scatter.27.cloned.1.call-start = ((), (), s32[]{:S(2)}) async-start(), calls=%async_computation.26 | async-start | bytes 29245440 | tf_op jit(solution)/shard_map/reduce_scatter | solution.py:157
  903.6 790.6 %reduce-scatter.25.cloned.1.call-start = ((), (), s32[]{:S(2)}) async-start(), calls=%async_computation.25 | async-start | bytes 29245440 | tf_op jit(solution)/shard_map/reduce_scatter | solution.py:156
  923.2 1038.4 %reduce-scatter.29.cloned.1.call-start = ((), (), s32[]{:S(2)}) async-start(), calls=%async_computation.27 | async-start | bytes 29245440 | tf_op jit(solution)/shard_map/reduce_scatter | solution.py:158
  942.4 15.6 copy-start.3
  942.4 15.6 copy-start.23
  942.4 15.6 copy-start.25
  (16 other events, 47.9 us)
Sparse Core Ops, SparseCore 0:
  79.4 28.8 all-gather.9
  110.6 45.1 all-gather.11
  158.1 41.0 all-gather.13
  204.6 50.7 reduce-scatter.12
  258.6 31.6 all-gather.15
  292.7 108.1 all-gather.19
  403.5 106.3 all-gather.17
  512.0 29.7 all-gather.23
  544.4 108.1 all-gather.21
  717.7 50.1 reduce-scatter.16
  771.9 31.6 all-gather.25
  848.9 55.7 reduce-scatter.30
  907.0 50.9 reduce-scatter.18
  960.7 30.8 reduce-scatter.14
  996.4 75.4 reduce-scatter.22
  1076.3 84.2 reduce-scatter.20
  1165.7 262.0 reduce-scatter.26
  1432.3 261.9 reduce-scatter.24
  1699.5 262.0 reduce-scatter.28
where the time goes:
time: 1970 us
  waiting for transfers between devices  1550 us (79%)
  matrix products  230 us (12%)
  blocking collectives  103 us (5%)
  other arithmetic  42.5 us (2%)
  local copies, waits for them, and re-layouts  23.6 us (1%)
    reduce_scatter x1, waiting for transfers between devices, body(): lax.psum_scatter(grad_down, 'fsdp', scatter_dimension=1, tiled=True)  267 us
    reduce_scatter x1, waiting for transfers between devices, body(): lax.psum_scatter(grad_up, 'fsdp', scatter_dimension=0, tiled=True)  267 us
    reduce_scatter x1, waiting for transfers between devices, body(): lax.psum_scatter(grad_gate, 'fsdp', scatter_dimension=0, tiled=True)  266 us
    all_gather x1, waiting for transfers between devices, body(): lax.all_gather(w_down, 'fsdp', axis=1, tiled=True)  111 us
    all_gather x1, waiting for transfers between devices, body(): lax.all_gather(w_up, 'fsdp', axis=0, tiled=True)  111 us
    unnamed x2, blocking collectives  103 us
    all_gather x1, waiting for transfers between devices, body(): lax.all_gather(w_gate, 'fsdp', axis=0, tiled=True)  93.1 us
    reduce_scatter x1, waiting for transfers between devices, body(): lax.psum_scatter(grad_qkv_weight, 'fsdp', scatter_dimension=0, tiled=True)  88.7 us
  transfers between devices with their start and end apart: 19, of which 17 were waited for; matrix products, arithmetic and copies ran while one was open for 8% of the time, Pallas kernels for 0%

commit v1 on v0

v1 whole, which is shorter than its diff:
```python
import math

import jax
import jax.numpy as jnp
from jax import lax
from jax.experimental import pallas as pl
from jax.experimental.pallas import tpu as pltpu
from jax.sharding import PartitionSpec as P

HEADS = 12
KV = 2
HD = 128

CORE = 1
NEAR = 4
SIDE = 2
LANES = 128
STEP = 320
SCALE = 8

norm_eps = 1e-06
rope_base = 1000000.0


def swap(values, axis, bit):
    count = lax.axis_size(axis)
    return lax.ppermute(values, axis, [(i, i ^ bit) for i in range(count)])


def swap_both(values, evens, odds):
    fsdp, tp = lax.axis_size("fsdp"), lax.axis_size("tp")
    pairs = []
    for f in range(fsdp):
        for t in range(tp):
            axis, bit = odds if f % 2 else evens
            to = (f, t ^ bit) if axis == "tp" else (f ^ bit, t)
            pairs.append((f * tp + t, to[0] * tp + to[1]))
    return lax.ppermute(values, ("fsdp", "tp"), pairs)


def own_bit(axis, bit):
    return lax.rem(lax.div(lax.axis_index(axis), bit), 2)


def far_bits():
    count = lax.axis_size("fsdp")
    bits = []
    bit = count // 2
    while bit >= 8:
        bits.append(bit)
        bit //= 2
    return bits


def choose(flag, first, second):
    return jnp.where(flag == 0, first, second)


def rope_tables(position):
    half_width = HD // 2
    freqs = jnp.exp(jnp.arange(half_width, dtype=jnp.float32) * (-2.0 * math.log(rope_base) / HD))
    angles = position.astype(jnp.float32)[:, None] * freqs[None, :]
    cosine = jnp.cos(angles)
    sine = jnp.sin(angles)
    return (jnp.concatenate([cosine, cosine], 1), jnp.concatenate([sine, -sine], 1))


def unrotate(grads, cosine, sine):
    half_width = grads.shape[-1] // 2
    turned = jnp.concatenate([grads[..., half_width:], grads[..., :half_width]], -1)
    return grads * cosine[:, None, :] + turned * sine[:, None, :]


def root_scale(values):
    return lax.rsqrt(jnp.mean(values * values, axis=1, keepdims=True) + norm_eps)


def norm_back(grad_normed, gain, hat_rows, scale_rows):
    scaled = grad_normed * gain[None, :]
    return scale_rows * (scaled - hat_rows * jnp.mean(scaled * hat_rows, axis=1, keepdims=True))


def segment_of(rows, seq_lens):
    seq_ends = jnp.cumsum(seq_lens)
    seq_starts = seq_ends - seq_lens
    slot_ids = jnp.arange(seq_lens.shape[0], dtype=jnp.int32)
    segment = jnp.sum((rows[:, None] >= seq_ends[None, :]).astype(jnp.int32), axis=1)
    member = (segment[:, None] == slot_ids[None, :]).astype(jnp.int32)
    position = rows - jnp.sum(member * seq_starts[None, :], axis=1)
    return segment, position


def after(values, earlier):
    return lax.optimization_barrier((values, earlier))[0]


def place_blocks(pieces, out_shapes, earlier=()):
    arrays = [array for array, _ in pieces]
    total = sum(len(moves) for _, moves in pieces)
    place = jnp.stack([lax.axis_index("tp"), lax.axis_index("fsdp")]).astype(jnp.int32)

    def kernel(place_ref, *refs):
        ins, outs, sems = refs[: len(arrays)], refs[len(arrays) + len(earlier) : -1], refs[-1]
        copies = []
        for ref, (_, moves) in zip(ins, pieces):
            for index, columns, number, (part, block), there in moves:
                source = ref.at[index]
                if part is None:
                    target = outs[number].at[place_ref[1] ^ block]
                else:
                    target = outs[number].at[place_ref[0] ^ part, place_ref[1] ^ block]
                if columns is not None:
                    source = source.at[:, pl.ds(columns[0], columns[1])]
                    target = target.at[:, pl.ds(there, columns[1])]
                copies.append(pltpu.make_async_copy(source, target, sems.at[len(copies)]))
        for copy in copies:
            copy.start()
        for copy in copies:
            copy.wait()

    size = sum(math.prod(shape) * 2 for shape in out_shapes)
    return pl.pallas_call(
        kernel,
        out_shape=[jax.ShapeDtypeStruct(shape, arrays[0].dtype) for shape in out_shapes],
        in_specs=[pl.BlockSpec(memory_space=pltpu.SMEM)]
        + [pl.BlockSpec(memory_space=pl.ANY)] * (len(arrays) + len(earlier)),
        out_specs=[pl.BlockSpec(memory_space=pltpu.VMEM)] * len(out_shapes),
        scratch_shapes=[pltpu.SemaphoreType.DMA((total,))],
        compiler_params=pltpu.CompilerParams(vmem_limit_bytes=2 * size + (8 << 20)),
        cost_estimate=pl.CostEstimate(flops=0, bytes_accessed=2 * size, transcendentals=0),
    )(place, *arrays, *earlier)


def send_units(shards, quarter):
    units = shards[0].shape[1]
    core, near = own_bit("fsdp", CORE), own_bit("fsdp", NEAR)
    padded = jnp.stack([jnp.pad(shard, ((0, 0), (0, 4 * quarter - units))) for shard in shards])
    low, high = padded[..., : 2 * quarter], padded[..., 2 * quarter :]
    kept, got = choose(core, low, high), swap(choose(core, high, low), "fsdp", CORE)

    def halves(kept, got):
        pair = jnp.stack([kept, got], axis=1)
        low, high = pair[..., :quarter], pair[..., quarter:]
        return choose(near, low, high), choose(near, high, low)

    return kept, got, halves


INNER = [0, CORE, NEAR, NEAR | CORE]


def far_units(quad, low, high):
    pieces = far_gather(quad[low:high])
    return [(p, [rel | INNER[i] for i in range(low, high)]) for rel, p in pieces.items() if rel]


def side_units(pieces):
    arrays = jnp.concatenate([array for array, _ in pieces])
    places = [place | SIDE for _, marks in pieces for place in marks]
    return [(swap(arrays, "fsdp", SIDE), places)]


def part_of(pieces, low, high):
    return [(array[low:high], marks[low:high]) for array, marks in pieces]


def join_units(pieces):
    count = lax.axis_size("fsdp")
    _, block, quarter = pieces[0][0].shape
    moves = [
        (array, [(i, None, 0, (None, place), None) for i, place in enumerate(marks)])
        for array, marks in pieces
    ]
    full = place_blocks(moves, [(count, block, quarter)])[0]
    return full.reshape(count * block, quarter)


def tie(*values):
    leaves, form = jax.tree.flatten(values)
    arrays = [i for i, leaf in enumerate(leaves) if isinstance(leaf, jax.Array)]
    for i, leaf in zip(arrays, lax.optimization_barrier([leaves[i] for i in arrays])):
        leaves[i] = leaf
    return jax.tree.unflatten(form, leaves)


def side_view(grad):
    rows, quarter = grad.shape
    block = rows // lax.axis_size("fsdp")
    side = own_bit("fsdp", SIDE)
    fars = far_bits()
    view = grad.reshape([2] * len(fars) + [2, 2, 2, block, quarter])

    def at(rel, side_rel):
        piece = view
        for bit, flip in zip(fars, rel):
            piece = lax.dynamic_index_in_dim(piece, own_bit("fsdp", bit) ^ flip, 0, keepdims=False)
        piece = lax.dynamic_index_in_dim(piece, side ^ side_rel, 1, keepdims=False)
        return piece.reshape(4, block, quarter)

    return at


def far_codes():
    count = len(far_bits())
    codes = [tuple((code >> (count - 1 - i)) & 1 for i in range(count)) for code in range(2**count)]
    return codes[1:], codes[0]


def add_pair(own, got):
    return slim(wide(own) + wide(got))


def far_sums(pieces):
    for bit in far_bits():
        merged = {}
        for rel in [key for key in pieces if key[0] == 1]:
            got = swap(pieces[rel], "fsdp", bit)
            other = (0,) + rel[1:]
            merged[rel[1:]] = add_pair(pieces[other], got) if other in pieces else got
        pieces = merged
    return pieces[()]


def share_near(total, near):
    view = total.reshape(2, 2, *total.shape[1:])
    keep = lax.dynamic_index_in_dim(view, near, 0, keepdims=False)
    return keep, swap(lax.dynamic_index_in_dim(view, near ^ 1, 0, keepdims=False), "fsdp", NEAR)


def share_cores(pairs, units):
    core, near = own_bit("fsdp", CORE), own_bit("fsdp", NEAR)
    keep, got = jnp.stack([keep for keep, _ in pairs]), jnp.stack([got for _, got in pairs])
    both = jnp.concatenate([choose(near, keep, got), choose(near, got, keep)], axis=3)
    keep = lax.dynamic_index_in_dim(both, core, 1, keepdims=False)
    got = swap(lax.dynamic_index_in_dim(both, core ^ 1, 1, keepdims=False), "fsdp", CORE)
    both = jnp.concatenate([choose(core, keep, got), choose(core, got, keep)], axis=2)
    return [wide(both[i, :, :units]) for i in range(len(pairs))]


def links():
    return [("tp", 1), ("fsdp", SIDE), ("fsdp", NEAR)]


def thirds(width):
    tiles = width // LANES
    cuts = [(tiles + 2 - i) // 3 * LANES for i in range(3)]
    starts = [0, cuts[0], cuts[0] + cuts[1]]
    return list(zip(starts, cuts))


def step_all(parts, marks, step):
    for turn in range(3):
        axis, bit = links()[(turn + step) % 3]
        parts[turn] = jnp.concatenate([parts[turn], swap(parts[turn], axis, bit)])
        marks[turn] = marks[turn] + [
            (part | bit, rel) if axis == "tp" else (part, rel | bit) for part, rel in marks[turn]
        ]


def join_all(parts, others, marks, widths):
    block = parts[0].shape[1]
    count = lax.axis_size("fsdp")
    spans, start = [], 0
    for item in widths:
        spans.append((start, start + item))
        start += item

    def moves_of(marks, start, size):
        moves = []
        for index, mark in enumerate(marks):
            for number, (low, high) in enumerate(spans):
                first, last = max(low, start), min(high, start + size)
                if first < last:
                    moves.append((index, (first - start, last - first), number, mark, first - low))
        return moves

    pieces = []
    for part, other, mark, (start, size) in zip(parts, others, marks, thirds(start)):
        pieces.append((part, moves_of(mark, start, size)))
        mark = [(tp_part, rel | CORE) for tp_part, rel in mark]
        pieces.append((other, moves_of(mark, start, size)))
    fulls = place_blocks(pieces, [(2, count, block, high - low) for low, high in spans])
    return [full.reshape(2, count * block, full.shape[3]) for full in fulls]


def far_gather(values):
    pieces = {0: values}
    for bit in far_bits():
        pieces.update({rel | bit: swap(piece, "fsdp", bit) for rel, piece in list(pieces.items())})
    return pieces


def scatter_step(parts, axes, step):
    results, left = [], []
    for turn, (piece, names) in enumerate(zip(parts, axes)):
        axis, bit = links()[(turn + step) % 3]
        dim = names.index((axis, bit))
        mine = own_bit(axis, bit)
        got = swap(lax.dynamic_index_in_dim(piece, mine ^ 1, dim, keepdims=False), axis, bit)
        results.append((lax.dynamic_index_in_dim(piece, mine, dim, keepdims=False), got))
        left.append(names[:dim] + names[dim + 1 :])
    return results, left


def scatter_small(values):
    flag = own_bit("tp", 1)
    keep = choose(flag, values[0], values[1])
    values = keep + swap(choose(flag, values[1], values[0]), "tp", 1)
    bit = lax.axis_size("fsdp") // 2
    while bit:
        flag = own_bit("fsdp", bit)
        keep = choose(flag, values[:bit], values[bit:])
        values = keep + swap(choose(flag, values[bit:], values[:bit]), "fsdp", bit)
        bit //= 2
    return values[0]


X, Z = ("tp", 1), ("fsdp", NEAR)


def spread_first(rows):
    return jnp.concatenate([rows, swap_both(rows, X, Z)])


def spread_second(rows):
    return swap_both(rows, Z, X)


def both_cores(rows):
    return jnp.concatenate([rows, swap(rows, "fsdp", CORE)])


def wide(values):
    return values.astype(jnp.float32)


def slim(values):
    return values.astype(jnp.bfloat16)


def sum_cores(chunk):
    half = chunk.shape[0] // 2
    return wide(chunk[:half]) + wide(swap(chunk[half:], "fsdp", CORE))


def dot(a, b):
    return jnp.dot(a, b, preferred_element_type=jnp.float32)


def dot_last(a, b):
    return lax.dot_general(a, b, (((1,), (1,)), ((), ())), preferred_element_type=jnp.float32)


def dot_first(a, b):
    return lax.dot_general(a, b, (((0,), (0,)), ((), ())), preferred_element_type=jnp.float32)


def cost(flops, operands, transcendentals=0):
    size = sum(math.prod(v.shape) * v.dtype.itemsize for v in operands)
    return pl.CostEstimate(
        flops=flops // SCALE, bytes_accessed=size // SCALE, transcendentals=transcendentals // SCALE
    )


def project(rows, weights, bias, cosine, sine):
    count, depth = rows.shape
    columns = weights.shape[2]
    tiles = columns // (2 * HD)

    def kernel(rows_ref, weights_ref, bias_ref, cosine_ref, sine_ref, out_ref):
        last = pl.program_id(1) == tiles - 1
        total = jnp.dot(rows_ref[...], weights_ref[0], preferred_element_type=jnp.float32)
        total = total + bias_ref[0].astype(jnp.float32)
        for j in range(2):
            part = total[:, j * HD : (j + 1) * HD]
            cos, sin = cosine_ref[...], sine_ref[...]
            if j == 1:
                cos, sin = jnp.where(last, 1.0, cos), jnp.where(last, 0.0, sin)
            part = part * cos - pltpu.roll(part, HD // 2, 1) * sin
            out_ref[:, j * HD : (j + 1) * HD] = part.astype(out_ref.dtype)

    return pl.pallas_call(
        kernel,
        out_shape=jax.ShapeDtypeStruct((count, KV * columns), jnp.bfloat16),
        grid=(KV, tiles),
        in_specs=[
            pl.BlockSpec((count, depth), lambda t, c: (0, 0)),
            pl.BlockSpec((1, depth, 2 * HD), lambda t, c: (t, 0, c)),
            pl.BlockSpec((1, 1, 2 * HD), lambda t, c: (t, 0, c)),
            pl.BlockSpec((count, HD), lambda t, c: (0, 0)),
            pl.BlockSpec((count, HD), lambda t, c: (0, 0)),
        ],
        out_specs=pl.BlockSpec((count, 2 * HD), lambda t, c: (0, t * tiles + c)),
        compiler_params=pltpu.CompilerParams(vmem_limit_bytes=40 << 20),
        cost_estimate=cost(2 * count * depth * KV * columns, [rows, weights]),
    )(rows, weights, bias[:, None, :], cosine, sine)


def softmax_rows(query, keys, mask):
    scores = lax.dot_general(
        query, keys, (((1,), (1,)), ((), ())), preferred_element_type=jnp.float32
    )
    scores = scores * HD ** (-0.5) + mask
    expd = jnp.exp(scores - jnp.max(scores, axis=1, keepdims=True))
    return expd / jnp.sum(expd, axis=1, keepdims=True)


def head_specs(count, total):
    group = HEADS // KV
    wide = group + 2
    return [
        pl.BlockSpec((count, HD), lambda h: (0, h // group * wide + h % group)),
        pl.BlockSpec((total, HD), lambda h: (0, h // group * 2)),
        pl.BlockSpec((total, HD), lambda h: (0, h // group * 2 + 1)),
        pl.BlockSpec((count, total), lambda h: (0, 0)),
    ]


def attend(turned, keys_values, mask):
    count, total = mask.shape

    def kernel(query_ref, keys_ref, values_ref, mask_ref, out_ref):
        probs = softmax_rows(query_ref[...], keys_ref[...], mask_ref[...])
        out_ref[...] = jnp.dot(
            probs.astype(jnp.bfloat16), values_ref[...], preferred_element_type=jnp.float32
        ).astype(out_ref.dtype)

    return pl.pallas_call(
        kernel,
        out_shape=jax.ShapeDtypeStruct((count, HEADS * HD), jnp.bfloat16),
        grid=(HEADS,),
        in_specs=head_specs(count, total),
        out_specs=pl.BlockSpec((count, HD), lambda h: (0, h)),
        compiler_params=pltpu.CompilerParams(vmem_limit_bytes=40 << 20),
        cost_estimate=cost(
            8 * HEADS * count * total * HD, [turned, keys_values, mask], HEADS * count * total
        ),
    )(turned, keys_values, keys_values, mask)


def attend_back(turned, keys_values, mask, grad_mixed, cosine, sine):
    count, total = mask.shape
    group = HEADS // KV

    def kernel(
        query_ref, keys_ref, values_ref, mask_ref, grad_ref, cosine_ref, sine_ref,
        out_ref, grad_keys_ref, grad_values_ref,
    ):
        query, keys, grad = query_ref[...], keys_ref[...], grad_ref[...]
        probs = softmax_rows(query, keys, mask_ref[...])
        grad_probs = dot_last(grad, values_ref[...])
        inner = jnp.sum(probs * grad_probs, axis=1, keepdims=True)
        grad_scores = (probs * (grad_probs - inner)).astype(jnp.bfloat16)
        grad_values = dot_first(probs.astype(jnp.bfloat16), grad)
        grad_keys = dot_first(grad_scores, query) * HD ** (-0.5)
        first = pl.program_id(0) % group == 0

        @pl.when(first)
        def _():
            grad_keys_ref[...] = grad_keys
            grad_values_ref[...] = grad_values

        @pl.when(jnp.logical_not(first))
        def _():
            grad_keys_ref[...] += grad_keys
            grad_values_ref[...] += grad_values

        part = jnp.dot(grad_scores, keys, preferred_element_type=jnp.float32) * HD ** (-0.5)
        part = part * cosine_ref[...] + pltpu.roll(part, HD // 2, 1) * sine_ref[...]
        out_ref[...] = part.astype(out_ref.dtype)

    return pl.pallas_call(
        kernel,
        out_shape=[
            jax.ShapeDtypeStruct((count, HEADS * HD), jnp.bfloat16),
            jax.ShapeDtypeStruct((total, KV * HD), jnp.float32),
            jax.ShapeDtypeStruct((total, KV * HD), jnp.float32),
        ],
        grid=(HEADS,),
        in_specs=head_specs(count, total)
        + [
            pl.BlockSpec((count, HD), lambda h: (0, h)),
            pl.BlockSpec((count, HD), lambda h: (0, 0)),
            pl.BlockSpec((count, HD), lambda h: (0, 0)),
        ],
        out_specs=[
            pl.BlockSpec((count, HD), lambda h: (0, h)),
            pl.BlockSpec((total, HD), lambda h: (0, h // group)),
            pl.BlockSpec((total, HD), lambda h: (0, h // group)),
        ],
        compiler_params=pltpu.CompilerParams(vmem_limit_bytes=40 << 20),
        cost_estimate=cost(
            20 * HEADS * count * total * HD, [turned, keys_values, mask], HEADS * count * total
        ),
    )(turned, keys_values, keys_values, mask, grad_mixed, cosine, sine)


def gated(rows, w_gate, w_up):
    count, depth = rows.shape
    columns = w_gate.shape[1]

    def kernel(rows_ref, gate_ref, up_ref, gate_out, up_out, act_out):
        block = rows_ref[...]
        gate = jnp.dot(block, gate_ref[...], preferred_element_type=jnp.float32)
        up = jnp.dot(block, up_ref[...], preferred_element_type=jnp.float32)
        gate_out[...] = gate.astype(jnp.bfloat16)
        up_out[...] = up.astype(jnp.bfloat16)
        act_out[...] = (gate * jax.nn.sigmoid(gate) * up).astype(jnp.bfloat16)

    whole = pl.BlockSpec((depth, columns), lambda i: (0, 0))
    part = pl.BlockSpec((STEP, columns), lambda i: (i, 0))
    out = jax.ShapeDtypeStruct((count, columns), jnp.bfloat16)
    return pl.pallas_call(
        kernel,
        out_shape=[out] * 3,
        grid=(count // STEP,),
        in_specs=[pl.BlockSpec((STEP, depth), lambda i: (i, 0)), whole, whole],
        out_specs=[part] * 3,
        compiler_params=pltpu.CompilerParams(vmem_limit_bytes=52 << 20),
        cost_estimate=cost(4 * count * depth * columns, [rows, w_gate, w_up, out, out, out]),
    )(rows, w_gate, w_up)


def gated_back(grad, gate, up, w_gate, w_up, w_down):
    count, depth = grad.shape
    columns = w_gate.shape[1]

    def kernel(grad_ref, gate_ref, up_ref, wg_ref, wu_ref, wd_ref, dg_out, du_out, out):
        gate = gate_ref[...].astype(jnp.float32)
        up = up_ref[...].astype(jnp.float32)
        act = jnp.dot(grad_ref[...], wd_ref[...], preferred_element_type=jnp.float32)
        sigma = jax.nn.sigmoid(gate)
        d_gate = (act * up * sigma * (1.0 + gate * (1.0 - sigma))).astype(jnp.bfloat16)
        d_up = (act * gate * sigma).astype(jnp.bfloat16)
        dg_out[...] = d_gate
        du_out[...] = d_up
        total = dot_last(d_gate, wg_ref[...]) + dot_last(d_up, wu_ref[...])
        out[...] = total.astype(jnp.bfloat16)

    whole = pl.BlockSpec((depth, columns), lambda i: (0, 0))
    part = pl.BlockSpec((STEP, columns), lambda i: (i, 0))
    rows = pl.BlockSpec((STEP, depth), lambda i: (i, 0))
    out = jax.ShapeDtypeStruct((count, columns), jnp.bfloat16)
    return pl.pallas_call(
        kernel,
        out_shape=[out, out, jax.ShapeDtypeStruct((count, depth), jnp.bfloat16)],
        grid=(count // STEP,),
        in_specs=[rows, part, part, whole, whole, whole],
        out_specs=[part, part, rows],
        compiler_params=pltpu.CompilerParams(vmem_limit_bytes=56 << 20),
        cost_estimate=cost(6 * count * depth * columns, [grad, grad, w_gate, w_up, w_down, out, out]),
    )(grad, gate, up, w_gate, w_up, w_down)


def weight_grad(lefts, rights):
    depth, columns = lefts[0].shape[1], rights[0].shape[1]
    tile = 2 * LANES

    def kernel(*refs):
        pairs = len(refs) // 2
        total = dot_first(refs[0][...], refs[pairs][...])
        for i in range(1, pairs):
            total += dot_first(refs[i][...], refs[pairs + i][...])
        refs[-1][...] = total.astype(jnp.bfloat16)

    out = jax.ShapeDtypeStruct((depth, columns), jnp.bfloat16)
    count = sum(left.shape[0] for left in lefts)
    return pl.pallas_call(
        kernel,
        out_shape=out,
        grid=(depth // tile,),
        in_specs=[pl.BlockSpec((left.shape[0], tile), lambda i: (0, i)) for left in lefts]
        + [pl.BlockSpec(right.shape, lambda i: (0, 0)) for right in rights],
        out_specs=pl.BlockSpec((tile, columns), lambda i: (i, 0)),
        compiler_params=pltpu.CompilerParams(vmem_limit_bytes=52 << 20),
        cost_estimate=cost(2 * count * depth * columns, [*lefts, *rights, out]),
    )(*lefts, *rights)


def body(
    tokens, seq_lens, gain_attn, gain_mlp, w_qkv, b_qkv, w_out, w_gate, w_up, w_down, cotangent
):
    low = jnp.bfloat16
    rows = tokens.shape[0]
    width = tokens.shape[1]
    count = lax.axis_size("fsdp")
    block = w_qkv.shape[0]
    units = w_gate.shape[1]
    quarter = -(-units // (4 * LANES)) * LANES
    head_group = HEADS // KV
    query_end = head_group * HD
    place = lax.axis_index("tp")

    own_rows = place * rows + jnp.arange(rows, dtype=jnp.int32)
    other_rows = (1 - place) * rows + jnp.arange(rows, dtype=jnp.int32)
    segment, position = segment_of(own_rows, seq_lens[0])
    other_segment, _ = segment_of(other_rows, seq_lens[0])
    key_rows = jnp.concatenate([own_rows, other_rows])
    key_segment = jnp.concatenate([segment, other_segment])
    allowed = (segment[:, None] == key_segment[None, :]) & (key_rows[None, :] <= own_rows[:, None])
    mask = jnp.where(allowed, 0.0, -1e30).astype(jnp.float32)
    valid = segment < seq_lens.shape[1]

    out_grad = cotangent * valid[:, None].astype(low)
    inputs = tokens.astype(jnp.float32)
    scale_one = root_scale(inputs)
    cosine, sine = rope_tables(position)

    near = own_bit("fsdp", NEAR)
    core = own_bit("fsdp", CORE)

    small = jnp.concatenate([gain_attn, gain_mlp, b_qkv[0]])
    used = -(-small.shape[0] // LANES)
    small = jnp.pad(small, (0, block * LANES - small.shape[0])).reshape(block, LANES)
    joint = jnp.concatenate([w_qkv, w_out.T, small], axis=1)
    cuts = thirds(joint.shape[1])
    cut = cuts[0][1]
    kept, got, halves = send_units([w_gate, w_up, w_down.T], quarter)
    fars = [far_gather(joint[:, :cut])]
    got, far, joint = tie(got, fars[0], joint)
    kept, given = halves(kept, got)
    near_got = swap(given[:2], *Z)
    far_rest = far_gather(joint[:, cut:])
    near_got, far_rest = tie(near_got, far_rest)
    quads = [jnp.concatenate([kept[i], near_got[i]]) for i in range(2)]
    parts = [jnp.stack(list(far.values()))]
    far_rest = jnp.stack(list(far_rest.values()))
    parts += [far_rest[:, :, start - cut : start - cut + size] for start, size in cuts[1:]]
    marks = [[(0, rel) for rel in far]] * 3

    far_gate = []
    for step, (begin, end) in enumerate([(0, 1), (1, 2), (2, 4)]):
        step_all(parts, marks, step)
        piece = far_units(quads[0], begin, end)
        parts, piece, quads, given, inputs, out_grad = tie(parts, piece, quads, given, inputs, out_grad)
        far_gate += piece
    own_gate = [(quads[0], INNER)]
    own_up = [(quads[1], INNER)]

    others = [swap(part, "fsdp", CORE) for part in parts]
    far_up = far_units(quads[1], 0, 1)
    all_gate = side_units(part_of(own_gate, 0, 2))
    parts, others, far_up, all_gate, quads, out_grad = tie(parts, others, far_up, all_gate, quads, out_grad)

    full_qkv, full_out, full_small = join_all(
        parts, others, marks, [w_qkv.shape[1], w_out.shape[0], LANES]
    )
    full_small = full_small.reshape(2, count, block, LANES)[:, :, :used].reshape(2, count, -1)
    gain_one = wide(full_small[0, :, :block].reshape(width))
    gain_two = wide(full_small[0, :, block : 2 * block].reshape(width))
    bias = wide(full_small[:, :, 2 * block : 2 * block + b_qkv.shape[1]].reshape(KV, -1))
    grad_first = spread_first(out_grad)
    piece_up = far_units(quads[1], 1, 2)
    piece_gate = side_units(part_of(own_gate, 2, 4))
    normed_one = (inputs * scale_one * gain_one[None, :]).astype(low)
    turned = project(normed_one, full_qkv, bias, cosine, sine)
    turned, grad_first, piece_up, piece_gate, given, quads = tie(
        turned, grad_first, piece_up, piece_gate, given, quads
    )
    far_up, all_gate = far_up + piece_up, all_gate + piece_gate

    columns = turned.shape[1] // KV
    own = turned.reshape(rows, KV, columns)[:, :, query_end:].reshape(rows, -1)
    other = swap(own, "tp", 1)
    near_down = swap(given[2], *Z)
    piece_up = far_units(quads[1], 2, 3)
    all_up = side_units(part_of(own_up, 0, 2))
    other, near_down, piece_up, all_up, grad_first, quads = tie(
        other, near_down, piece_up, all_up, grad_first, quads
    )
    far_up += piece_up

    keys_values = jnp.concatenate([own, other])
    mixed = attend(turned, keys_values, mask)
    grad_second = [spread_second(grad_first[:rows])]
    piece_up = far_units(quads[1], 3, 4)
    piece_side = side_units(part_of(own_up, 2, 4))
    mixed, grad_second, piece_up, piece_side, near_down, far_gate, far_up = tie(
        mixed, grad_second, piece_up, piece_side, near_down, far_gate, far_up
    )
    far_up, all_up = far_up + piece_up, all_up + piece_side
    quads.append(jnp.concatenate([kept[2], near_down]))
    own_down = [(quads[2], INNER)]

    mixed = [mixed[:, :query_end], mixed[:, query_end:]]
    hidden = inputs + dot_last(mixed[0], full_out[0]) + dot_last(mixed[1], full_out[1])
    scale_two = root_scale(hidden)
    normed_two = (hidden * scale_two * gain_two[None, :]).astype(low)
    far_down = far_units(quads[2], 0, 1)
    all_gate += side_units(far_gate)
    normed_two, far_down, all_gate, quads, far_up = tie(normed_two, far_down, all_gate, quads, far_up)

    normed_first = spread_first(normed_two)
    piece_down = far_units(quads[2], 1, 2)
    full_gate = join_units(own_gate + far_gate + all_gate)
    piece_side = side_units([far_up[0]])
    normed_first, piece_down, full_gate, piece_side, far_up, quads = tie(
        normed_first, piece_down, full_gate, piece_side, far_up, quads
    )
    far_down, all_up = far_down + piece_down, all_up + piece_side

    normed_second = spread_second(normed_first)
    piece_down = far_units(quads[2], 2, 4)
    all_up += side_units(far_up[1:])
    normed_chunks = [both_cores(normed_first)]
    normed_second, piece_down, all_up, normed_chunks, own_down, grad_first, normed_first = tie(
        normed_second, piece_down, all_up, normed_chunks, own_down, grad_first, normed_first
    )
    far_down += piece_down

    full_up = join_units(own_up + far_up + all_up)
    normed_chunks.append(both_cores(normed_second))
    grad_second.append(spread_second(grad_first[rows:]))
    all_down = side_units(own_down)
    gates, ups, acts = [[None, None] for _ in range(3)]
    gates[0], ups[0], acts[0] = gated(normed_chunks[0], full_gate, full_up)
    acts, normed_chunks, grad_second, all_down, far_down = tie(
        acts, normed_chunks, grad_second, all_down, far_down
    )
    all_down += side_units(far_down)
    grad_chunks = [both_cores(grad_first), both_cores(jnp.concatenate(grad_second))]
    gates[1], ups[1], acts[1] = gated(normed_chunks[1], full_gate, full_up)
    acts, all_down, grad_chunks = tie(acts, all_down, grad_chunks)

    full_down = join_units(own_down + far_down + all_down)
    grad_down = weight_grad(grad_chunks, acts)
    full_down, grad_down, grad_chunks = tie(full_down, grad_down, grad_chunks)

    codes, home = far_codes()
    down_at = side_view(grad_down)
    down_got = {rel: swap(down_at(rel, 1), "fsdp", SIDE) for rel in codes}
    grad_gate_1, grad_up_1, part_1 = gated_back(
        grad_chunks[1], gates[1], ups[1], full_gate, full_up, full_down
    )
    down_got, part_1 = tie(down_got, part_1)
    part_1 = slim(sum_cores(part_1))
    down_out = {rel: add_pair(down_at(rel, 0), got) for rel, got in down_got.items()}
    part_1, down_out, grad_chunk = tie(part_1, down_out, grad_chunks[0])

    down_got = swap(down_at(home, 1), "fsdp", SIDE)
    down_sum = far_sums({rel: piece[:2] for rel, piece in down_out.items()})
    got_1 = swap_both(part_1, Z, X)
    grad_gate_0, grad_up_0, part_0 = gated_back(
        grad_chunk, gates[0], ups[0], full_gate, full_up, full_down
    )
    part_0, got_1, normed_sent, down_got, down_sum, down_out = tie(
        part_0, got_1, normed_chunks, down_got, down_sum, down_out
    )

    core_0 = swap(part_0[2 * rows :], "fsdp", CORE)
    down_rest = far_sums({rel: piece[2:] for rel, piece in down_out.items()})
    grad_gate = weight_grad(normed_sent, [grad_gate_0, grad_gate_1])
    core_0, grad_gate, down_rest, down_got = tie(core_0, grad_gate, down_rest, down_got)
    down_sum = add_pair(
        wide(down_at(home, 0)) + wide(down_got), jnp.concatenate([down_sum, down_rest])
    )

    part_0 = wide(part_0[: 2 * rows]) + wide(core_0) + wide(got_1)
    part_sent = slim(part_0[rows:])
    gate_at = side_view(grad_gate)
    gate_sent = {rel: gate_at(rel, 1) for rel in codes}
    normed_sent, part_sent, gate_sent = tie(normed_sent, part_sent, gate_sent)
    got_0 = swap_both(part_sent, X, Z)
    gate_got = {rel: swap(piece, "fsdp", SIDE) for rel, piece in gate_sent.items()}
    grad_up = weight_grad(normed_sent, [grad_up_0, grad_up_1])
    got_0, gate_got, grad_up, down_sum = tie(got_0, gate_got, grad_up, down_sum)

    gate_out = {rel: add_pair(gate_at(rel, 0), got) for rel, got in gate_got.items()}
    gate_sent = gate_at(home, 1)
    gate_out, gate_sent, got_0 = tie(gate_out, gate_sent, got_0)
    gate_sum = [far_sums({rel: piece[:1] for rel, piece in gate_out.items()})]
    gate_home = [swap(gate_sent[:2], "fsdp", SIDE)]
    grad_normed_two = part_0[:rows] + wide(got_0)
    hidden_hat = hidden * scale_two
    grad_gain_two = jnp.sum(grad_normed_two * hidden_hat, axis=0)
    grad_hidden = wide(out_grad) + norm_back(grad_normed_two, gain_two, hidden_hat, scale_two)
    branch_grad = grad_hidden.astype(low)
    grad_mixed = jnp.concatenate([dot(branch_grad, full_out[t]).astype(low) for t in range(KV)], 1)
    up_at = side_view(grad_up)
    up_sent = {rel: up_at(rel, 1) for rel in codes}
    grad_mixed, gate_sum, gate_home, gate_out, gate_sent, up_sent, down_sum = tie(
        grad_mixed, gate_sum, gate_home, gate_out, gate_sent, up_sent, down_sum
    )

    gate_sum.append(far_sums({rel: piece[1:3] for rel, piece in gate_out.items()}))
    up_got = {rel: swap(piece, "fsdp", SIDE) for rel, piece in up_sent.items()}
    down_share = share_near(down_sum, near)
    grad_query, grad_keys, grad_values = attend_back(
        turned, keys_values, mask, grad_mixed, cosine, sine
    )
    grad_query, grad_keys, grad_values, gate_sum, up_got, down_share, gate_sent, acts = tie(
        grad_query, grad_keys, grad_values, gate_sum, up_got, down_share, gate_sent, acts
    )

    other = swap(jnp.concatenate([grad_keys[rows:], grad_values[rows:]], 1).astype(low), "tp", 1)
    gate_sum.append(far_sums({rel: piece[3:] for rel, piece in gate_out.items()}))
    gate_home.append(swap(gate_sent[2:], "fsdp", SIDE))
    up_out = {rel: add_pair(up_at(rel, 0), got) for rel, got in up_got.items()}
    up_sent = up_at(home, 1)
    out_parts = [dot_last(act, full_down).astype(low) for act in acts]
    other, gate_sum, gate_home, up_out, up_sent, out_parts, grad_query = tie(
        other, gate_sum, gate_home, up_out, up_sent, out_parts, grad_query
    )
    gate_sum = add_pair(
        wide(gate_at(home, 0)) + wide(jnp.concatenate(gate_home)), jnp.concatenate(gate_sum)
    )

    out_cores = [swap(part[2 * rows :], "fsdp", CORE) for part in out_parts]
    up_sum = [far_sums({rel: piece[:2] for rel, piece in up_out.items()})]
    up_home = [swap(up_sent[:2], "fsdp", SIDE)]
    other = wide(other)
    grad_keys = (grad_keys[:rows] + other[:, : KV * HD]).reshape(rows, KV, HD)
    grad_values = (grad_values[:rows] + other[:, KV * HD :]).reshape(rows, KV, HD)
    grad_keys = unrotate(grad_keys, cosine, sine).astype(low)
    grad_values = grad_values.astype(low)
    grad_qkv = [
        jnp.concatenate(
            [grad_query[:, t * query_end : (t + 1) * query_end], grad_keys[:, t], grad_values[:, t]], 1
        )
        for t in range(KV)
    ]
    grad_bias = jnp.stack([jnp.sum(wide(part), axis=0) for part in grad_qkv])
    grad_joint = jnp.stack(
        [
            jnp.concatenate([dot_first(normed_one, grad_qkv[t]), dot_first(branch_grad, mixed[t])], 1)
            for t in range(KV)
        ]
    ).astype(low)
    grad_joint, out_cores, up_sum, up_home, up_out, up_sent, gate_sum = tie(
        grad_joint, out_cores, up_sum, up_home, up_out, up_sent, gate_sum
    )

    size = grad_joint.shape[2]
    view = grad_joint.reshape(2, count // 2, 2, block, size)
    joint_got = swap(lax.dynamic_index_in_dim(view, core ^ 1, 2, keepdims=False), "fsdp", CORE)
    out_parts = [wide(part[: 2 * rows]) + wide(got) for part, got in zip(out_parts, out_cores)]
    out_got = swap_both(slim(out_parts[1]), Z, X)
    up_sum.append(far_sums({rel: piece[2:3] for rel, piece in up_out.items()}))
    up_home.append(swap(up_sent[2:], "fsdp", SIDE))
    grad_normed_one = dot_last(grad_qkv[0], full_qkv[0]) + dot_last(grad_qkv[1], full_qkv[1])
    grad_normed_one, joint_got, out_got, up_sum, up_home, up_out = tie(
        grad_normed_one, joint_got, out_got, up_sum, up_home, up_out
    )

    view = add_pair(lax.dynamic_index_in_dim(view, core, 2, keepdims=False), joint_got)
    far_names = [("fsdp", bit) for bit in far_bits()]
    view = view.reshape([2] * (1 + len(far_names)) + [2, 2, block, size])
    parts = [view[..., start : start + length] for start, length in thirds(size)]
    axes = [[("tp", 1)] + far_names + [("fsdp", NEAR), ("fsdp", SIDE)]] * 3
    out_parts = out_parts[0] + wide(out_got)
    out_sent = slim(out_parts[rows:])
    parts, out_sent = tie(parts, out_sent)
    parts, axes = scatter_step(parts, axes, 0)
    out_got = swap_both(out_sent, X, Z)
    up_sum.append(far_sums({rel: piece[3:] for rel, piece in up_out.items()}))
    input_hat = inputs * scale_one
    grad_gain_one = jnp.sum(grad_normed_one * input_hat, axis=0)
    grad_inputs = grad_hidden + norm_back(grad_normed_one, gain_one, input_hat, scale_one)
    share = block // 2
    small = jnp.concatenate(
        [
            grad_gain_one.reshape(count, 2, share).swapaxes(0, 1),
            grad_gain_two.reshape(count, 2, share).swapaxes(0, 1),
            grad_bias.reshape(2, count, -1),
        ],
        axis=2,
    )
    parts, out_got, up_sum, up_home, small, gate_sum = tie(parts, out_got, up_sum, up_home, small, gate_sum)
    small_sum = scatter_small(small)
    out_rows = (hidden + out_parts[:rows] + wide(out_got)).astype(low)
    up_sum = add_pair(wide(up_at(home, 0)) + wide(jnp.concatenate(up_home)), jnp.concatenate(up_sum))
    parts, axes = scatter_step([add_pair(*part) for part in parts], axes, 1)
    gate_share = share_near(gate_sum, near)
    parts, gate_share, up_sum = tie(parts, gate_share, up_sum)
    parts, axes = scatter_step([add_pair(*part) for part in parts], axes, 2)
    up_share = share_near(up_sum, near)
    parts, up_share = tie(parts, up_share)

    gate_sum, up_sum, down_sum = share_cores([gate_share, up_share, down_share], units)
    joint_sum = jnp.concatenate([add_pair(*part) for part in parts], axis=-1)
    for bit in far_bits():
        mine = own_bit("fsdp", bit)
        got = swap(lax.dynamic_index_in_dim(joint_sum, mine ^ 1, 0, keepdims=False), "fsdp", bit)
        keep = lax.dynamic_index_in_dim(joint_sum, mine, 0, keepdims=False)
        joint_sum = wide(keep) + wide(got)
    qkv_sum, out_sum = joint_sum[:, : w_qkv.shape[1]], joint_sum[:, w_qkv.shape[1] :].T
    return (
        out_rows,
        grad_inputs,
        small_sum[:share],
        small_sum[share : 2 * share],
        qkv_sum,
        small_sum[None, 2 * share :],
        out_sum,
        gate_sum,
        up_sum,
        down_sum.T,
    )


def solution(mesh):
    placed = (
        P(("fsdp", "tp"), None),
        P("fsdp", None),
        P("fsdp"),
        P("fsdp"),
        P("fsdp", "tp"),
        P("tp", "fsdp"),
        P("tp", "fsdp"),
        P("fsdp", "tp"),
        P("fsdp", "tp"),
        P("tp", "fsdp"),
        P(("fsdp", "tp"), None),
    )
    return jax.shard_map(
        body,
        mesh=mesh,
        in_specs=placed,
        out_specs=(
            P(("fsdp", "tp"), None),
            P(("fsdp", "tp"), None),
            P(("fsdp", "tp")),
            P(("fsdp", "tp")),
            P("fsdp", "tp"),
            P("tp", "fsdp"),
            P("tp", "fsdp"),
            P("fsdp", "tp"),
            P("fsdp", "tp"),
            P("tp", "fsdp"),
        ),
        check_vma=False,
    )
```

time: 1970 us -> 773 us (0.39)
  waiting for transfers between devices: 1550 us -> 247 us
  matrix products: 230 us -> 36.9 us
  Pallas kernels: 0 us -> 190 us
  blocking collectives: 103 us -> 0 us
  starting transfers between devices: 0.77 us -> 98.2 us
  local copies, waits for them, and re-layouts: 23.6 us -> 107 us
  other arithmetic: 42.5 us -> 82.3 us
    reduce_scatter x9 -> x0, waiting for transfers between devices: 1070 us -> none  [the longest x1 267 us: body(): lax.psum_scatter(grad_down, 'fsdp', scatter_dimension=1, tiled=True)]
    all_gather x9 -> x0, waiting for transfers between devices: 479 us -> none  [the longest x1 111 us: body(): lax.all_gather(w_down, 'fsdp', axis=1, tiled=True)]
    ppermute x0 -> x91, waiting for transfers between devices: none -> 247 us  [the longest x82 228 us: swap(): return lax.ppermute(values, axis, [(i, i ^ bit) for i in range(count)])]
    dot_general x21 -> x12, matrix products: 230 us -> 36.9 us  [the longest x6 24.4 us: dot_last(): lax.dot_general(a, b, (((1,), (1,)), ((), ())), preferred_element_type=jn...]
    pallas_call x0 -> x14, Pallas kernels: none -> 190 us  [the longest x2 56.7 us: gated_back(): pl.pallas_call(kernel, out_shape=[out, out, jax.ShapeDtypeStruct((count,...]
    unnamed x2 -> x0, blocking collectives: 103 us -> none
    ppermute x0 -> x91, starting transfers between devices: none -> 98.2 us  [the longest x82 91.1 us: swap(): return lax.ppermute(values, axis, [(i, i ^ bit) for i in range(count)])]
    slice x2 -> x48, local copies, waits for them, and re-layouts: 3.49 us -> 40.1 us  [the longest x1 6.65 us: body(): full_qkv[1]]
  transfers between devices with their start and end apart: 19 -> 91, of which waited for: 17 -> 37; matrix products, arithmetic and copies ran while one was open for 8% -> 17% of each run, Pallas kernels for 0% -> 22%
where the time goes in v1:
time: 773 us; the launch traced here: 764 us
  waiting for transfers between devices  247 us (32%)
  Pallas kernels  190 us (25%)
  local copies, waits for them, and re-layouts  107 us (14%)
  starting transfers between devices  98.2 us (13%)
  other arithmetic  82.3 us (11%)
  matrix products  36.9 us (5%)
    ppermute x82, waiting for transfers between devices, swap(): return lax.ppermute(values, axis, [(i, i ^ bit) for i in range(count)])  228 us
    ppermute x82, starting transfers between devices, swap(): return lax.ppermute(values, axis, [(i, i ^ bit) for i in range(count)])  91.1 us
    pallas_call x2, Pallas kernels, gated_back(): pl.pallas_call(kernel, out_shape=[out, out, jax.ShapeDtypeStruct((count,...  56.7 us
    pallas_call x3, Pallas kernels, weight_grad(): pl.pallas_call(kernel, out_shape=out, grid=(depth // tile,), in_specs=[pl...  47.1 us
    pallas_call x2, Pallas kernels, gated(): pl.pallas_call(kernel, out_shape=[out] * 3, grid=(count // STEP,), in_spe...  30.9 us
    unnamed x246, local copies, waits for them, and re-layouts  26.3 us
    dot_general x6, matrix products, dot_last(): lax.dot_general(a, b, (((1,), (1,)), ((), ())), preferred_element_type=jn...  24.4 us
    convert_element_type x18, other arithmetic, slim(): return values.astype(jnp.bfloat16)  20.6 us
  transfers between devices with their start and end apart: 91, of which 37 were waited for; matrix products, arithmetic and copies ran while one was open for 17% of the time, Pallas kernels for 22%

profile of v1, /device:TPU:0, one launch (start us, length us, event | category | flops | bytes accessed | tf_op | source)
XLA Modules:
  0.0 764.0 jit_solution(12613062440636508868)
XLA Ops:
  28.6 14.3 %collective-permute-done.4 = bf16[96,1280]{1,0:T(8,128)(2,1)S(1)} collective-permute-done((bf16[96,1280]{1,0:T(8,128)(2,1)S(1)}, bf16[96,1280]{1,0:T(8,128)(2,1)S(1)}, u32[]{:S(2)}, u32[]{:S(2)}) %collective-permute-start.4) | collective-permute-done | bytes 245792 | tf_op jit(solution)/shard_map/ppermute | solution.py:27
  42.9 5.4 collective-permute-done.3
  80.2 12.8 %collective-permute-done.14 = bf16[8,96,640]{2,1,0:T(8,128)(2,1)S(1)} collective-permute-done((bf16[8,96,640]{2,1,0:T(8,128)(2,1)S(1)}, bf16[8,96,640]{2,1,0:T(8,128)(2,1)S(1)}, u32[]{:S(2)}, u32[]{:S(2)}) %collective-permute-start.14) | collective-permute-done | bytes 983072 | tf_op jit(solution)/shard_map/ppermute | solution.py:27
  94.4 11.9 %collective-permute-done.12 = bf16[8,96,640]{2,1,0:T(8,128)(2,1)S(1)} collective-permute-done((bf16[8,96,640]{2,1,0:T(8,128)(2,1)S(1)}, bf16[8,96,640]{2,1,0:T(8,128)(2,1)S(1)}, u32[]{:S(2)}, u32[]{:S(2)}) %collective-permute-start.12) | collective-permute-done | bytes 983072 | tf_op jit(solution)/shard_map/ppermute | solution.py:27
  113.0 9.9 %collective-permute-done.19.refs_1_ = bf16[1,96,1152]{2,1,0:T(8,128)(2,1)S(1)} collective-permute-done((bf16[1,96,1152]{2,1,0:T(8,128)(2,1)S(1)}, bf16[1,96,1152]{2,1,0:T(8,128)(2,1)S(1)}, u32[]{:S(2)}, u32[]{:S(2)}) %collective-permute-start.19) | collective-permute-done | bytes 221216 | tf_op jit(solution)/shard_map/ppermute | solution.py:27
  160.1 11.1 %collective-permute-done.26.refs_3_ = bf16[1,96,1152]{2,1,0:T(8,128)(2,1)S(1)} collective-permute-done((bf16[1,96,1152]{2,1,0:T(8,128)(2,1)S(1)}, bf16[1,96,1152]{2,1,0:T(8,128)(2,1)S(1)}, u32[]{:S(2)}, u32[]{:S(2)}) %collective-permute-start.26) | collective-permute-done | bytes 221216 | tf_op jit(solution)/shard_map/ppermute | solution.py:27
  188.1 11.2 %shard_map.188 = bf16[320,1536]{1,0:T(8,128)(2,1)S(1)} custom-call(bf16[320,2048]{1,0:T(8,128)(2,1)S(1)} %shard_map.187.query_ref, bf16[640,512]{1,0:T(8,128)(2,1)S(1)} %constant_dynamic-update-slice_fusion.keys_ref.values_ref, bf16[640,512]{1,0:T(8,128)(2,1)S(1)} %constant_dynamic-update-slice_fusion.keys_ref.values_ref, f32[320,640]{1,0:T(8,128)S(1)} %copy-done.8), custom_call_target="tpu_custom_call" | custom-call | flops 314572800 | bytes 348160 | tf_op jit(solution)/shard_map/pallas_call | solution.py:428
  205.9 13.2 %collective-permute-done.32.refs_6_ = bf16[4,96,1152]{2,1,0:T(8,128)(2,1)S(1)} collective-permute-done((bf16[4,96,1152]{2,1,0:T(8,128)(2,1)S(1)}, bf16[4,96,1152]{2,1,0:T(8,128)(2,1)S(1)}, u32[]{:S(2)}, u32[]{:S(2)}) %collective-permute-start.32) | collective-permute-done | bytes 884768 | tf_op jit(solution)/shard_map/ppermute | solution.py:27
  239.8 26.3 %collective-permute-done.37.refs_3_ = bf16[2,96,1152]{2,1,0:T(8,128)(2,1)S(1)} collective-permute-done((bf16[2,96,1152]{2,1,0:T(8,128)(2,1)S(1)}, bf16[2,96,1152]{2,1,0:T(8,128)(2,1)S(1)}, u32[]{:S(2)}, u32[]{:S(2)}) %collective-permute-start.37) | collective-permute-done | bytes 442400 | tf_op jit(solution)/shard_map/ppermute | solution.py:27
  278.0 15.5 %shard_map.191 = (bf16[1280,1152]{1,0:T(8,128)(2,1)}, bf16[1280,1152]{1,0:T(8,128)(2,1)}, bf16[1280,1152]{1,0:T(8,128)(2,1)}) custom-call(bf16[1280,1536]{1,0:T(8,128)(2,1)} %pad_maximum_fusion.1.rows_ref.refs_0_, bf16[1536,1152]{1,0:T(8,128)(2,1)} %bitcast.226, bf16[1536,1152]{1,0:T(8,128)(2,1)} %bitcast.230), custom_call_target="tpu_custom_call" | custom-call | flops 1132462080 | bytes 2482176 | tf_op jit(solution)/shard_map/pallas_call | solution.py:513
  308.1 15.5 %shard_map.192 = (bf16[1280,1152]{1,0:T(8,128)(2,1)}, bf16[1280,1152]{1,0:T(8,128)(2,1)}, bf16[1280,1152]{1,0:T(8,128)(2,1)}) custom-call(bf16[1280,1536]{1,0:T(8,128)(2,1)} %pad_maximum_fusion.2.rows_ref.refs_1_, bf16[1536,1152]{1,0:T(8,128)(2,1)} %bitcast.227, bf16[1536,1152]{1,0:T(8,128)(2,1)} %bitcast.231), custom_call_target="tpu_custom_call" | custom-call | flops 1132462080 | bytes 2482176 | tf_op jit(solution)/shard_map/pallas_call | solution.py:513
  334.0 15.5 %shard_map.194 = bf16[1536,1152]{1,0:T(8,128)(2,1)} custom-call(bf16[1280,1536]{1,0:T(8,128)(2,1)} %pad_maximum_fusion.3.refs_0_.grad_ref, bf16[1280,1536]{1,0:T(8,128)(2,1)} %pad_maximum_fusion.4.refs_1_.grad_ref, bf16[1280,1152]{1,0:T(8,128)(2,1)} %get-tuple-element.421.refs_2_, bf16[1280,1152]{1,0:T(8,128)(2,1)} %get-tuple-element.422.refs_3_), custom_call_target="tpu_custom_call" | custom-call | flops 1132462080 | bytes 2162688 | tf_op jit(solution)/shard_map/pallas_call | solution.py:568
  353.2 28.5 %shard_map.195 = (bf16[1280,1152]{1,0:T(8,128)(2,1)}, bf16[1280,1152]{1,0:T(8,128)(2,1)}, bf16[1280,1536]{1,0:T(8,128)(2,1)}) custom-call(bf16[1280,1536]{1,0:T(8,128)(2,1)} %pad_maximum_fusion.4.refs_1_.grad_ref, bf16[1280,1152]{1,0:T(8,128)(2,1)} %get-tuple-element.365.gate_ref, bf16[1280,1152]{1,0:T(8,128)(2,1)} %get-tuple-element.366.up_ref, ...), custom_call_target="tpu_custom_call" | custom-call | flops 1698693120 | bytes 3047424 | tf_op jit(solution)/shard_map/pallas_call | solution.py:544
  393.4 28.2 %shard_map.196 = (bf16[1280,1152]{1,0:T(8,128)(2,1)}, bf16[1280,1152]{1,0:T(8,128)(2,1)}, bf16[1280,1536]{1,0:T(8,128)(2,1)}) custom-call(bf16[1280,1536]{1,0:T(8,128)(2,1)} %pad_maximum_fusion.3.refs_0_.grad_ref, bf16[1280,1152]{1,0:T(8,128)(2,1)} %get-tuple-element.373.gate_ref, bf16[1280,1152]{1,0:T(8,128)(2,1)} %get-tuple-element.374.up_ref, ...), custom_call_target="tpu_custom_call" | custom-call | flops 1698693120 | bytes 3047424 | tf_op jit(solution)/shard_map/pallas_call | solution.py:544
  428.7 15.6 %shard_map.197 = bf16[1536,1152]{1,0:T(8,128)(2,1)} custom-call(bf16[1280,1536]{1,0:T(8,128)(2,1)} %pad_maximum_fusion.1.rows_ref.refs_0_, bf16[1280,1536]{1,0:T(8,128)(2,1)} %pad_maximum_fusion.2.rows_ref.refs_1_, bf16[1280,1152]{1,0:T(8,128)(2,1)} %get-tuple-element.382.refs_2_, bf16[1280,1152]{1,0:T(8,128)(2,1)} %get-tuple-element.383.refs_3_), custom_call_target="tpu_custom_call" | custom-call | flops 1132462080 | bytes 2162688 | tf_op jit(solution)/shard_map/pallas_call | solution.py:568
  444.3 5.4 collective-permute-done.52
  457.5 16.1 %shard_map.198 = bf16[1536,1152]{1,0:T(8,128)(2,1)} custom-call(bf16[1280,1536]{1,0:T(8,128)(2,1)} %pad_maximum_fusion.1.rows_ref.refs_0_, bf16[1280,1536]{1,0:T(8,128)(2,1)} %pad_maximum_fusion.2.rows_ref.refs_1_, bf16[1280,1152]{1,0:T(8,128)(2,1)} %get-tuple-element.393.refs_2_, bf16[1280,1152]{1,0:T(8,128)(2,1)} %get-tuple-element.394.refs_3_), custom_call_target="tpu_custom_call" | custom-call | flops 1132462080 | bytes 2162688 | tf_op jit(solution)/shard_map/pallas_call | solution.py:568
  488.7 10.1 %collective-permute-done.55 = bf16[1,96,1152]{2,1,0:T(8,128)(2,1)S(1)} collective-permute-done((bf16[1,96,1152]{2,1,0:T(8,128)(2,1)S(1)}, bf16[1,96,1152]{2,1,0:T(8,128)(2,1)S(1)}, u32[]{:S(2)}, u32[]{:S(2)}) %collective-permute-start.55) | collective-permute-done | bytes 221216 | tf_op jit(solution)/shard_map/ppermute | solution.py:27
  510.1 20.3 %shard_map.199 = (bf16[320,1536]{1,0:T(8,128)(2,1)S(1)}, f32[640,256]{1,0:T(8,128)S(1)}, f32[640,256]{1,0:T(8,128)S(1)}) custom-call(bf16[320,2048]{1,0:T(8,128)(2,1)S(1)} %shard_map.187.query_ref, bf16[640,512]{1,0:T(8,128)(2,1)S(1)} %constant_dynamic-update-slice_fusion.keys_ref.values_ref, ...), custom_call_target="tpu_custom_call" | custom-call | flops 786432000 | bytes 348160 | tf_op jit(solution)/shard_map/pallas_call | solution.py:472
  531.3 6.8 convolution_convert_fusion
  538.1 7.0 convolution_convert_fusion.1
  547.9 5.7 collective-permute-done.60
  579.3 8.9 %collective-permute-done.65 = bf16[2,96,1152]{2,1,0:T(8,128)(2,1)} collective-permute-done((bf16[2,96,1152]{2,1,0:T(8,128)(2,1)}, bf16[2,96,1152]{2,1,0:T(8,128)(2,1)}, u32[]{:S(2)}, u32[]{:S(2)}) %collective-permute-start.65) | collective-permute-done | bytes 442400 | tf_op jit(solution)/shard_map/ppermute | solution.py:27
  588.2 14.5 %copy.42 = bf16[2,1536,1792]{2,1,0:T(8,128)(2,1)} copy(bf16[2,1536,1792]{1,2,0:T(8,128)(2,1)} %pad_maximum_fusion) | data formatting | bytes 22020096 | tf_op jit(solution)/shard_map/optimization_barrier | solution.py:181
  602.7 5.5 dynamic-slice_bitcast_fusion
  611.6 6.6 fusion.42
  633.2 5.4 collective-permute-done.69
  641.1 5.8 fusion
  667.0 14.7 %collective-permute-done.75 = bf16[1,96,1152]{2,1,0:T(8,128)(2,1)S(1)} collective-permute-done((bf16[1,96,1152]{2,1,0:T(8,128)(2,1)S(1)}, bf16[1,96,1152]{2,1,0:T(8,128)(2,1)S(1)}, u32[]{:S(2)}, u32[]{:S(2)}) %collective-permute-start.75) | collective-permute-done | bytes 221216 | tf_op jit(solution)/shard_map/ppermute | solution.py:27
  683.7 7.3 collective-permute-done.74
  732.1 7.2 collective-permute-done.85
  742.5 16.6 %collective-permute-done.89 = bf16[96,1792]{1,0:T(8,128)(2,1)S(1)} collective-permute-done((bf16[96,1792]{1,0:T(8,128)(2,1)S(1)}, bf16[96,1792]{1,0:T(8,128)(2,1)S(1)}, u32[]{:S(2)}, u32[]{:S(2)}) %collective-permute-start.89) | collective-permute-done | bytes 344096 | tf_op jit(solution)/shard_map/ppermute | solution.py:27
  (615 shorter events, 362.3 us)
Async XLA Ops:
  16.8 31.5 %collective-permute-start.3 = (bf16[2,2,96,1152]{3,2,1,0:T(8,128)(2,1)S(1)}, bf16[2,2,96,1152]{3,2,1,0:T(8,128)(2,1)S(1)}, u32[]{:S(2)}, u32[]{:S(2)}) collective-permute-start(bf16[2,2,96,1152]{3,2,1,0:T(8,128)(2,1)S(1)} %slice.447), channel_id=1, source_target_pairs={{0,8},{2,10},{4,12},{6,14},{8,0},{10,2},{12,4},{14,6},{16,24},{18,... | collective-permute-start | bytes 2654216 | tf_op jit(solution)/shard_map/ppermute | solution.py:27
  17.6 25.3 %collective-permute-start.4 = (bf16[96,1280]{1,0:T(8,128)(2,1)S(1)}, bf16[96,1280]{1,0:T(8,128)(2,1)S(1)}, u32[]{:S(2)}, u32[]{:S(2)}) collective-permute-start(bf16[96,1280]{1,0:T(8,128)(2,1)S(1)} %slice.344), channel_id=1, source_target_pairs={{0,16},{2,18},{4,20},{6,22},{8,24},{10,26},{12,28},{14,30},{16,0},... | collective-permute-start | bytes 737288 | tf_op jit(solution)/shard_map/ppermute | solution.py:27
  24.2 31.3 %collective-permute-start.7 = (bf16[1,96,1152]{2,1,0:T(8,128)(2,1)S(1)}, bf16[1,96,1152]{2,1,0:T(8,128)(2,1)S(1)}, u32[]{:S(2)}, u32[]{:S(2)}) collective-permute-start(bf16[1,96,1152]{2,1,0:T(8,128)(2,1)S(1)} %get-tuple-element.535), channel_id=1, source_target_pairs={{0,16},{2,18},{4,20},{6,22},{8,24},{10,26},{12,28},{14,30},{16,0},... | collective-permute-start | bytes 663560 | tf_op jit(solution)/shard_map/ppermute | solution.py:27
  74.6 31.7 %collective-permute-start.12 = (bf16[8,96,640]{2,1,0:T(8,128)(2,1)S(1)}, bf16[8,96,640]{2,1,0:T(8,128)(2,1)S(1)}, u32[]{:S(2)}, u32[]{:S(2)}) collective-permute-start(bf16[8,96,640]{2,1,0:T(8,128)(2,1)S(1)} %pad_maximum_fusion.15), channel_id=1, source_target_pairs={{0,8},{2,10},{4,12},{6,14},{8,0},{10,2},{12,4},{14,6},{16,24},{18,... | collective-permute-start | bytes 2949128 | tf_op jit(solution)/shard_map/ppermute | solution.py:27
  79.1 27.4 %collective-permute-start.15 = (bf16[2,96,1152]{2,1,0:T(8,128)(2,1)S(1)}, bf16[2,96,1152]{2,1,0:T(8,128)(2,1)S(1)}, u32[]{:S(2)}, u32[]{:S(2)}) collective-permute-start(bf16[2,96,1152]{2,1,0:T(8,128)(2,1)S(1)} %slice.354), channel_id=1, source_target_pairs={{0,16},{2,18},{4,20},{6,22},{8,24},{10,26},{12,28},{14,30},{16,0},... | collective-permute-start | bytes 1327112 | tf_op jit(solution)/shard_map/ppermute | solution.py:27
  122.9 27.9 %collective-permute-start.23 = (bf16[2,96,1152]{2,1,0:T(8,128)(2,1)}, bf16[2,96,1152]{2,1,0:T(8,128)(2,1)}, u32[]{:S(2)}, u32[]{:S(2)}) collective-permute-start(bf16[2,96,1152]{2,1,0:T(8,128)(2,1)} %get-tuple-element.550), channel_id=1, source_target_pairs={{0,4},{2,6},{4,0},{6,2},{8,12},{10,14},{12,8},{14,10},{16,20},{18,... | collective-permute-start | bytes 1327112 | tf_op jit(solution)/shard_map/ppermute | solution.py:27
  124.4 35.7 %collective-permute-start.27 = (bf16[2,96,1152]{2,1,0:T(8,128)(2,1)}, bf16[2,96,1152]{2,1,0:T(8,128)(2,1)}, u32[]{:S(2)}, u32[]{:S(2)}) collective-permute-start(bf16[2,96,1152]{2,1,0:T(8,128)(2,1)} %get-tuple-element.549), channel_id=1, source_target_pairs={{0,4},{2,6},{4,0},{6,2},{8,12},{10,14},{12,8},{14,10},{16,20},{18,... | collective-permute-start | bytes 1327112 | tf_op jit(solution)/shard_map/ppermute | solution.py:27
  174.2 25.2 %collective-permute-start.28 = (bf16[320,1536]{1,0:T(8,128)(2,1)}, bf16[320,1536]{1,0:T(8,128)(2,1)}, u32[]{:S(2)}, u32[]{:S(2)}) collective-permute-start(bf16[320,1536]{1,0:T(8,128)(2,1)} %slice.366), channel_id=1, source_target_pairs={{0,8},{1,9},{2,3},{3,2},{4,12},{5,13},{6,7},{7,6},{8,0},{9,1},{10,... | collective-permute-start | bytes 2949128 | tf_op jit(solution)/shard_map/ppermute | solution.py:38
  175.3 30.6 %collective-permute-start.31 = (bf16[1,96,1152]{2,1,0:T(8,128)(2,1)}, bf16[1,96,1152]{2,1,0:T(8,128)(2,1)}, u32[]{:S(2)}, u32[]{:S(2)}) collective-permute-start(bf16[1,96,1152]{2,1,0:T(8,128)(2,1)} %get-tuple-element.534), channel_id=1, source_target_pairs={{0,16},{2,18},{4,20},{6,22},{8,24},{10,26},{12,28},{14,30},{16,0},... | collective-permute-start | bytes 663560 | tf_op jit(solution)/shard_map/ppermute | solution.py:27
  234.0 34.1 %collective-permute-start.36 = (bf16[640,1536]{1,0:T(8,128)(2,1)S(1)}, bf16[640,1536]{1,0:T(8,128)(2,1)S(1)}, u32[]{:S(2)}, u32[]{:S(2)}) collective-permute-start(bf16[640,1536]{1,0:T(8,128)(2,1)S(1)} %pad_maximum_fusion.10), channel_id=1, source_target_pairs={{0,8},{1,9},{2,3},{3,2},{4,12},{5,13},{6,7},{7,6},{8,0},{9,1},{10,... | collective-permute-start | bytes 5898248 | tf_op jit(solution)/shard_map/ppermute | solution.py:38
  234.6 31.5 %collective-permute-start.38 = (bf16[3,96,1152]{2,1,0:T(8,128)(2,1)S(1)}, bf16[3,96,1152]{2,1,0:T(8,128)(2,1)S(1)}, u32[]{:S(2)}, u32[]{:S(2)}) collective-permute-start(bf16[3,96,1152]{2,1,0:T(8,128)(2,1)S(1)} %pad_maximum_fusion.26), channel_id=1, source_target_pairs={{0,4},{2,6},{4,0},{6,2},{8,12},{10,14},{12,8},{14,10},{16,20},{18,... | collective-permute-start | bytes 1990664 | tf_op jit(solution)/shard_map/ppermute | solution.py:27
  235.0 31.1 %collective-permute-start.37 = (bf16[2,96,1152]{2,1,0:T(8,128)(2,1)S(1)}, bf16[2,96,1152]{2,1,0:T(8,128)(2,1)S(1)}, u32[]{:S(2)}, u32[]{:S(2)}) collective-permute-start(bf16[2,96,1152]{2,1,0:T(8,128)(2,1)S(1)} %slice.378), channel_id=1, source_target_pairs={{0,16},{2,18},{4,20},{6,22},{8,24},{10,26},{12,28},{14,30},{16,0},... | collective-permute-start | bytes 1327112 | tf_op jit(solution)/shard_map/ppermute | solution.py:27
  268.1 25.4 %collective-permute-start.40 = (bf16[640,1536]{1,0:T(8,128)(2,1)S(1)}, bf16[640,1536]{1,0:T(8,128)(2,1)}, u32[]{:S(2)}, u32[]{:S(2)}) collective-permute-start(bf16[640,1536]{1,0:T(8,128)(2,1)S(1)} %collective-permute-done.36), channel_id=1, source_target_pairs={{0,2},{2,0},{4,6},{6,4},{8,10},{10,8},{12,14},{14,12},{16,18},{18,... | collective-permute-start | bytes 5898248 | tf_op jit(solution)/shard_map/ppermute | solution.py:27
  270.3 27.0 %collective-permute-start.41 = (bf16[320,1536]{1,0:T(8,128)(2,1)}, bf16[320,1536]{1,0:T(8,128)(2,1)S(1)}, u32[]{:S(2)}, u32[]{:S(2)}) collective-permute-start(bf16[320,1536]{1,0:T(8,128)(2,1)} %slice.379), channel_id=1, source_target_pairs={{0,8},{1,9},{2,3},{3,2},{4,12},{5,13},{6,7},{7,6},{8,0},{9,1},{10,... | collective-permute-start | bytes 2949128 | tf_op jit(solution)/shard_map/ppermute | solution.py:38
  271.4 25.9 %collective-permute-start.42 = (bf16[4,96,1152]{2,1,0:T(8,128)(2,1)S(1)}, bf16[4,96,1152]{2,1,0:T(8,128)(2,1)S(1)}, u32[]{:S(2)}, u32[]{:S(2)}) collective-permute-start(bf16[4,96,1152]{2,1,0:T(8,128)(2,1)S(1)} %pad_maximum_fusion.22.refs_0_), channel_id=1, source_target_pairs={{0,4},{2,6},{4,0},{6,2},{8,12},{10,14},{12,8},{14,10},{16,20},{18,... | collective-permute-start | bytes 2654216 | tf_op jit(solution)/shard_map/ppermute | solution.py:27
  272.0 31.8 %collective-permute-start.44 = (bf16[640,1536]{1,0:T(8,128)(2,1)}, bf16[640,1536]{1,0:T(8,128)(2,1)}, u32[]{:S(2)}, u32[]{:S(2)}) collective-permute-start(bf16[640,1536]{1,0:T(8,128)(2,1)} %pad_maximum_fusion.9), channel_id=1, source_target_pairs={{0,2},{2,0},{4,6},{6,4},{8,10},{10,8},{12,14},{14,12},{16,18},{18,... | collective-permute-start | bytes 5898248 | tf_op jit(solution)/shard_map/ppermute | solution.py:27
  352.7 29.0 %collective-permute-start.46 = (bf16[4,96,1152]{2,1,0:T(8,128)(2,1)S(1)}, bf16[4,96,1152]{2,1,0:T(8,128)(2,1)S(1)}, u32[]{:S(2)}, u32[]{:S(2)}) collective-permute-start(bf16[4,96,1152]{2,1,0:T(8,128)(2,1)S(1)} %bitcast.271), channel_id=1, source_target_pairs={{0,4},{2,6},{4,0},{6,2},{8,12},{10,14},{12,8},{14,10},{16,20},{18,... | collective-permute-start | bytes 2654216 | tf_op jit(solution)/shard_map/ppermute | solution.py:27
  389.3 34.3 %collective-permute-start.48 = (bf16[640,1536]{1,0:T(8,128)(2,1)}, bf16[640,1536]{1,0:T(8,128)(2,1)S(1)}, u32[]{:S(2)}, u32[]{:S(2)}) collective-permute-start(bf16[640,1536]{1,0:T(8,128)(2,1)} %add_convert_fusion.1), channel_id=1, source_target_pairs={{0,8},{1,9},{2,3},{3,2},{4,12},{5,13},{6,7},{7,6},{8,0},{9,1},{10,... | collective-permute-start | bytes 5898248 | tf_op jit(solution)/shard_map/ppermute | solution.py:38
  390.2 31.4 %collective-permute-start.49 = (bf16[4,96,1152]{2,1,0:T(8,128)(2,1)S(1)}, bf16[4,96,1152]{2,1,0:T(8,128)(2,1)S(1)}, u32[]{:S(2)}, u32[]{:S(2)}) collective-permute-start(bf16[4,96,1152]{2,1,0:T(8,128)(2,1)S(1)} %bitcast.270), channel_id=1, source_target_pairs={{0,4},{2,6},{4,0},{6,2},{8,12},{10,14},{12,8},{14,10},{16,20},{18,... | collective-permute-start | bytes 2654216 | tf_op jit(solution)/shard_map/ppermute | solution.py:27
  391.8 30.3 %collective-permute-start.50 = (bf16[2,96,1152]{2,1,0:T(8,128)(2,1)S(1)}, bf16[2,96,1152]{2,1,0:T(8,128)(2,1)S(1)}, u32[]{:S(2)}, u32[]{:S(2)}) collective-permute-start(bf16[2,96,1152]{2,1,0:T(8,128)(2,1)S(1)} %slice.382), channel_id=1, source_target_pairs={{0,16},{2,18},{4,20},{6,22},{8,24},{10,26},{12,28},{14,30},{16,0},... | collective-permute-start | bytes 1327112 | tf_op jit(solution)/shard_map/ppermute | solution.py:27
  498.9 31.5 %collective-permute-start.58 = (bf16[4,96,1152]{2,1,0:T(8,128)(2,1)S(1)}, bf16[4,96,1152]{2,1,0:T(8,128)(2,1)S(1)}, u32[]{:S(2)}, u32[]{:S(2)}) collective-permute-start(bf16[4,96,1152]{2,1,0:T(8,128)(2,1)S(1)} %bitcast.269), channel_id=1, source_target_pairs={{0,4},{2,6},{4,0},{6,2},{8,12},{10,14},{12,8},{14,10},{16,20},{18,... | collective-permute-start | bytes 2654216 | tf_op jit(solution)/shard_map/ppermute | solution.py:27
  500.7 29.7 %collective-permute-start.59 = (bf16[2,96,1152]{2,1,0:T(8,128)(2,1)S(1)}, bf16[2,96,1152]{2,1,0:T(8,128)(2,1)S(1)}, u32[]{:S(2)}, u32[]{:S(2)}) collective-permute-start(bf16[2,96,1152]{2,1,0:T(8,128)(2,1)S(1)} %get-tuple-element.546), channel_id=1, source_target_pairs={{0,8},{2,10},{4,12},{6,14},{8,0},{10,2},{12,4},{14,6},{16,24},{18,... | collective-permute-start | bytes 1327112 | tf_op jit(solution)/shard_map/ppermute | solution.py:27
  501.2 29.2 %collective-permute-start.57 = (bf16[2,96,1152]{2,1,0:T(8,128)(2,1)S(1)}, bf16[2,96,1152]{2,1,0:T(8,128)(2,1)S(1)}, u32[]{:S(2)}, u32[]{:S(2)}) collective-permute-start(bf16[2,96,1152]{2,1,0:T(8,128)(2,1)S(1)} %slice.390), channel_id=1, source_target_pairs={{0,16},{2,18},{4,20},{6,22},{8,24},{10,26},{12,28},{14,30},{16,0},... | collective-permute-start | bytes 1327112 | tf_op jit(solution)/shard_map/ppermute | solution.py:27
  508.4 39.4 %collective-permute-start.61 = (bf16[1,96,1152]{2,1,0:T(8,128)(2,1)S(1)}, bf16[1,96,1152]{2,1,0:T(8,128)(2,1)S(1)}, u32[]{:S(2)}, u32[]{:S(2)}) collective-permute-start(bf16[1,96,1152]{2,1,0:T(8,128)(2,1)S(1)} %slice.393), channel_id=1, source_target_pairs={{0,16},{2,18},{4,20},{6,22},{8,24},{10,26},{12,28},{14,30},{16,0},... | collective-permute-start | bytes 663560 | tf_op jit(solution)/shard_map/ppermute | solution.py:27
  562.6 25.5 %collective-permute-start.63 = (bf16[640,1536]{1,0:T(8,128)(2,1)}, bf16[640,1536]{1,0:T(8,128)(2,1)}, u32[]{:S(2)}, u32[]{:S(2)}) collective-permute-start(bf16[640,1536]{1,0:T(8,128)(2,1)} %slice.408), channel_id=1, source_target_pairs={{0,2},{2,0},{4,6},{6,4},{8,10},{10,8},{12,14},{14,12},{16,18},{18,... | collective-permute-start | bytes 5898248 | tf_op jit(solution)/shard_map/ppermute | solution.py:27
  608.2 32.9 %collective-permute-start.67 = (bf16[2,8,96,1792]{3,2,1,0:T(8,128)(2,1)}, bf16[2,8,96,1792]{3,2,1,0:T(8,128)(2,1)}, u32[]{:S(2)}, u32[]{:S(2)}) collective-permute-start(bf16[2,8,96,1792]{3,2,1,0:T(8,128)(2,1)} %dynamic-slice_bitcast_fusion), channel_id=1, source_target_pairs={{0,2},{2,0},{4,6},{6,4},{8,10},{10,8},{12,14},{14,12},{16,18},{18,... | collective-permute-start | bytes 16515080 | tf_op jit(solution)/shard_map/ppermute | solution.py:27
  611.6 29.6 %collective-permute-start.68 = (bf16[640,1536]{1,0:T(8,128)(2,1)}, bf16[640,1536]{1,0:T(8,128)(2,1)S(1)}, u32[]{:S(2)}, u32[]{:S(2)}) collective-permute-start(bf16[640,1536]{1,0:T(8,128)(2,1)} %add_convert_fusion), channel_id=1, source_target_pairs={{0,8},{1,9},{2,3},{3,2},{4,12},{5,13},{6,7},{7,6},{8,0},{9,1},{10,... | collective-permute-start | bytes 5898248 | tf_op jit(solution)/shard_map/ppermute | solution.py:38
  656.0 27.6 %collective-permute-start.72 = (bf16[2,2,2,96,640]{4,3,2,1,0:T(8,128)(2,1)}, bf16[2,2,2,96,640]{4,3,2,1,0:T(8,128)(2,1)}, u32[]{:S(2)}, u32[]{:S(2)}) collective-permute-start(bf16[2,2,2,96,640]{4,3,2,1,0:T(8,128)(2,1)} %get-tuple-element.525), channel_id=1, source_target_pairs={{0,4},{2,6},{4,0},{6,2},{8,12},{10,14},{12,8},{14,10},{16,20},{18,... | collective-permute-start | bytes 2949128 | tf_op jit(solution)/shard_map/ppermute | solution.py:27
  658.1 25.5 %collective-permute-start.73 = (bf16[2,2,2,96,512]{4,3,2,1,0:T(8,128)(2,1)}, bf16[2,2,2,96,512]{4,3,2,1,0:T(8,128)(2,1)}, u32[]{:S(2)}, u32[]{:S(2)}) collective-permute-start(bf16[2,2,2,96,512]{4,3,2,1,0:T(8,128)(2,1)} %get-tuple-element.529), channel_id=1, source_target_pairs={{0,8},{2,10},{4,12},{6,14},{8,0},{10,2},{12,4},{14,6},{16,24},{18,... | collective-permute-start | bytes 2359304 | tf_op jit(solution)/shard_map/ppermute | solution.py:27
  660.8 30.2 %collective-permute-start.74 = (bf16[320,1536]{1,0:T(8,128)(2,1)}, bf16[320,1536]{1,0:T(8,128)(2,1)}, u32[]{:S(2)}, u32[]{:S(2)}) collective-permute-start(bf16[320,1536]{1,0:T(8,128)(2,1)} %slice.585), channel_id=1, source_target_pairs={{0,1},{1,0},{2,10},{3,11},{4,5},{5,4},{6,14},{7,15},{8,9},{9,8},{1... | collective-permute-start | bytes 2949128 | tf_op jit(solution)/shard_map/ppermute | solution.py:38
  692.6 29.2 %collective-permute-start.83 = (bf16[2,2,96,512]{3,2,1,0:T(8,128)(2,1)S(1)}, bf16[2,2,96,512]{3,2,1,0:T(8,128)(2,1)S(1)}, u32[]{:S(2)}, u32[]{:S(2)}) collective-permute-start(bf16[2,2,96,512]{3,2,1,0:T(8,128)(2,1)S(1)} %get-tuple-element.554), channel_id=1, source_target_pairs={{0,1},{1,0},{2,3},{3,2},{4,5},{5,4},{6,7},{7,6},{8,9},{9,8},{10,11... | collective-permute-start | bytes 1179656 | tf_op jit(solution)/shard_map/ppermute | solution.py:27
  695.3 26.4 %collective-permute-start.82 = (bf16[2,2,96,640]{3,2,1,0:T(8,128)(2,1)S(1)}, bf16[2,2,96,640]{3,2,1,0:T(8,128)(2,1)S(1)}, u32[]{:S(2)}, u32[]{:S(2)}) collective-permute-start(bf16[2,2,96,640]{3,2,1,0:T(8,128)(2,1)S(1)} %get-tuple-element.536), channel_id=1, source_target_pairs={{0,8},{2,10},{4,12},{6,14},{8,0},{10,2},{12,4},{14,6},{16,24},{18,... | collective-permute-start | bytes 1474568 | tf_op jit(solution)/shard_map/ppermute | solution.py:27
  (180 other events, 1942.3 us)

commit v2 on v0

v2 whole, which is shorter than its diff:
```python
import math

import jax
import jax.numpy as jnp
from jax import lax
from jax.experimental import pallas as pl
from jax.experimental.pallas import tpu as pltpu
from jax.sharding import PartitionSpec as P

HEADS = 12
KV = 2
HD = 128

CORE = 1
NEAR = 4
SIDE = 2
LANES = 128
STEP = 320
SCALE = 64
VMEM = 60 << 20

norm_eps = 1e-06
rope_base = 1000000.0


def swap(values, axis, bit):
    count = lax.axis_size(axis)
    return lax.ppermute(values, axis, [(i, i ^ bit) for i in range(count)])


def swap_both(values, evens, odds):
    fsdp, tp = lax.axis_size("fsdp"), lax.axis_size("tp")
    pairs = []
    for f in range(fsdp):
        for t in range(tp):
            axis, bit = odds if f % 2 else evens
            to = (f, t ^ bit) if axis == "tp" else (f ^ bit, t)
            pairs.append((f * tp + t, to[0] * tp + to[1]))
    return lax.ppermute(values, ("fsdp", "tp"), pairs)


def own_bit(axis, bit):
    return lax.rem(lax.div(lax.axis_index(axis), bit), 2)


def far_bits():
    count = lax.axis_size("fsdp")
    bits = []
    bit = count // 2
    while bit >= 8:
        bits.append(bit)
        bit //= 2
    return bits


def choose(flag, first, second):
    return jnp.where(flag == 0, first, second)


def rope_tables(position):
    half_width = HD // 2
    freqs = jnp.exp(jnp.arange(half_width, dtype=jnp.float32) * (-2.0 * math.log(rope_base) / HD))
    angles = position.astype(jnp.float32)[:, None] * freqs[None, :]
    cosine = jnp.cos(angles)
    sine = jnp.sin(angles)
    return (jnp.concatenate([cosine, cosine], 1), jnp.concatenate([sine, -sine], 1))


def unrotate(grads, cosine, sine):
    half_width = grads.shape[-1] // 2
    turned = jnp.concatenate([grads[..., half_width:], grads[..., :half_width]], -1)
    return grads * cosine[:, None, :] + turned * sine[:, None, :]


def root_scale(values):
    return lax.rsqrt(jnp.mean(values * values, axis=1, keepdims=True) + norm_eps)


def norm_back(grad_normed, gain, hat_rows, scale_rows):
    scaled = grad_normed * gain[None, :]
    return scale_rows * (scaled - hat_rows * jnp.mean(scaled * hat_rows, axis=1, keepdims=True))


def segment_of(rows, seq_lens):
    seq_ends = jnp.cumsum(seq_lens)
    seq_starts = seq_ends - seq_lens
    slot_ids = jnp.arange(seq_lens.shape[0], dtype=jnp.int32)
    segment = jnp.sum((rows[:, None] >= seq_ends[None, :]).astype(jnp.int32), axis=1)
    member = (segment[:, None] == slot_ids[None, :]).astype(jnp.int32)
    position = rows - jnp.sum(member * seq_starts[None, :], axis=1)
    return segment, position


def here():
    return jnp.stack([lax.axis_index("tp"), lax.axis_index("fsdp")]).astype(jnp.int32)


def place_blocks(arrays, moves, out_shapes):
    def kernel(place_ref, *refs):
        ins, outs, sems = refs[: len(arrays)], refs[len(arrays) : -1], refs[-1]
        copies = []
        for array, index, columns, number, part, block, there in moves:
            source, target = ins[array].at[index], outs[number]
            if part is not None:
                target = target.at[place_ref[0] ^ part]
            target = target.at[place_ref[1] ^ block]
            rows = target.shape[0]
            if columns is not None:
                source = source.at[pl.ds(0, rows), pl.ds(columns[0], columns[1])]
                target = target.at[:, pl.ds(there, columns[1])]
            copies.append(pltpu.make_async_copy(source, target, sems.at[len(copies)]))
        for copy in copies:
            copy.start()
        for copy in copies:
            copy.wait()

    size = sum(math.prod(shape) * 2 for shape in out_shapes)
    return pl.pallas_call(
        kernel,
        out_shape=[jax.ShapeDtypeStruct(shape, jnp.bfloat16) for shape in out_shapes],
        in_specs=[pl.BlockSpec(memory_space=pltpu.SMEM)]
        + [pl.BlockSpec(memory_space=pl.ANY)] * len(arrays),
        out_specs=[pl.BlockSpec(memory_space=pltpu.VMEM)] * len(out_shapes),
        scratch_shapes=[pltpu.SemaphoreType.DMA((len(moves),))],
        compiler_params=pltpu.CompilerParams(vmem_limit_bytes=VMEM),
        cost_estimate=pl.CostEstimate(flops=0, bytes_accessed=2 * size, transcendentals=0),
    )(here(), *arrays)


def bundle(arrays, moves, shape):
    block = shape[-2] // lax.axis_size("fsdp")
    if block % 16 == 0:
        return (arrays, moves, shape, block)
    split = shape[:-2] + (lax.axis_size("fsdp"), block, shape[-1])
    moves = [(move[0], move[1], move[2], 0) + move[3:] for move in moves]
    return ([place_blocks(arrays, moves, [split])[0].reshape(shape)], None, shape, block)


def bundle_copies(item, refs, place_ref, target, sems, first):
    _, moves, _, block = item
    if moves is None:
        return [pltpu.make_async_copy(refs[0], target, sems.at[first])]
    copies = []
    for array, index, columns, part, rel, there in moves:
        source = refs[array].at[index]
        row = pl.ds(pl.multiple_of((place_ref[1] ^ rel) * block, 16), block)
        there_part = target if part is None else target.at[place_ref[0] ^ part]
        if columns is None:
            there_part = there_part.at[row]
        else:
            source = source.at[:, pl.ds(columns[0], columns[1])]
            there_part = there_part.at[row, pl.ds(there, columns[1])]
        copies.append(pltpu.make_async_copy(source, there_part, sems.at[first + len(copies)]))
    return copies


def run_kernel(kernel, steps, operands, specs, bundles, outs, out_specs, flops):
    arrays = [array for item in bundles for array in item[0]]
    counts = [1 if item[1] is None else len(item[1]) for item in bundles]

    def wrapped(place_ref, *refs):
        ins, refs = refs[: len(operands)], refs[len(operands) :]
        parts, refs = refs[: len(arrays)], refs[len(arrays) :]
        results, refs = refs[: len(outs)], refs[len(outs) :]
        targets = refs[: len(bundles)]
        step = pl.program_id(0)
        if bundles:

            @pl.when(step == 0)
            def _():
                copies, first, array = [], 0, 0
                for item, target, count in zip(bundles, targets, counts):
                    own = parts[array : array + len(item[0])]
                    copies += bundle_copies(item, own, place_ref, target, refs[-1], first)
                    first += count
                    array += len(item[0])
                for copy in copies:
                    copy.start()
                for copy in copies:
                    copy.wait()

        kernel(step, ins, targets, results)

    scratch = [pltpu.VMEM(item[2], jnp.bfloat16) for item in bundles]
    if bundles:
        scratch.append(pltpu.SemaphoreType.DMA((sum(counts),)))
    size = sum(math.prod(v.shape) * v.dtype.itemsize for v in [*operands, *arrays, *outs])
    return pl.pallas_call(
        wrapped,
        out_shape=outs,
        grid=(steps,),
        in_specs=[pl.BlockSpec(memory_space=pltpu.SMEM)]
        + specs
        + [pl.BlockSpec(memory_space=pl.ANY)] * len(arrays),
        out_specs=out_specs,
        scratch_shapes=scratch,
        compiler_params=pltpu.CompilerParams(vmem_limit_bytes=VMEM),
        cost_estimate=pl.CostEstimate(
            flops=flops // SCALE, bytes_accessed=size // SCALE, transcendentals=0
        ),
    )(here(), *operands, *arrays)


def shaped(shape, dtype=jnp.bfloat16):
    return jax.ShapeDtypeStruct(shape, dtype)


def full_spec(value):
    return pl.BlockSpec(value.shape, lambda i: (0,) * len(value.shape))


def send_units(shards, quarter):
    units = shards[0].shape[1]
    core, near = own_bit("fsdp", CORE), own_bit("fsdp", NEAR)
    padded = jnp.stack([jnp.pad(shard, ((0, 0), (0, 4 * quarter - units))) for shard in shards])
    low, high = padded[..., : 2 * quarter], padded[..., 2 * quarter :]
    kept, got = choose(core, low, high), swap(choose(core, high, low), "fsdp", CORE)

    def halves(kept, got):
        pair = jnp.stack([kept, got], axis=1)
        low, high = pair[..., :quarter], pair[..., quarter:]
        return choose(near, low, high), choose(near, high, low)

    return kept, got, halves


INNER = [0, CORE, NEAR, NEAR | CORE]


def far_units(quad, low, high):
    pieces = far_gather(quad[low:high])
    return [(p, [rel | INNER[i] for i in range(low, high)]) for rel, p in pieces.items() if rel]


def side_units(pieces):
    arrays = jnp.concatenate([array for array, _ in pieces])
    places = [place | SIDE for _, marks in pieces for place in marks]
    return [(swap(arrays, "fsdp", SIDE), places)]


def part_of(pieces, low, high):
    return [(array[low:high], marks[low:high]) for array, marks in pieces]


def pick_units(piece, low, high):
    array, marks = piece
    return (array, marks, low, high)


def unit_bundle(pieces):
    count = lax.axis_size("fsdp")
    _, block, quarter = pieces[0][0].shape
    moves = [
        (number, i, None, None, piece[1][i], None)
        for number, piece in enumerate(pieces)
        for i in range(*(piece[2:] or (0, len(piece[1]))))
    ]
    return bundle([piece[0] for piece in pieces], moves, (count * block, quarter))


def tie(*values):
    leaves, form = jax.tree.flatten(values)
    arrays = [i for i, leaf in enumerate(leaves) if isinstance(leaf, jax.Array)]
    for i, leaf in zip(arrays, lax.optimization_barrier([leaves[i] for i in arrays])):
        leaves[i] = leaf
    return jax.tree.unflatten(form, leaves)


def add_pair(own, got):
    return slim(wide(own) + wide(got))


def far_sums(pieces):
    for bit in far_bits():
        merged = {}
        for rel in [key for key in pieces if key & bit]:
            got = swap(pieces[rel], "fsdp", bit)
            other = rel ^ bit
            merged[other] = add_pair(pieces[other], got) if other in pieces else got
        pieces = merged
    return pieces[0]


def share_near(total):
    return total[:2], swap(total[2:], "fsdp", NEAR)


def share_cores(pairs, units):
    core, near = own_bit("fsdp", CORE), own_bit("fsdp", NEAR)
    keep, got = jnp.stack([keep for keep, _ in pairs]), jnp.stack([got for _, got in pairs])
    both = jnp.concatenate([choose(near, keep, got), choose(near, got, keep)], axis=3)
    keep, got = both[:, 0], swap(both[:, 1], "fsdp", CORE)
    both = jnp.concatenate([choose(core, keep, got), choose(core, got, keep)], axis=2)
    return [wide(both[i, :, :units]) for i in range(len(pairs))]


def links():
    return [("tp", 1), ("fsdp", SIDE), ("fsdp", NEAR)]


def thirds(width):
    tiles = width // LANES
    cuts = [(tiles + 2 - i) // 3 * LANES for i in range(3)]
    starts = [0, cuts[0], cuts[0] + cuts[1]]
    return list(zip(starts, cuts))


def step_all(parts, marks, step):
    for turn in range(3):
        axis, bit = links()[(turn + step) % 3]
        parts[turn] = jnp.concatenate([parts[turn], swap(parts[turn], axis, bit)])
        marks[turn] = marks[turn] + [
            (part | bit, rel) if axis == "tp" else (part, rel | bit) for part, rel in marks[turn]
        ]


def joint_moves(marks, widths):
    spans, start = [], 0
    for item in widths:
        spans.append((start, start + item))
        start += item
    moves = [[] for _ in widths]
    for turn, (first, size) in enumerate(thirds(start)):
        for other in range(2):
            for index, (part, rel) in enumerate(marks[turn]):
                for number, (low, high) in enumerate(spans):
                    begin, end = max(low, first), min(high, first + size)
                    if begin < end:
                        columns = (begin - first, end - begin)
                        rel_there = rel | CORE if other else rel
                        moves[number].append(
                            (turn + 3 * other, index, columns, part, rel_there, begin - low)
                        )
    return moves


def far_gather(values):
    pieces = {0: values}
    for bit in far_bits():
        pieces.update({rel | bit: swap(piece, "fsdp", bit) for rel, piece in list(pieces.items())})
    return pieces


def scatter_step(piece, names, link):
    axis, bit = link
    dim = names.index(link)
    mine = own_bit(axis, bit)
    got = swap(lax.dynamic_index_in_dim(piece, mine ^ 1, dim, keepdims=False), axis, bit)
    keep = lax.dynamic_index_in_dim(piece, mine, dim, keepdims=False)
    return (keep, got), names[:dim] + names[dim + 1 :]


def far_totals(piece):
    for bit in far_bits():
        mine = own_bit("fsdp", bit)
        got = swap(lax.dynamic_index_in_dim(piece, mine ^ 1, 0, keepdims=False), "fsdp", bit)
        keep = lax.dynamic_index_in_dim(piece, mine, 0, keepdims=False)
        total = wide(keep) + wide(got)
        piece = slim(total)
    return total


def scatter_small(values):
    flag = own_bit("tp", 1)
    keep = choose(flag, values[0], values[1])
    values = keep + swap(choose(flag, values[1], values[0]), "tp", 1)
    bit = lax.axis_size("fsdp") // 2
    while bit:
        flag = own_bit("fsdp", bit)
        keep = choose(flag, values[:bit], values[bit:])
        values = keep + swap(choose(flag, values[bit:], values[:bit]), "fsdp", bit)
        bit //= 2
    return values[0]


X, Z = ("tp", 1), ("fsdp", NEAR)


def spread_first(rows):
    return jnp.concatenate([rows, swap_both(rows, X, Z)])


def spread_second(rows):
    return swap_both(rows, Z, X)


def wide(values):
    return values.astype(jnp.float32)


def slim(values):
    return values.astype(jnp.bfloat16)


def dot(a, b):
    return jnp.dot(a, b, preferred_element_type=jnp.float32)


def dot_last(a, b):
    return lax.dot_general(a, b, (((1,), (1,)), ((), ())), preferred_element_type=jnp.float32)


def dot_first(a, b):
    return lax.dot_general(a, b, (((0,), (0,)), ((), ())), preferred_element_type=jnp.float32)


def project(tokens, gain, bias, cosine, sine, weights):
    rows, depth = tokens.shape
    columns = weights[2][2]
    tiles = columns // (2 * HD)

    def kernel(step, ins, targets, outs):
        tokens_ref, gain_ref, bias_ref, cosine_ref, sine_ref = ins
        values = wide(tokens_ref[...])
        scale = lax.rsqrt(jnp.mean(values * values, axis=1, keepdims=True) + norm_eps)
        normed = slim(values * scale * gain_ref[...])
        outs[0][...] = normed
        cos, sin = cosine_ref[...], sine_ref[...]
        for t in range(KV):
            for c in range(tiles):
                span = slice(c * 2 * HD, (c + 1) * 2 * HD)
                total = dot(normed, targets[0][t, :, span]) + bias_ref[t : t + 1, span]
                for j in range(2):
                    part = total[:, j * HD : (j + 1) * HD]
                    if (c, j) != (tiles - 1, 1):
                        part = part * cos - pltpu.roll(part, HD // 2, 1) * sin
                    number = 2 * c + j
                    if c < tiles - 1:
                        at = (t * (tiles - 1) * 2 + number) * HD
                        outs[1][:, at : at + HD] = slim(part)
                    else:
                        at = (t * 2 + j) * HD
                        outs[2][:, at : at + HD] = slim(part)

    operands = [tokens, gain, bias, cosine, sine]
    outs = [shaped((rows, depth)), shaped((rows, HEADS * HD)), shaped((rows, 2 * KV * HD))]
    return run_kernel(
        kernel, 1, operands, [full_spec(v) for v in operands], [weights], outs,
        [full_spec(v) for v in outs], 2 * rows * depth * KV * columns,
    )


def softmax_rows(query, keys, mask):
    scores = dot_last(query, keys) * HD ** (-0.5) + mask
    expd = jnp.exp(scores - jnp.max(scores, axis=1, keepdims=True))
    return expd / jnp.sum(expd, axis=1, keepdims=True)


def head_specs(count, total):
    group = HEADS // KV
    return [
        pl.BlockSpec((count, HD), lambda h: (0, h)),
        pl.BlockSpec((total, HD), lambda h: (0, h // group * 2)),
        pl.BlockSpec((total, HD), lambda h: (0, h // group * 2 + 1)),
        pl.BlockSpec((count, total), lambda h: (0, 0)),
    ]


def attend(queries, keys_values, mask):
    count, total = mask.shape

    def kernel(step, ins, targets, outs):
        probs = softmax_rows(ins[0][...], ins[1][...], ins[3][...])
        outs[0][...] = slim(dot(slim(probs), ins[2][...]))

    return run_kernel(
        kernel, HEADS, [queries, keys_values, keys_values, mask], head_specs(count, total), [],
        [shaped(queries.shape)], [pl.BlockSpec((count, HD), lambda h: (0, h))],
        4 * HEADS * count * total * HD,
    )[0]


def attend_back(queries, keys_values, mask, grad_mixed, cosine, sine):
    count, total = mask.shape
    group = HEADS // KV

    def kernel(step, ins, targets, outs):
        query, keys, grad = ins[0][...], ins[1][...], ins[4][...]
        probs = softmax_rows(query, keys, ins[3][...])
        grad_probs = dot_last(grad, ins[2][...])
        inner = jnp.sum(probs * grad_probs, axis=1, keepdims=True)
        grad_scores = slim(probs * (grad_probs - inner))
        grad_values = dot_first(slim(probs), grad)
        grad_keys = dot_first(grad_scores, query) * HD ** (-0.5)
        first = step % group == 0

        @pl.when(first)
        def _():
            outs[1][...] = grad_keys
            outs[2][...] = grad_values

        @pl.when(jnp.logical_not(first))
        def _():
            outs[1][...] += grad_keys
            outs[2][...] += grad_values

        part = dot(grad_scores, keys) * HD ** (-0.5)
        part = part * ins[5][...] + pltpu.roll(part, HD // 2, 1) * ins[6][...]
        outs[0][...] = slim(part)

    specs = head_specs(count, total) + [
        pl.BlockSpec((count, HD), lambda h: (0, h)),
        full_spec(cosine),
        full_spec(sine),
    ]
    sums = shaped((total, KV * HD), jnp.float32)
    return run_kernel(
        kernel, HEADS, [queries, keys_values, keys_values, mask, grad_mixed, cosine, sine], specs, [],
        [shaped(queries.shape), sums, sums],
        [
            pl.BlockSpec((count, HD), lambda h: (0, h)),
            pl.BlockSpec((total, HD), lambda h: (0, h // group)),
            pl.BlockSpec((total, HD), lambda h: (0, h // group)),
        ],
        10 * HEADS * count * total * HD,
    )


def finish_keys(grad_keys, grad_values, other, grad_query, cosine, sine):
    rows = other.shape[0]

    def kernel(step, ins, targets, outs):
        for t in range(KV):
            span = slice(t * HD, (t + 1) * HD)
            keys = ins[0][:, span] + wide(ins[2][:, span])
            keys = keys * ins[4][...] + pltpu.roll(keys, HD // 2, 1) * ins[5][...]
            there = slice((KV + t) * HD, (KV + t + 1) * HD)
            values = ins[1][:, span] + wide(ins[2][:, there])
            outs[0][:, 2 * t * HD : (2 * t + 1) * HD] = slim(keys)
            outs[0][:, (2 * t + 1) * HD : (2 * t + 2) * HD] = slim(values)
        outs[1][...] = jnp.sum(wide(ins[3][...]), axis=0, keepdims=True)
        outs[2][...] = jnp.sum(wide(outs[0][...]), axis=0, keepdims=True)

    half = pl.BlockSpec((rows, KV * HD), lambda i: (0, 0))
    operands = [grad_keys, grad_values, other, grad_query, cosine, sine]
    outs = [
        shaped((rows, 2 * KV * HD)),
        shaped((1, HEADS * HD), jnp.float32),
        shaped((1, 2 * KV * HD), jnp.float32),
    ]
    return run_kernel(
        kernel, 1, operands, [half, half] + [full_spec(v) for v in operands[2:]], [], outs,
        [full_spec(v) for v in outs], 0,
    )


def project_out(mixed, tokens, gain, weights):
    def kernel(step, ins, targets, outs):
        columns = weights[2][2]
        hidden = wide(ins[1][...])
        for t in range(KV):
            hidden = hidden + dot_last(ins[0][:, t * columns : (t + 1) * columns], targets[0][t])
        outs[0][...] = hidden
        scale = lax.rsqrt(jnp.mean(hidden * hidden, axis=1, keepdims=True) + norm_eps)
        outs[1][...] = slim(hidden * scale * ins[2][...])

    operands = [mixed, tokens, gain]
    outs = [shaped(tokens.shape, jnp.float32), shaped(tokens.shape)]
    return run_kernel(
        kernel, 1, operands, [full_spec(v) for v in operands], [weights], outs,
        [full_spec(v) for v in outs], 2 * tokens.shape[0] * tokens.shape[1] * mixed.shape[1],
    )


def norm_parts(grad_normed, values, gain):
    scale = lax.rsqrt(jnp.mean(values * values, axis=1, keepdims=True) + norm_eps)
    hat = values * scale
    scaled = grad_normed * gain
    back = scale * (scaled - hat * jnp.mean(scaled * hat, axis=1, keepdims=True))
    return back, jnp.sum(grad_normed * hat, axis=0, keepdims=True)


def norm_back_out(grads, hidden, out_grad, gain, weights):
    rows, depth = hidden.shape
    columns = weights[2][2]

    def kernel(step, ins, targets, outs):
        total = wide(ins[0][...])
        for ref in ins[1 : len(grads)]:
            total = total + wide(ref[...])
        hidden_ref, out_grad_ref, gain_ref = ins[len(grads) :]
        back, outs[1][...] = norm_parts(total, hidden_ref[...], gain_ref[...])
        total = wide(out_grad_ref[...]) + back
        outs[0][...] = total
        branch = slim(total)
        outs[2][...] = branch
        for t in range(KV):
            outs[3][:, t * columns : (t + 1) * columns] = slim(dot(branch, targets[0][t]))

    operands = [*grads, hidden, out_grad, gain]
    outs = [
        shaped((rows, depth), jnp.float32),
        shaped((1, depth), jnp.float32),
        shaped((rows, depth)),
        shaped((rows, KV * columns)),
    ]
    specs = [pl.BlockSpec((rows, depth), lambda i: (0, 0))] * (len(grads) + 2) + [full_spec(gain)]
    return run_kernel(
        kernel, 1, operands, specs, [weights], outs, [full_spec(v) for v in outs],
        2 * rows * depth * KV * columns,
    )


def project_back(grad_query, grad_kv, tokens, grad_hidden, gain, weights):
    def kernel(step, ins, targets, outs):
        query, kv = HEADS // KV * HD, 2 * HD
        total = None
        for t in range(KV):
            part = dot_last(ins[0][:, t * query : (t + 1) * query], targets[0][t, :, :query])
            part += dot_last(ins[1][:, t * kv : (t + 1) * kv], targets[0][t, :, query:])
            total = part if total is None else total + part
        back, outs[1][...] = norm_parts(total, wide(ins[2][...]), ins[4][...])
        outs[0][...] = ins[3][...] + back

    operands = [grad_query, grad_kv, tokens, grad_hidden, gain]
    outs = [shaped(tokens.shape, jnp.float32), shaped((1, tokens.shape[1]), jnp.float32)]
    return run_kernel(
        kernel, 1, operands, [full_spec(v) for v in operands], [weights], outs,
        [full_spec(v) for v in outs], 4 * tokens.shape[0] * tokens.shape[1] * weights[2][2],
    )


def piece_specs(pieces):
    specs, start = [], 0
    for piece in pieces:
        steps = piece.shape[0] // STEP
        specs.append(
            pl.BlockSpec(
                (STEP, piece.shape[1]),
                lambda i, start=start, steps=steps: (jnp.clip(i - start, 0, steps - 1), 0),
            )
        )
        start += steps
    return specs, start


def pick_piece(step, refs, pieces):
    block, start = refs[0][...], 0
    for ref, piece in list(zip(refs, pieces))[1:]:
        start += piece.shape[0] // STEP
        block = jnp.where(step < start, block, ref[...])
        start = start
    return block


def gated(pieces, w_gate, w_up):
    specs, steps = piece_specs(pieces)
    depth, columns = w_gate[2]

    def kernel(step, ins, targets, outs):
        block = pick_piece(step, ins, pieces)
        gate, up = dot(block, targets[0][...]), dot(block, targets[1][...])
        outs[0][...] = slim(gate)
        outs[1][...] = slim(up)
        outs[2][...] = slim(gate * jax.nn.sigmoid(gate) * up)

    outs = [shaped((steps * STEP, columns))] * 3
    return run_kernel(
        kernel, steps, pieces, specs, [w_gate, w_up], outs,
        [pl.BlockSpec((STEP, columns), lambda i: (i, 0))] * 3, 4 * steps * STEP * depth * columns,
    )


def gated_back(pieces, gate, up, w_gate, w_up, w_down):
    specs, steps = piece_specs(pieces)
    depth, columns = w_gate[2]
    tile = columns // 3

    def kernel(step, ins, targets, outs):
        block = pick_piece(step, ins, pieces)
        for c in range(3):
            span = slice(c * tile, (c + 1) * tile)
            gate, up = wide(ins[-2][:, span]), wide(ins[-1][:, span])
            act = dot(block, targets[2][:, span])
            sigma = jax.nn.sigmoid(gate)
            outs[0][:, span] = slim(act * up * sigma * (1.0 + gate * (1.0 - sigma)))
            outs[1][:, span] = slim(act * gate * sigma)
        total = dot_last(outs[0][...], targets[0][...]) + dot_last(outs[1][...], targets[1][...])
        store_piece(step, outs[2:], pieces, slim(total))

    part = pl.BlockSpec((STEP, columns), lambda i: (i, 0))
    outs = [shaped((steps * STEP, columns))] * 2 + [shaped(piece.shape) for piece in pieces]
    return run_kernel(
        kernel, steps, pieces + [gate, up], specs + [part, part], [w_gate, w_up, w_down], outs,
        [part, part] + specs, 6 * steps * STEP * depth * columns,
    )


def store_piece(step, refs, pieces, value):
    start = 0
    for ref, piece in zip(refs, pieces):
        end = start + piece.shape[0] // STEP

        @pl.when((step >= start) & (step < end))
        def _(ref=ref):
            ref[...] = value

        start = end


def down_rows(acts, w_down, pieces):
    specs, steps = piece_specs(acts)
    depth, columns = w_down[2]
    owner, starts, place = [], [0, 0], 0
    for number, piece in enumerate(pieces):
        owner += [number % 2] * (piece.shape[0] // STEP)
    index = [owner[:i].count(owner[i]) for i in range(steps)]
    outs = [shaped((owner.count(side) * STEP, depth)) for side in range(2)]

    def kernel(step, ins, targets, results):
        block = pick_piece(step, ins, acts)
        value = slim(dot_last(block, targets[0][...]))
        mine = step >= steps
        for i in range(steps):
            if owner[i] == 0:
                mine = mine | (step == i)

        @pl.when(mine)
        def _():
            results[0][...] = value

        @pl.when(jnp.logical_not(mine))
        def _():
            results[1][...] = value

    def spec(side):
        def place_of(i):
            reached = 0
            for k in range(steps):
                if owner[k] == side and index[k] > 0:
                    reached = jnp.where(i >= k, index[k], reached)
            return (reached, 0)

        return pl.BlockSpec((STEP, depth), place_of)

    return run_kernel(
        kernel, steps, acts, specs, [w_down], outs, [spec(0), spec(1)],
        2 * steps * STEP * depth * columns,
    )


def weight_grad(lefts, rights):
    depth, columns = lefts[0].shape[1], rights[0].shape[1]
    count = lax.axis_size("fsdp")
    block = depth // count
    rels = [0]
    for bit in far_bits() + [SIDE]:
        rels += [rel | bit for rel in rels]
    direct = block % 16 == 0
    tile = 4 * block if direct else 2 * LANES
    steps = depth // tile
    total_rows = sum(left.shape[0] for left in lefts)

    def wrapped(place_ref, *refs):
        ins, refs = refs[: len(lefts) + len(rights)], refs[len(lefts) + len(rights) :]
        step = pl.program_id(0)
        total, number, row = None, len(lefts), 0
        for ref, left in zip(ins, lefts):
            part = dot_first(ref[...], ins[number][row : row + left.shape[0], :])
            total = part if total is None else total + part
            row += left.shape[0]
            if row == rights[number - len(lefts)].shape[0]:
                number, row = number + 1, 0
        if not direct:
            refs[0][...] = slim(total)
            return
        outs, held, sems = refs[: len(rels)], refs[-2], refs[-1]
        held[step] = slim(total).reshape(4, block, columns)

        @pl.when(step == steps - 1)
        def _():
            copies = []
            for out, rel in zip(outs, rels):
                for i, inner in enumerate(INNER):
                    number = place_ref[1] ^ (rel | inner)
                    source = held.at[lax.div(number, 4), lax.rem(number, 4)]
                    copies.append(pltpu.make_async_copy(source, out.at[i], sems.at[len(copies)]))
            for copy in copies:
                copy.start()
            for copy in copies:
                copy.wait()

    operands = [*lefts, *rights]
    specs = [pl.BlockSpec((left.shape[0], tile), lambda i: (0, i)) for left in lefts]
    specs += [full_spec(right) for right in rights]
    scratch = []
    if direct:
        outs = [shaped((4, block, columns)) for _ in rels]
        out_specs = [pl.BlockSpec(memory_space=pl.ANY)] * len(rels)
        scratch = [
            pltpu.VMEM((steps, 4, block, columns), jnp.bfloat16),
            pltpu.SemaphoreType.DMA((4 * len(rels),)),
        ]
    else:
        outs = [shaped((depth, columns))]
        out_specs = [pl.BlockSpec((tile, columns), lambda i: (i, 0))]
    results = pl.pallas_call(
        wrapped,
        out_shape=outs,
        grid=(steps,),
        in_specs=[pl.BlockSpec(memory_space=pltpu.SMEM)] + specs,
        out_specs=out_specs,
        scratch_shapes=scratch,
        compiler_params=pltpu.CompilerParams(vmem_limit_bytes=VMEM),
        cost_estimate=pl.CostEstimate(
            flops=2 * total_rows * depth * columns // SCALE,
            bytes_accessed=depth * columns // SCALE,
            transcendentals=0,
        ),
    )(here(), *operands)
    if direct:
        return dict(zip(rels, results))
    blocks = results[0].reshape(count, block, columns)
    places = lax.axis_index("fsdp") ^ jnp.array([rel | inner for rel in rels for inner in INNER])
    blocks = blocks[places].reshape(len(rels), 4, block, columns)
    return {rel: blocks[i] for i, rel in enumerate(rels)}


def joint_grad(lefts, rights, cuts):
    depth = lefts[0].shape[1]
    count = lax.axis_size("fsdp")
    block = depth // count
    direct = block % 16 == 0
    tile = 4 * block if direct else 2 * LANES
    rows = tile // 2 if direct else tile

    def kernel(step, ins, targets, outs):
        place_ref, held = targets
        for number in range(len(rights)):
            total = None
            for side in range(2):
                part = dot_first(ins[side][...], ins[2 + 2 * number + side][...])
                total = part if total is None else total + part
            held[: tile, : total.shape[1]] = slim(total)
            for out, (which, starts, length) in zip(outs, cuts):
                if which != number:
                    continue
                for t, start in enumerate(starts):
                    span = slice(start, start + length)
                    if not direct:
                        out[t] = held[:, span]
                        continue
                    for k in range(2):
                        first = (2 * k + lax.rem(place_ref[1], 2)) * block
                        first = pl.multiple_of(first, 16)
                        out[t, k * block : (k + 1) * block] = held[pl.ds(first, block), span]

    flat = [right for pair in rights for right in pair]
    outs = [shaped((2, depth * rows // tile, length)) for _, _, length in cuts]

    def wrapped(place_ref, *refs):
        ins, results = refs[: 2 + len(flat)], refs[2 + len(flat) : -1]
        kernel(pl.program_id(0), ins, (place_ref, refs[-1]), results)

    flops = sum(2 * right.shape[0] * depth * right.shape[1] for right in flat)
    results = pl.pallas_call(
        wrapped,
        out_shape=outs,
        grid=(depth // tile,),
        in_specs=[pl.BlockSpec(memory_space=pltpu.SMEM)]
        + [pl.BlockSpec((left.shape[0], tile), lambda i: (0, i)) for left in lefts]
        + [full_spec(right) for right in flat],
        out_specs=[pl.BlockSpec((2, rows, out.shape[2]), lambda i: (0, i, 0)) for out in outs],
        scratch_shapes=[pltpu.VMEM((tile, max(right.shape[1] for right in flat)), jnp.bfloat16)],
        compiler_params=pltpu.CompilerParams(vmem_limit_bytes=VMEM),
        cost_estimate=pl.CostEstimate(flops=flops // SCALE, bytes_accessed=0, transcendentals=0),
    )(here(), *lefts, *flat)
    if direct:
        return results
    core = own_bit("fsdp", CORE)
    views = [out.reshape(2, count // 2, 2, block, -1) for out in results]
    return [
        choose(core, view[:, :, 0], view[:, :, 1]).reshape(2, depth // 2, -1) for view in views
    ]


def body(
    tokens, seq_lens, gain_attn, gain_mlp, w_qkv, b_qkv, w_out, w_gate, w_up, w_down, cotangent
):
    rows, width = tokens.shape
    count = lax.axis_size("fsdp")
    block = w_qkv.shape[0]
    units = w_gate.shape[1]
    quarter = -(-units // (4 * LANES)) * LANES
    query_end = HEADS // KV * HD
    place = lax.axis_index("tp")

    own_rows = place * rows + jnp.arange(rows, dtype=jnp.int32)
    other_rows = (1 - place) * rows + jnp.arange(rows, dtype=jnp.int32)
    segment, position = segment_of(own_rows, seq_lens[0])
    other_segment, _ = segment_of(other_rows, seq_lens[0])
    key_rows = jnp.concatenate([own_rows, other_rows])
    key_segment = jnp.concatenate([segment, other_segment])
    allowed = (segment[:, None] == key_segment[None, :]) & (key_rows[None, :] <= own_rows[:, None])
    mask = jnp.where(allowed, 0.0, -1e30).astype(jnp.float32)
    valid = segment < seq_lens.shape[1]
    out_grad = cotangent * valid[:, None].astype(jnp.bfloat16)
    cosine, sine = rope_tables(position)

    small = jnp.concatenate([gain_attn, gain_mlp, b_qkv[0]])
    used = -(-small.shape[0] // LANES)
    small = jnp.pad(small, (0, block * LANES - small.shape[0])).reshape(block, LANES)
    joint = jnp.concatenate([w_qkv, w_out.T, small], axis=1)
    widths = [w_qkv.shape[1], w_out.shape[0], LANES]
    cuts = thirds(joint.shape[1])
    cut = cuts[0][1]
    kept, got, halves = send_units([w_gate, w_up, w_down.T], quarter)
    far = far_gather(joint[:, :cut])
    got, far, joint = tie(got, far, joint)
    kept, given = halves(kept, got)
    near_got = swap(given[0], *Z)
    far_rest = far_gather(joint[:, cut:])
    near_got, far_rest, mask, out_grad, cosine, sine = tie(
        near_got, far_rest, mask, out_grad, cosine, sine
    )
    quads = [jnp.concatenate([kept[0], near_got])]
    parts = [jnp.stack(list(far.values()))]
    far_rest = jnp.stack(list(far_rest.values()))
    parts += [far_rest[:, :, start - cut : start - cut + size] for start, size in cuts[1:]]
    marks = [[(0, rel) for rel in far]] * 3

    far_gate = []
    for step in range(3):
        step_all(parts, marks, step)
        piece = far_units(quads[0], step, step + 1)
        parts, piece, quads, given, out_grad = tie(parts, piece, quads, given, out_grad)
        far_gate += piece
    own_gate = [(quads[0], INNER)]

    others = [swap(part, "fsdp", CORE) for part in parts]
    near_got = swap(given[1], *Z)
    all_gate = side_units(part_of(own_gate, 0, 2))
    parts, others, near_got, all_gate, quads, out_grad, given, far_gate = tie(
        parts, others, near_got, all_gate, quads, out_grad, given, far_gate
    )
    quads.append(jnp.concatenate([kept[1], near_got]))
    own_up = [(quads[1], INNER)]

    moves = joint_moves(marks, widths)
    arrays = parts + others
    qkv_weights = bundle(arrays, moves[0], (2, width, widths[0]))
    out_weights = bundle(arrays, moves[1], (2, width, widths[1]))
    tops = [array[:, : min(block, 16)] for array in (arrays[2], arrays[5])]
    small_moves = [
        (move[0] // 3, move[1], (move[2][0], LANES), 0, move[3], move[4], 0) for move in moves[2]
    ]
    small = place_blocks(tops, small_moves, [(2, count, min(block, 16), LANES)])[0]
    small = wide(small[:, :, :used].reshape(2, count, -1))
    gain_one = small[0, :, :block].reshape(1, width)
    gain_two = small[0, :, block : 2 * block].reshape(1, width)
    bias = small[:, :, 2 * block : 2 * block + b_qkv.shape[1]].reshape(KV, -1)
    grad_first = spread_first(out_grad)
    piece_gate = far_units(quads[0], 3, 4)
    piece_side = side_units(part_of(own_gate, 2, 4) + far_gate[:1])
    normed_one, queries, own = project(tokens, gain_one, bias, cosine, sine, qkv_weights)
    own, grad_first, piece_gate, piece_side, given, quads, far_gate = tie(
        own, grad_first, piece_gate, piece_side, given, quads, far_gate
    )
    far_gate, all_gate = far_gate + piece_gate, all_gate + piece_side

    other = swap(own, "tp", 1)
    near_got = swap(given[2], *Z)
    far_up = far_units(quads[1], 0, 1)
    piece_side = side_units(far_gate[1:3])
    other, near_got, far_up, piece_side, quads, far_gate = tie(
        other, near_got, far_up, piece_side, quads, far_gate
    )
    all_gate = all_gate + piece_side
    quads.append(jnp.concatenate([kept[2], near_got]))
    own_down = [(quads[2], INNER)]

    keys_values = jnp.concatenate([own, other])
    mixed = attend(queries, keys_values, mask)
    piece_up = far_units(quads[1], 1, 2)
    all_up = side_units(part_of(own_up, 0, 3))
    mixed, piece_up, all_up, quads, far_gate = tie(mixed, piece_up, all_up, quads, far_gate)
    far_up += piece_up

    piece_up = far_units(quads[1], 2, 3)
    piece_side = side_units(part_of(own_up, 3, 4) + far_gate[3:])
    hidden, normed_two = project_out(mixed, tokens, gain_two, out_weights)
    normed_two, piece_up, piece_side, quads, far_up = tie(normed_two, piece_up, piece_side, quads, far_up)
    far_up, all_up = far_up + piece_up, all_up + piece_side

    normed_first = spread_first(normed_two)
    piece_up = far_units(quads[1], 3, 4)
    piece_side = side_units(far_up)
    own_sent = jnp.concatenate([normed_one, mixed], axis=1)
    normed_first, piece_up, piece_side, quads, grad_first, own_sent = tie(
        normed_first, piece_up, piece_side, quads, grad_first, own_sent
    )
    far_up, all_up = far_up + piece_up, all_up + piece_side

    normed_second = spread_second(normed_first)
    far_down = far_units(quads[2], 0, 1)
    all_up += side_units(far_up[3:] + part_of(own_down, 0, 3))
    normed_core = [swap(normed_first, "fsdp", CORE)]
    core_got = swap(own_sent, "fsdp", CORE)
    normed_second, far_down, all_up, normed_core, quads, grad_first, core_got = tie(
        normed_second, far_down, all_up, normed_core, quads, grad_first, core_got
    )

    normed_core.append(swap(normed_second, "fsdp", CORE))
    piece_down = far_units(quads[2], 1, 2)
    all_down = side_units(part_of(own_down, 3, 4) + far_down)
    grad_second = [spread_second(grad_first[:rows])]
    grad_core = [swap(grad_first, "fsdp", CORE)]
    gate_pieces = own_gate + far_gate + all_gate + [pick_units(all_up[1], 1, 2)]
    up_pieces = own_up + far_up + [all_up[0], pick_units(all_up[1], 0, 1), all_up[2]]
    up_pieces += [pick_units(all_up[3], 0, 1)]
    down_pieces = [pick_units(all_up[3], 1, 4)]
    gate_weights = unit_bundle(gate_pieces)
    up_weights = unit_bundle(up_pieces)
    normed_pieces = [[normed_first, normed_core[0]], None]
    gates, ups, acts = [[None, None] for _ in range(3)]
    gates[0], ups[0], acts[0] = gated(normed_pieces[0], gate_weights, up_weights)
    acts, normed_core, piece_down, all_down, grad_second, grad_core, grad_first, normed_second, far_down = tie(
        acts, normed_core, piece_down, all_down, grad_second, grad_core, grad_first, normed_second, far_down
    )

    far_down, all_down = far_down + piece_down, all_down
    normed_pieces[1] = [normed_second, normed_core[1]]
    piece_down = far_units(quads[2], 2, 4)
    all_down += side_units(far_down[1:])
    grad_second.append(spread_second(grad_first[rows:]))
    gates[1], ups[1], acts[1] = gated(normed_pieces[1], gate_weights, up_weights)
    acts, piece_down, all_down, grad_second = tie(acts, piece_down, all_down, grad_second)
    far_down += piece_down
    grad_second = jnp.concatenate(grad_second)
    grad_core.append(swap(grad_second, "fsdp", CORE))
    grad_pieces = [[grad_first, grad_core[0]], [grad_second, grad_core[1]]]
    grad_pieces, far_down = tie(grad_pieces, far_down)

    all_down += side_units(far_down[2:])
    grad_down = weight_grad(grad_pieces[0] + grad_pieces[1], acts)
    grad_down, grad_pieces, all_down, far_down = tie(grad_down, grad_pieces, all_down, far_down)
    down_weights = unit_bundle(own_down + far_down + all_down + down_pieces)

    codes = [rel for rel in grad_down if rel & SIDE == 0]
    far_codes = [rel for rel in codes if rel]
    down_got = {rel: swap(grad_down[rel | SIDE], "fsdp", SIDE) for rel in far_codes}
    grad_gate_1, grad_up_1, part_1, core_1 = gated_back(
        grad_pieces[1], gates[1], ups[1], gate_weights, up_weights, down_weights
    )
    down_got, part_1, core_1, acts, grad_down = tie(down_got, part_1, core_1, acts, grad_down)

    core_1 = swap(core_1, "fsdp", CORE)
    down_sum = far_sums({rel: add_pair(grad_down[rel], got) for rel, got in down_got.items()})
    down_got = swap(grad_down[SIDE], "fsdp", SIDE)
    out_own, out_other = down_rows(acts, down_weights, normed_pieces[0] + normed_pieces[1])
    core_1, down_got, out_own, out_other, part_1, grad_pieces = tie(
        core_1, down_got, out_own, out_other, part_1, grad_pieces
    )

    got_1 = swap_both(add_pair(part_1, core_1), Z, X)
    out_core = swap(out_other, "fsdp", CORE)
    grad_gate_0, grad_up_0, part_0, core_0 = gated_back(
        grad_pieces[0], gates[0], ups[0], gate_weights, up_weights, down_weights
    )
    part_0, core_0, got_1, down_sum, out_core, out_own, normed_sent = tie(
        part_0, core_0, got_1, down_sum, out_core, out_own, normed_pieces
    )

    core_0 = swap(core_0, "fsdp", CORE)
    out_got = swap_both(add_pair(out_own[2 * rows :], out_core[2 * rows :]), Z, X)
    grad_gate = weight_grad(normed_sent[0] + normed_sent[1], [grad_gate_0, grad_gate_1])
    core_0, out_got, grad_gate, part_0, got_1, normed_sent = tie(
        core_0, out_got, grad_gate, part_0, got_1, normed_sent
    )

    got_0 = swap_both(slim(wide(part_0[rows:]) + wide(core_0[rows:]) + wide(got_1[rows:])), X, Z)
    gate_got = {rel: swap(grad_gate[rel | SIDE], "fsdp", SIDE) for rel in far_codes}
    grad_up = weight_grad(normed_sent[0] + normed_sent[1], [grad_up_0, grad_up_1])
    got_0, gate_got, grad_up, part_0, core_0, got_1, out_got, grad_gate = tie(
        got_0, gate_got, grad_up, part_0, core_0, got_1, out_got, grad_gate
    )

    gate_sum = far_sums({rel: add_pair(grad_gate[rel], got) for rel, got in gate_got.items()})
    out_sums = [
        wide(out_own[at : at + rows]) + wide(out_core[at : at + rows]) + wide(out_got[at : at + rows])
        for at in (0, rows)
    ]
    out_got = swap_both(slim(out_sums[1]), X, Z)
    grads = [part_0, core_0, got_1, got_0]
    grad_hidden, grad_gain_two, branch, grad_mixed = norm_back_out(
        grads, hidden, out_grad, gain_two, out_weights
    )
    down_sum = add_pair(wide(grad_down[0]) + wide(down_got), down_sum)
    grad_mixed, branch, out_got, grad_up, down_sum = tie(grad_mixed, branch, out_got, grad_up, down_sum)

    branch_got = swap(branch, "fsdp", CORE)
    up_got = {rel: swap(grad_up[rel | SIDE], "fsdp", SIDE) for rel in far_codes}
    down_share = share_near(down_sum)
    grad_query, grad_keys, grad_values = attend_back(
        queries, keys_values, mask, grad_mixed, cosine, sine
    )
    grad_query, grad_keys, grad_values, branch_got, gate_sum, up_got, down_share, grad_gate, grad_up = tie(
        grad_query, grad_keys, grad_values, branch_got, gate_sum, up_got, down_share, grad_gate, grad_up
    )

    other = swap(slim(jnp.concatenate([grad_keys[rows:], grad_values[rows:]], 1)), "tp", 1)
    gate_got = swap(grad_gate[SIDE], "fsdp", SIDE)
    up_sum = far_sums({rel: add_pair(grad_up[rel], got) for rel, got in up_got.items()})
    normed_got, mixed_got = core_got[:, :width], core_got[:, width:]
    out_piece = joint_grad(
        [branch, branch_got], [(mixed, mixed_got)], [(0, [0, query_end], query_end)]
    )[0]
    other, out_piece = tie(other, out_piece)

    far_names = [("fsdp", bit) for bit in far_bits()]
    names = [("tp", 1)] + far_names + [("fsdp", NEAR), ("fsdp", SIDE)]
    lead = [2] * (3 + len(far_names))
    grad_kv, query_sums, kv_sums = finish_keys(
        grad_keys, grad_values, other, grad_query, cosine, sine
    )
    query_got, kv_got = swap(grad_query, "fsdp", CORE), swap(grad_kv, "fsdp", CORE)
    out_pair, out_names = scatter_step(out_piece.reshape(lead + [block, -1]), names, X)
    grad_inputs, grad_gain_one = project_back(
        grad_query, grad_kv, tokens, grad_hidden, gain_one, qkv_weights
    )
    grad_inputs, query_got, kv_got, out_pair, gate_got, grad_up = tie(
        grad_inputs, query_got, kv_got, out_pair, gate_got, grad_up
    )

    gate_sum = add_pair(wide(grad_gate[0]) + wide(gate_got), gate_sum)
    out_pair, out_names = scatter_step(add_pair(*out_pair), out_names, ("fsdp", SIDE))
    up_got = swap(grad_up[SIDE], "fsdp", SIDE)
    gate_share = share_near(gate_sum)
    half = query_end // 2
    parts = joint_grad(
        [normed_one, normed_got],
        [(grad_query, query_got), (grad_kv, kv_got)],
        [(0, [0, query_end], half), (0, [half, query_end + half], half), (1, [0, 2 * HD], 2 * HD)],
    )
    parts = [part.reshape(lead + [block, -1]) for part in parts]
    parts, out_pair, gate_share = tie(parts, out_pair, gate_share)

    share = block // 2
    query_sums = query_sums.reshape(KV, query_end)
    grad_bias = jnp.concatenate([query_sums, kv_sums.reshape(KV, 2 * HD)], axis=1)
    small = jnp.concatenate(
        [
            grad_gain_one.reshape(count, 2, share).swapaxes(0, 1),
            grad_gain_two.reshape(count, 2, share).swapaxes(0, 1),
            grad_bias.reshape(2, count, -1),
        ],
        axis=2,
    )
    all_names = [names] * 3
    for step in range(3):
        pairs = [scatter_step(parts[i], all_names[i], links()[(i + step) % 3]) for i in range(3)]
        all_names = [left for _, left in pairs]
        pairs = [pair for pair, _ in pairs]
        if step == 0:
            pairs, up_sum, up_got, small, out_pair = tie(pairs, up_sum, up_got, small, out_pair)
            up_sum = add_pair(wide(grad_up[0]) + wide(up_got), up_sum)
            out_part = add_pair(*out_pair)
        elif step == 1:
            out_pair, _ = scatter_step(out_part, out_names, Z)
            up_share = share_near(up_sum)
            pairs, out_pair = tie(pairs, out_pair)
        else:
            out_total = far_totals(add_pair(*out_pair))
            pairs, up_share, out_total = tie(pairs, up_share, out_total)
        parts = [add_pair(*pair) for pair in pairs]
    small_sum = scatter_small(small)

    gate_sum, up_sum, down_sum = share_cores([gate_share, up_share, down_share], units)
    qkv_total = far_totals(jnp.concatenate(parts, axis=-1))
    out_rows = slim(hidden + out_sums[0] + wide(out_got))
    return (
        out_rows,
        grad_inputs,
        small_sum[:share],
        small_sum[share : 2 * share],
        qkv_total,
        small_sum[None, 2 * share :],
        out_total.T,
        gate_sum,
        up_sum,
        down_sum.T,
    )


def solution(mesh):
    placed = (
        P(("fsdp", "tp"), None),
        P("fsdp", None),
        P("fsdp"),
        P("fsdp"),
        P("fsdp", "tp"),
        P("tp", "fsdp"),
        P("tp", "fsdp"),
        P("fsdp", "tp"),
        P("fsdp", "tp"),
        P("tp", "fsdp"),
        P(("fsdp", "tp"), None),
    )
    return jax.shard_map(
        body,
        mesh=mesh,
        in_specs=placed,
        out_specs=(
            P(("fsdp", "tp"), None),
            P(("fsdp", "tp"), None),
            P(("fsdp", "tp")),
            P(("fsdp", "tp")),
            P("fsdp", "tp"),
            P("tp", "fsdp"),
            P("tp", "fsdp"),
            P("fsdp", "tp"),
            P("fsdp", "tp"),
            P("tp", "fsdp"),
        ),
        check_vma=False,
    )
```

time: 1970 us -> 675 us (0.34)
  waiting for transfers between devices: 1550 us -> 215 us
  Pallas kernels: 0 us -> 257 us
  matrix products: 230 us -> 0 us
  blocking collectives: 103 us -> 0 us
  starting transfers between devices: 0.77 us -> 94 us
    reduce_scatter x9 -> x0, waiting for transfers between devices: 1070 us -> none  [the longest x1 267 us: body(): lax.psum_scatter(grad_down, 'fsdp', scatter_dimension=1, tiled=True)]
    all_gather x9 -> x0, waiting for transfers between devices: 479 us -> none  [the longest x1 111 us: body(): lax.all_gather(w_down, 'fsdp', axis=1, tiled=True)]
    pallas_call x0 -> x18, Pallas kernels: none -> 257 us  [the longest x12 179 us: run_kernel(): pl.pallas_call(wrapped, out_shape=outs, grid=(steps,), in_specs=[pl.Block...]
    dot_general x21 -> x0, matrix products: 230 us -> none  [the longest x1 26.6 us: body(): jnp.dot(grad_up_rows, back_up.T, preferred_element_type=jnp.float32)]
    ppermute x0 -> x93, waiting for transfers between devices: none -> 215 us  [the longest x84 192 us: swap(): return lax.ppermute(values, axis, [(i, i ^ bit) for i in range(count)])]
    unnamed x2 -> x0, blocking collectives: 103 us -> none
    ppermute x0 -> x93, starting transfers between devices: none -> 94 us  [the longest x84 83.5 us: swap(): return lax.ppermute(values, axis, [(i, i ^ bit) for i in range(count)])]
    convert_element_type x7 -> x25, other arithmetic: 7.68 us -> 34.4 us  [the longest x23 33.5 us: slim(): return values.astype(jnp.bfloat16)]
  transfers between devices with their start and end apart: 19 -> 93, of which waited for: 17 -> 38; matrix products, arithmetic and copies ran while one was open for 8% -> 9% of each run, Pallas kernels for 0% -> 39%
where the time goes in v2:
time: 675 us; the launch traced here: 665 us
  Pallas kernels  257 us (38%)
  waiting for transfers between devices  215 us (32%)
  starting transfers between devices  94 us (14%)
  other arithmetic  62.1 us (9%)
  local copies, waits for them, and re-layouts  34.9 us (5%)
    ppermute x84, waiting for transfers between devices, swap(): return lax.ppermute(values, axis, [(i, i ^ bit) for i in range(count)])  192 us
    pallas_call x12, Pallas kernels, run_kernel(): pl.pallas_call(wrapped, out_shape=outs, grid=(steps,), in_specs=[pl.Block...  179 us
    ppermute x84, starting transfers between devices, swap(): return lax.ppermute(values, axis, [(i, i ^ bit) for i in range(count)])  83.5 us
    pallas_call x3, Pallas kernels, weight_grad(): pl.pallas_call(wrapped, out_shape=outs, grid=(steps,), in_specs=[pl.Block...  55 us
    convert_element_type x23, other arithmetic, slim(): return values.astype(jnp.bfloat16)  33.5 us
    ppermute x9, waiting for transfers between devices, swap_both(): return lax.ppermute(values, ('fsdp', 'tp'), pairs)  22.3 us
    pallas_call x2, Pallas kernels, joint_grad(): pl.pallas_call(wrapped, out_shape=outs, grid=(depth // tile,), in_specs=[...  19.7 us
  transfers between devices with their start and end apart: 93, of which 38 were waited for; matrix products, arithmetic and copies ran while one was open for 9% of the time, Pallas kernels for 39%

profile of v2, /device:TPU:0, one launch (start us, length us, event | category | flops | bytes accessed | tf_op | source)
XLA Modules:
  0.0 665.0 jit_solution(14261125738433079849)
XLA Ops:
  24.3 5.1 collective-permute-done.2
  38.9 7.0 %collective-permute-done.6 = bf16[2,96,640]{2,1,0:T(8,128)(2,1)S(1)} collective-permute-done((bf16[2,96,640]{2,1,0:T(8,128)(2,1)S(1)}, bf16[2,96,640]{2,1,0:T(8,128)(2,1)S(1)}, u32[]{:S(2)}, u32[]{:S(2)}) %collective-permute-start.6) | collective-permute-done | bytes 245792 | tf_op jit(solution)/shard_map/ppermute | solution.py:28
  52.2 6.2 collective-permute-done.10
  58.5 5.8 collective-permute-done.9
  69.6 17.2 %collective-permute-done.14 = bf16[8,96,640]{2,1,0:T(8,128)(2,1)S(1)} collective-permute-done((bf16[8,96,640]{2,1,0:T(8,128)(2,1)S(1)}, bf16[8,96,640]{2,1,0:T(8,128)(2,1)S(1)}, u32[]{:S(2)}, u32[]{:S(2)}) %collective-permute-start.14) | collective-permute-done | bytes 983072 | tf_op jit(solution)/shard_map/ppermute | solution.py:28
  95.6 11.3 %collective-permute-done.20.refs_7_.refs_9_ = bf16[2,96,1152]{2,1,0:T(8,128)(2,1)S(1)} collective-permute-done((bf16[2,96,1152]{2,1,0:T(8,128)(2,1)S(1)}, bf16[2,96,1152]{2,1,0:T(8,128)(2,1)S(1)}, u32[]{:S(2)}, u32[]{:S(2)}) %collective-permute-start.20) | collective-permute-done | bytes 442400 | tf_op jit(solution)/shard_map/ppermute | solution.py:28
  119.0 8.4 %shard_map.187 = (bf16[320,1536]{1,0:T(8,128)(2,1)}, bf16[320,1536]{1,0:T(8,128)(2,1)}, bf16[320,512]{1,0:T(8,128)(2,1)}) custom-call(s32[2]{0:T(128)} %pad_add_fusion.2.place_ref, bf16[320,1536]{1,0:T(8,128)(2,1)} %refs_2_.1, f32[1,1536]{1,0:T(1,128)} %reshape_squeeze.6.refs_1_.refs_4_, f32[2,1024]{1,0:T(2,128)} %reshape.115.refs_2_, ...), custom_call_target="tpu_custom_call" | custom-call | flops 31457280 | bytes 240864 | tf_op jit(solution)/shard_map/pallas_call | solution.py:188
  138.4 8.1 %collective-permute-done.26.refs_12_.refs_14_ = bf16[1,96,1152]{2,1,0:T(8,128)(2,1)S(1)} collective-permute-done((bf16[1,96,1152]{2,1,0:T(8,128)(2,1)S(1)}, bf16[1,96,1152]{2,1,0:T(8,128)(2,1)S(1)}, u32[]{:S(2)}, u32[]{:S(2)}) %collective-permute-start.26) | collective-permute-done | bytes 221216 | tf_op jit(solution)/shard_map/ppermute | solution.py:28
  151.5 13.0 %shard_map.188.refs_0_.refs_2_ = bf16[320,1536]{1,0:T(8,128)(2,1)} custom-call(s32[2]{0:T(128)} %pad_add_fusion.2.place_ref, bf16[320,1536]{1,0:T(8,128)(2,1)} %get-tuple-element.344.refs_0_, bf16[640,512]{1,0:T(8,128)(2,1)} %copy-done.14, bf16[640,512]{1,0:T(8,128)(2,1)} %copy-done.14, f32[320,640]{1,0:T(8,128)} %and_select_fusion.refs_3_), custom_call_target="tpu_custom_call" | custom-call | flops 19660800 | bytes 64000 | tf_op jit(solution)/shard_map/pallas_call | solution.py:188
  171.6 7.9 %shard_map.189 = (f32[320,1536]{1,0:T(8,128)}, bf16[320,1536]{1,0:T(8,128)(2,1)}) custom-call(s32[2]{0:T(128)} %pad_add_fusion.2.place_ref, bf16[320,1536]{1,0:T(8,128)(2,1)} %shard_map.188.refs_0_.refs_2_, bf16[320,1536]{1,0:T(8,128)(2,1)} %refs_2_.1, f32[1,1536]{1,0:T(1,128)} %reshape_squeeze.7.refs_2_.refs_6_, bf16[16,96,640]{2,1,0:T(8,128)(2,1)} %copy-done.2, ...), custom_call_target="tpu_custom_call" | custom-call | flops 23592960 | bytes 261216 | tf_op jit(solution)/shard_map/pallas_call | solution.py:188
  184.0 10.0 %collective-permute-done.32 = bf16[320,1536]{1,0:T(8,128)(2,1)S(1)} collective-permute-done((bf16[320,1536]{1,0:T(8,128)(2,1)}, bf16[320,1536]{1,0:T(8,128)(2,1)S(1)}, u32[]{:S(2)}, u32[]{:S(2)}) %collective-permute-start.32) | collective-permute-done | bytes 983072 | tf_op jit(solution)/shard_map/ppermute | solution.py:39
  199.9 22.4 %collective-permute-done.36.refs_23_.refs_3_ = bf16[1,96,1152]{2,1,0:T(8,128)(2,1)S(1)} collective-permute-done((bf16[1,96,1152]{2,1,0:T(8,128)(2,1)S(1)}, bf16[1,96,1152]{2,1,0:T(8,128)(2,1)S(1)}, u32[]{:S(2)}, u32[]{:S(2)}) %collective-permute-start.36) | collective-permute-done | bytes 221216 | tf_op jit(solution)/shard_map/ppermute | solution.py:28
  231.0 17.0 %shard_map.190 = (bf16[1280,1152]{1,0:T(8,128)(2,1)}, bf16[1280,1152]{1,0:T(8,128)(2,1)}, bf16[1280,1152]{1,0:T(8,128)(2,1)}) custom-call(s32[2]{0:T(128)} %pad_add_fusion.2.place_ref, bf16[640,1536]{1,0:T(8,128)(2,1)} %copy-done.7, bf16[640,1536]{1,0:T(8,128)(2,1)} %copy-done.12, bf16[4,96,1152]{2,1,0:T(8,128)(2,1)} %copy-done.4, ...), custom_call_target="tpu_custom_call" | custom-call | flops 141557760 | bytes 327552 | tf_op jit(solution)/shard_map/pallas_call | solution.py:188
  254.1 17.0 %shard_map.191 = (bf16[1280,1152]{1,0:T(8,128)(2,1)}, bf16[1280,1152]{1,0:T(8,128)(2,1)}, bf16[1280,1152]{1,0:T(8,128)(2,1)}) custom-call(s32[2]{0:T(128)} %pad_add_fusion.2.place_ref, bf16[640,1536]{1,0:T(8,128)(2,1)} %collective-permute-done.35.refs_0_.refs_2_, bf16[640,1536]{1,0:T(8,128)(2,1)} %collective-permute-done.40.refs_1_.refs_3_, ...), custom_call_target="tpu_custom_call" | custom-call | flops 141557760 | bytes 327552 | tf_op jit(solution)/shard_map/pallas_call | solution.py:188
  281.0 18.1 %shard_map.192 = (bf16[4,96,1152]{2,1,0:T(8,128)(2,1)}, bf16[4,96,1152]{2,1,0:T(8,128)(2,1)}, bf16[4,96,1152]{2,1,0:T(8,128)(2,1)}, bf16[4,96,1152]{2,1,0:T(8,128)(2,1)}) custom-call(s32[2]{0:T(128)} %pad_add_fusion.2.place_ref, bf16[640,1536]{1,0:T(8,128)(2,1)} %pad_maximum_fusion.4.refs_0_, bf16[640,1536]{1,0:T(8,128)(2,1)} %collective-permute-done.44.refs_1_, ...), custom_call_target="tpu_custom_call" | custom-call | flops 141557760 | bytes 27648 | tf_op jit(solution)/shard_map/pallas_call | solution.py:797
  300.0 27.0 %shard_map.193 = (bf16[1280,1152]{1,0:T(8,128)(2,1)}, bf16[1280,1152]{1,0:T(8,128)(2,1)}, bf16[640,1536]{1,0:T(8,128)(2,1)}, bf16[640,1536]{1,0:T(8,128)(2,1)}) custom-call(s32[2]{0:T(128)} %pad_add_fusion.2.place_ref, bf16[640,1536]{1,0:T(8,128)(2,1)} %copy-done.15, bf16[640,1536]{1,0:T(8,128)(2,1)} %copy-done.20, ...), custom_call_target="tpu_custom_call" | custom-call | flops 212336640 | bytes 493824 | tf_op jit(solution)/shard_map/pallas_call | solution.py:188
  329.2 17.9 %shard_map.194 = (bf16[1280,1536]{1,0:T(8,128)(2,1)}, bf16[1280,1536]{1,0:T(8,128)(2,1)}) custom-call(s32[2]{0:T(128)} %pad_add_fusion.2.place_ref, bf16[1280,1152]{1,0:T(8,128)(2,1)} %get-tuple-element.454.refs_4_.refs_0_, bf16[1280,1152]{1,0:T(8,128)(2,1)} %get-tuple-element.455.refs_5_.refs_1_, bf16[4,96,1152]{2,1,0:T(8,128)(2,1)} %pad_maximum_fusion.12.refs_22_.refs_2_, ...), custom_call_target="tpu_custom_call" | custom-call | flops 141557760 | bytes 273792 | tf_op jit(solution)/shard_map/pallas_call | solution.py:188
  357.8 26.7 %shard_map.195 = (bf16[1280,1152]{1,0:T(8,128)(2,1)}, bf16[1280,1152]{1,0:T(8,128)(2,1)}, bf16[640,1536]{1,0:T(8,128)(2,1)}, bf16[640,1536]{1,0:T(8,128)(2,1)}) custom-call(s32[2]{0:T(128)} %pad_add_fusion.2.place_ref, bf16[640,1536]{1,0:T(8,128)(2,1)} %pad_maximum_fusion.4.refs_0_, bf16[640,1536]{1,0:T(8,128)(2,1)} %collective-permute-done.44.refs_1_, ...), custom_call_target="tpu_custom_call" | custom-call | flops 212336640 | bytes 493824 | tf_op jit(solution)/shard_map/pallas_call | solution.py:188
  384.5 15.2 %collective-permute-done.54 = bf16[4,96,1152]{2,1,0:T(8,128)(2,1)} collective-permute-done((bf16[4,96,1152]{2,1,0:T(8,128)(2,1)}, bf16[4,96,1152]{2,1,0:T(8,128)(2,1)}, u32[]{:S(2)}, u32[]{:S(2)}) %collective-permute-start.54) | collective-permute-done | bytes 884768 | tf_op jit(solution)/shard_map/ppermute | solution.py:28
  404.6 18.7 %shard_map.196 = (bf16[4,96,1152]{2,1,0:T(8,128)(2,1)}, bf16[4,96,1152]{2,1,0:T(8,128)(2,1)}, bf16[4,96,1152]{2,1,0:T(8,128)(2,1)}, bf16[4,96,1152]{2,1,0:T(8,128)(2,1)}) custom-call(s32[2]{0:T(128)} %pad_add_fusion.2.place_ref, bf16[640,1536]{1,0:T(8,128)(2,1)} %copy-done.7, bf16[640,1536]{1,0:T(8,128)(2,1)} %copy-done.12, ...), custom_call_target="tpu_custom_call" | custom-call | flops 141557760 | bytes 27648 | tf_op jit(solution)/shard_map/pallas_call | solution.py:797
  423.3 6.0 collective-permute-done.57
  433.2 18.1 %shard_map.197 = (bf16[4,96,1152]{2,1,0:T(8,128)(2,1)}, bf16[4,96,1152]{2,1,0:T(8,128)(2,1)}, bf16[4,96,1152]{2,1,0:T(8,128)(2,1)}, bf16[4,96,1152]{2,1,0:T(8,128)(2,1)}) custom-call(s32[2]{0:T(128)} %pad_add_fusion.2.place_ref, bf16[640,1536]{1,0:T(8,128)(2,1)} %copy-done.7, bf16[640,1536]{1,0:T(8,128)(2,1)} %copy-done.12, ...), custom_call_target="tpu_custom_call" | custom-call | flops 141557760 | bytes 27648 | tf_op jit(solution)/shard_map/pallas_call | solution.py:797
  457.6 10.0 %shard_map.198 = (f32[320,1536]{1,0:T(8,128)}, f32[1,1536]{1,0:T(1,128)}, bf16[320,1536]{1,0:T(8,128)(2,1)}, bf16[320,1536]{1,0:T(8,128)(2,1)}) custom-call(s32[2]{0:T(128)} %pad_add_fusion.2.place_ref, bf16[640,1536]{1,0:T(8,128)(2,1)} %get-tuple-element.507.refs_0_, bf16[640,1536]{1,0:T(8,128)(2,1)} %collective-permute-done.56.refs_1_, ...), custom_call_target="tpu_custom_call" | custom-call | flops 23592960 | bytes 399552 | tf_op jit(solution)/shard_map/pallas_call | solution.py:188
  475.3 22.2 %shard_map.199 = (bf16[320,1536]{1,0:T(8,128)(2,1)}, f32[640,256]{1,0:T(8,128)}, f32[640,256]{1,0:T(8,128)}) custom-call(s32[2]{0:T(128)} %pad_add_fusion.2.place_ref, bf16[320,1536]{1,0:T(8,128)(2,1)} %get-tuple-element.344.refs_0_, bf16[640,512]{1,0:T(8,128)(2,1)} %copy-done.14, bf16[640,512]{1,0:T(8,128)(2,1)} %copy-done.14, ...), custom_call_target="tpu_custom_call" | custom-call | flops 49152000 | bytes 104960 | tf_op jit(solution)/shard_map/pallas_call | solution.py:188
  497.5 16.6 %collective-permute-done.62 = bf16[4,96,1152]{2,1,0:T(8,128)(2,1)S(1)} collective-permute-done((bf16[4,96,1152]{2,1,0:T(8,128)(2,1)}, bf16[4,96,1152]{2,1,0:T(8,128)(2,1)S(1)}, u32[]{:S(2)}, u32[]{:S(2)}) %collective-permute-start.62) | collective-permute-done | bytes 884768 | tf_op jit(solution)/shard_map/ppermute | solution.py:28
  517.9 8.8 %shard_map.200 = bf16[2,768,768]{2,1,0:T(8,128)(2,1)} custom-call(s32[2]{0:T(128)} %pad_add_fusion.2.place_ref, bf16[320,1536]{1,0:T(8,128)(2,1)} %get-tuple-element.525.refs_0_, bf16[320,1536]{1,0:T(8,128)(2,1)} %collective-permute-done.61.refs_1_, bf16[320,1536]{1,0:T(8,128)(2,1)} %shard_map.188.refs_0_.refs_2_, bf16[320,1536]{1,0:T(8,128)(2,1)} %get-tuple-element.621.refs_3_), custom_call_target="tpu_custom_call" | custom-call | flops 47185920 | tf_op jit(solution)/shard_map/pallas_call | solution.py:856
  535.4 9.7 %shard_map.202 = (f32[320,1536]{1,0:T(8,128)}, f32[1,1536]{1,0:T(1,128)}) custom-call(s32[2]{0:T(128)} %pad_add_fusion.2.place_ref, bf16[320,1536]{1,0:T(8,128)(2,1)} %get-tuple-element.535.refs_3_.refs_0_.refs_2_, bf16[320,512]{1,0:T(8,128)(2,1)} %get-tuple-element.541.refs_1_.refs_4_, bf16[320,1536]{1,0:T(8,128)(2,1)} %refs_2_.1, ...), custom_call_target="tpu_custom_call" | custom-call | flops 31457280 | bytes 281792 | tf_op jit(solution)/shard_map/pallas_call | solution.py:188
  545.1 9.4 %collective-permute-done.69 = bf16[4,96,1152]{2,1,0:T(8,128)(2,1)} collective-permute-done((bf16[4,96,1152]{2,1,0:T(8,128)(2,1)}, bf16[4,96,1152]{2,1,0:T(8,128)(2,1)}, u32[]{:S(2)}, u32[]{:S(2)}) %collective-permute-start.69) | collective-permute-done | bytes 884768 | tf_op jit(solution)/shard_map/ppermute | solution.py:28
  567.8 10.9 %shard_map.203 = (bf16[2,768,384]{2,1,0:T(8,128)(2,1)}, bf16[2,768,384]{2,1,0:T(8,128)(2,1)}, bf16[2,768,256]{2,1,0:T(8,128)(2,1)}) custom-call(s32[2]{0:T(128)} %pad_add_fusion.2.place_ref, bf16[320,1536]{1,0:T(8,128)(2,1)} %get-tuple-element.383.refs_0_, bf16[320,1536]{1,0:T(8,128)(2,1)} %get-tuple-element.620.refs_1_, ...), custom_call_target="tpu_custom_call" | custom-call | flops 62914560 | tf_op jit(solution)/shard_map/pallas_call | solution.py:856
  590.8 14.1 %collective-permute-done.75 = bf16[4,96,1152]{2,1,0:T(8,128)(2,1)} collective-permute-done((bf16[4,96,1152]{2,1,0:T(8,128)(2,1)}, bf16[4,96,1152]{2,1,0:T(8,128)(2,1)}, u32[]{:S(2)}, u32[]{:S(2)}) %collective-permute-start.75) | collective-permute-done | bytes 884768 | tf_op jit(solution)/shard_map/ppermute | solution.py:28
  634.8 7.6 %collective-permute-done.90 = bf16[96,768]{1,0:T(8,128)(2,1)S(1)} collective-permute-done((bf16[96,768]{1,0:T(8,128)(2,1)S(1)}, bf16[96,768]{1,0:T(8,128)(2,1)S(1)}, u32[]{:S(2)}, u32[]{:S(2)}) %collective-permute-start.90) | collective-permute-done | bytes 147488 | tf_op jit(solution)/shard_map/ppermute | solution.py:28
  650.5 10.6 %collective-permute-done.91 = bf16[96,1024]{1,0:T(8,128)(2,1)S(1)} collective-permute-done((bf16[96,1024]{1,0:T(8,128)(2,1)S(1)}, bf16[96,1024]{1,0:T(8,128)(2,1)S(1)}, u32[]{:S(2)}, u32[]{:S(2)}) %collective-permute-start.91) | collective-permute-done | bytes 196640 | tf_op jit(solution)/shard_map/ppermute | solution.py:28
  (509 shorter events, 238.3 us)
Async XLA Ops:
  23.5 22.4 %collective-permute-start.7 = (bf16[1,96,1152]{2,1,0:T(8,128)(2,1)S(1)}, bf16[1,96,1152]{2,1,0:T(8,128)(2,1)S(1)}, u32[]{:S(2)}, u32[]{:S(2)}) collective-permute-start(bf16[1,96,1152]{2,1,0:T(8,128)(2,1)S(1)} %slice_bitcast_fusion.6), channel_id=1, source_target_pairs={{0,16},{2,18},{4,20},{6,22},{8,24},{10,26},{12,28},{14,30},{16,0},... | collective-permute-start | bytes 663560 | tf_op jit(solution)/shard_map/ppermute | solution.py:28
  64.6 22.2 %collective-permute-start.14 = (bf16[8,96,640]{2,1,0:T(8,128)(2,1)S(1)}, bf16[8,96,640]{2,1,0:T(8,128)(2,1)S(1)}, u32[]{:S(2)}, u32[]{:S(2)}) collective-permute-start(bf16[8,96,640]{2,1,0:T(8,128)(2,1)S(1)} %pad_maximum_fusion.15), channel_id=1, source_target_pairs={{0,4},{2,6},{4,0},{6,2},{8,12},{10,14},{12,8},{14,10},{16,20},{18,... | collective-permute-start | bytes 2949128 | tf_op jit(solution)/shard_map/ppermute | solution.py:28
  66.7 26.6 %collective-permute-start.12 = (bf16[8,96,640]{2,1,0:T(8,128)(2,1)S(1)}, bf16[8,96,640]{2,1,0:T(8,128)(2,1)S(1)}, u32[]{:S(2)}, u32[]{:S(2)}) collective-permute-start(bf16[8,96,640]{2,1,0:T(8,128)(2,1)S(1)} %pad_maximum_fusion.13), channel_id=1, source_target_pairs={{0,8},{2,10},{4,12},{6,14},{8,0},{10,2},{12,4},{14,6},{16,24},{18,... | collective-permute-start | bytes 2949128 | tf_op jit(solution)/shard_map/ppermute | solution.py:28
  67.5 26.0 %collective-permute-start.15 = (bf16[1,96,1152]{2,1,0:T(8,128)(2,1)S(1)}, bf16[1,96,1152]{2,1,0:T(8,128)(2,1)S(1)}, u32[]{:S(2)}, u32[]{:S(2)}) collective-permute-start(bf16[1,96,1152]{2,1,0:T(8,128)(2,1)S(1)} %slice.270), channel_id=1, source_target_pairs={{0,16},{2,18},{4,20},{6,22},{8,24},{10,26},{12,28},{14,30},{16,0},... | collective-permute-start | bytes 663560 | tf_op jit(solution)/shard_map/ppermute | solution.py:28
  136.3 30.4 %collective-permute-start.29 = (bf16[3,96,1152]{2,1,0:T(8,128)(2,1)}, bf16[3,96,1152]{2,1,0:T(8,128)(2,1)S(1)}, u32[]{:S(2)}, u32[]{:S(2)}) collective-permute-start(bf16[3,96,1152]{2,1,0:T(8,128)(2,1)} %fusion.8), channel_id=1, source_target_pairs={{0,4},{2,6},{4,0},{6,2},{8,12},{10,14},{12,8},{14,10},{16,20},{18,... | collective-permute-start | bytes 1990664 | tf_op jit(solution)/shard_map/ppermute | solution.py:28
  194.2 29.5 %collective-permute-start.35 = (bf16[640,1536]{1,0:T(8,128)(2,1)S(1)}, bf16[640,1536]{1,0:T(8,128)(2,1)}, u32[]{:S(2)}, u32[]{:S(2)}) collective-permute-start(bf16[640,1536]{1,0:T(8,128)(2,1)S(1)} %pad_maximum_fusion.5.refs_0_), channel_id=1, source_target_pairs={{0,8},{1,9},{2,3},{3,2},{4,12},{5,13},{6,7},{7,6},{8,0},{9,1},{10,... | collective-permute-start | bytes 5898248 | tf_op jit(solution)/shard_map/ppermute | solution.py:39
  195.4 28.3 %collective-permute-start.38 = (bf16[640,1536]{1,0:T(8,128)(2,1)S(1)}, bf16[640,1536]{1,0:T(8,128)(2,1)S(1)}, u32[]{:S(2)}, u32[]{:S(2)}) collective-permute-start(bf16[640,1536]{1,0:T(8,128)(2,1)S(1)} %pad_maximum_fusion.5.refs_0_), channel_id=1, source_target_pairs={{0,2},{2,0},{4,6},{6,4},{8,10},{10,8},{12,14},{14,12},{16,18},{18,... | collective-permute-start | bytes 5898248 | tf_op jit(solution)/shard_map/ppermute | solution.py:28
  197.6 26.2 %collective-permute-start.39 = (bf16[320,3072]{1,0:T(8,128)(2,1)S(1)}, bf16[320,3072]{1,0:T(8,128)(2,1)S(1)}, u32[]{:S(2)}, u32[]{:S(2)}) collective-permute-start(bf16[320,3072]{1,0:T(8,128)(2,1)S(1)} %pad_maximum_fusion.6), channel_id=1, source_target_pairs={{0,2},{2,0},{4,6},{6,4},{8,10},{10,8},{12,14},{14,12},{16,18},{18,... | collective-permute-start | bytes 5898248 | tf_op jit(solution)/shard_map/ppermute | solution.py:28
  197.8 24.5 %collective-permute-start.37 = (bf16[4,96,1152]{2,1,0:T(8,128)(2,1)S(1)}, bf16[4,96,1152]{2,1,0:T(8,128)(2,1)S(1)}, u32[]{:S(2)}, u32[]{:S(2)}) collective-permute-start(bf16[4,96,1152]{2,1,0:T(8,128)(2,1)S(1)} %pad_maximum_fusion.17), channel_id=1, source_target_pairs={{0,4},{2,6},{4,0},{6,2},{8,12},{10,14},{12,8},{14,10},{16,20},{18,... | collective-permute-start | bytes 2654216 | tf_op jit(solution)/shard_map/ppermute | solution.py:28
  198.0 24.3 %collective-permute-start.36 = (bf16[1,96,1152]{2,1,0:T(8,128)(2,1)S(1)}, bf16[1,96,1152]{2,1,0:T(8,128)(2,1)S(1)}, u32[]{:S(2)}, u32[]{:S(2)}) collective-permute-start(bf16[1,96,1152]{2,1,0:T(8,128)(2,1)S(1)} %slice.290), channel_id=1, source_target_pairs={{0,16},{2,18},{4,20},{6,22},{8,24},{10,26},{12,28},{14,30},{16,0},... | collective-permute-start | bytes 663560 | tf_op jit(solution)/shard_map/ppermute | solution.py:28
  223.7 24.3 %collective-permute-start.40 = (bf16[640,1536]{1,0:T(8,128)(2,1)}, bf16[640,1536]{1,0:T(8,128)(2,1)}, u32[]{:S(2)}, u32[]{:S(2)}) collective-permute-start(bf16[640,1536]{1,0:T(8,128)(2,1)} %collective-permute-done.35.refs_0_.refs_2_), channel_id=1, source_target_pairs={{0,2},{2,0},{4,6},{6,4},{8,10},{10,8},{12,14},{14,12},{16,18},{18,... | collective-permute-start | bytes 5898248 | tf_op jit(solution)/shard_map/ppermute | solution.py:28
  223.8 24.2 %collective-permute-start.44 = (bf16[640,1536]{1,0:T(8,128)(2,1)}, bf16[640,1536]{1,0:T(8,128)(2,1)}, u32[]{:S(2)}, u32[]{:S(2)}) collective-permute-start(bf16[640,1536]{1,0:T(8,128)(2,1)} %pad_maximum_fusion.4.refs_0_), channel_id=1, source_target_pairs={{0,2},{2,0},{4,6},{6,4},{8,10},{10,8},{12,14},{14,12},{16,18},{18,... | collective-permute-start | bytes 5898248 | tf_op jit(solution)/shard_map/ppermute | solution.py:28
  250.5 23.9 %collective-permute-start.47 = (bf16[320,1536]{1,0:T(8,128)(2,1)}, bf16[320,1536]{1,0:T(8,128)(2,1)}, u32[]{:S(2)}, u32[]{:S(2)}) collective-permute-start(bf16[320,1536]{1,0:T(8,128)(2,1)} %slice.296), channel_id=1, source_target_pairs={{0,8},{1,9},{2,3},{3,2},{4,12},{5,13},{6,7},{7,6},{8,0},{9,1},{10,... | collective-permute-start | bytes 2949128 | tf_op jit(solution)/shard_map/ppermute | solution.py:39
  299.1 27.9 %collective-permute-start.50 = (bf16[4,96,1152]{2,1,0:T(8,128)(2,1)}, bf16[4,96,1152]{2,1,0:T(8,128)(2,1)S(1)}, u32[]{:S(2)}, u32[]{:S(2)}) collective-permute-start(bf16[4,96,1152]{2,1,0:T(8,128)(2,1)} %get-tuple-element.436), channel_id=1, source_target_pairs={{0,4},{2,6},{4,0},{6,2},{8,12},{10,14},{12,8},{14,10},{16,20},{18,... | collective-permute-start | bytes 2654216 | tf_op jit(solution)/shard_map/ppermute | solution.py:28
  328.0 22.4 %collective-permute-start.51 = (bf16[640,1536]{1,0:T(8,128)(2,1)}, bf16[640,1536]{1,0:T(8,128)(2,1)S(1)}, u32[]{:S(2)}, u32[]{:S(2)}) collective-permute-start(bf16[640,1536]{1,0:T(8,128)(2,1)} %get-tuple-element.452), channel_id=1, source_target_pairs={{0,2},{2,0},{4,6},{6,4},{8,10},{10,8},{12,14},{14,12},{16,18},{18,... | collective-permute-start | bytes 5898248 | tf_op jit(solution)/shard_map/ppermute | solution.py:28
  328.0 22.4 %collective-permute-start.52 = (bf16[4,96,1152]{2,1,0:T(8,128)(2,1)}, bf16[4,96,1152]{2,1,0:T(8,128)(2,1)}, u32[]{:S(2)}, u32[]{:S(2)}) collective-permute-start(bf16[4,96,1152]{2,1,0:T(8,128)(2,1)} %get-tuple-element.453), channel_id=1, source_target_pairs={{0,4},{2,6},{4,0},{6,2},{8,12},{10,14},{12,8},{14,10},{16,20},{18,... | collective-permute-start | bytes 2654216 | tf_op jit(solution)/shard_map/ppermute | solution.py:28
  351.7 48.0 %collective-permute-start.55 = (bf16[1280,1536]{1,0:T(8,128)(2,1)}, bf16[1280,1536]{1,0:T(8,128)(2,1)}, u32[]{:S(2)}, u32[]{:S(2)}) collective-permute-start(bf16[1280,1536]{1,0:T(8,128)(2,1)} %get-tuple-element.471), channel_id=1, source_target_pairs={{0,2},{2,0},{4,6},{6,4},{8,10},{10,8},{12,14},{14,12},{16,18},{18,... | collective-permute-start | bytes 11796488 | tf_op jit(solution)/shard_map/ppermute | solution.py:28
  353.8 45.8 %collective-permute-start.53 = (bf16[640,1536]{1,0:T(8,128)(2,1)S(1)}, bf16[640,1536]{1,0:T(8,128)(2,1)S(1)}, u32[]{:S(2)}, u32[]{:S(2)}) collective-permute-start(bf16[640,1536]{1,0:T(8,128)(2,1)S(1)} %add_convert_fusion.1), channel_id=1, source_target_pairs={{0,8},{1,9},{2,3},{3,2},{4,12},{5,13},{6,7},{7,6},{8,0},{9,1},{10,... | collective-permute-start | bytes 5898248 | tf_op jit(solution)/shard_map/ppermute | solution.py:39
  357.2 42.5 %collective-permute-start.54 = (bf16[4,96,1152]{2,1,0:T(8,128)(2,1)}, bf16[4,96,1152]{2,1,0:T(8,128)(2,1)}, u32[]{:S(2)}, u32[]{:S(2)}) collective-permute-start(bf16[4,96,1152]{2,1,0:T(8,128)(2,1)} %add_convert_fusion.11), channel_id=1, source_target_pairs={{0,16},{2,18},{4,20},{6,22},{8,24},{10,26},{12,28},{14,30},{16,0},... | collective-permute-start | bytes 2654216 | tf_op jit(solution)/shard_map/ppermute | solution.py:28
  404.3 24.9 %collective-permute-start.57 = (bf16[640,1536]{1,0:T(8,128)(2,1)}, bf16[640,1536]{1,0:T(8,128)(2,1)}, u32[]{:S(2)}, u32[]{:S(2)}) collective-permute-start(bf16[640,1536]{1,0:T(8,128)(2,1)} %add_convert_fusion), channel_id=1, source_target_pairs={{0,8},{1,9},{2,3},{3,2},{4,12},{5,13},{6,7},{7,6},{8,0},{9,1},{10,... | collective-permute-start | bytes 5898248 | tf_op jit(solution)/shard_map/ppermute | solution.py:39
  404.6 24.7 %collective-permute-start.56 = (bf16[640,1536]{1,0:T(8,128)(2,1)}, bf16[640,1536]{1,0:T(8,128)(2,1)}, u32[]{:S(2)}, u32[]{:S(2)}) collective-permute-start(bf16[640,1536]{1,0:T(8,128)(2,1)} %get-tuple-element.475), channel_id=1, source_target_pairs={{0,2},{2,0},{4,6},{6,4},{8,10},{10,8},{12,14},{14,12},{16,18},{18,... | collective-permute-start | bytes 5898248 | tf_op jit(solution)/shard_map/ppermute | solution.py:28
  469.7 44.4 %collective-permute-start.61 = (bf16[320,1536]{1,0:T(8,128)(2,1)}, bf16[320,1536]{1,0:T(8,128)(2,1)}, u32[]{:S(2)}, u32[]{:S(2)}) collective-permute-start(bf16[320,1536]{1,0:T(8,128)(2,1)} %get-tuple-element.525.refs_0_), channel_id=1, source_target_pairs={{0,2},{2,0},{4,6},{6,4},{8,10},{10,8},{12,14},{14,12},{16,18},{18,... | collective-permute-start | bytes 2949128 | tf_op jit(solution)/shard_map/ppermute | solution.py:28
  472.3 41.8 %collective-permute-start.62 = (bf16[4,96,1152]{2,1,0:T(8,128)(2,1)}, bf16[4,96,1152]{2,1,0:T(8,128)(2,1)S(1)}, u32[]{:S(2)}, u32[]{:S(2)}) collective-permute-start(bf16[4,96,1152]{2,1,0:T(8,128)(2,1)} %add_convert_fusion.9), channel_id=1, source_target_pairs={{0,16},{2,18},{4,20},{6,22},{8,24},{10,26},{12,28},{14,30},{16,0},... | collective-permute-start | bytes 2654216 | tf_op jit(solution)/shard_map/ppermute | solution.py:28
  473.5 40.6 %collective-permute-start.63 = (bf16[4,96,1152]{2,1,0:T(8,128)(2,1)}, bf16[4,96,1152]{2,1,0:T(8,128)(2,1)}, u32[]{:S(2)}, u32[]{:S(2)}) collective-permute-start(bf16[4,96,1152]{2,1,0:T(8,128)(2,1)} %get-tuple-element.528), channel_id=1, source_target_pairs={{0,4},{2,6},{4,0},{6,2},{8,12},{10,14},{12,8},{14,10},{16,20},{18,... | collective-permute-start | bytes 2654216 | tf_op jit(solution)/shard_map/ppermute | solution.py:28
  474.4 39.7 %collective-permute-start.64 = (bf16[2,96,1152]{2,1,0:T(8,128)(2,1)S(1)}, bf16[2,96,1152]{2,1,0:T(8,128)(2,1)}, u32[]{:S(2)}, u32[]{:S(2)}) collective-permute-start(bf16[2,96,1152]{2,1,0:T(8,128)(2,1)S(1)} %get-tuple-element.635), channel_id=1, source_target_pairs={{0,8},{2,10},{4,12},{6,14},{8,0},{10,2},{12,4},{14,6},{16,24},{18,... | collective-permute-start | bytes 1327112 | tf_op jit(solution)/shard_map/ppermute | solution.py:28
  530.4 27.3 %collective-permute-start.68 = (bf16[2,2,2,96,768]{4,3,2,1,0:T(8,128)(2,1)}, bf16[2,2,2,96,768]{4,3,2,1,0:T(8,128)(2,1)}, u32[]{:S(2)}, u32[]{:S(2)}) collective-permute-start(bf16[2,2,2,96,768]{4,3,2,1,0:T(8,128)(2,1)} %get-tuple-element.618), channel_id=1, source_target_pairs={{0,1},{1,0},{2,3},{3,2},{4,5},{5,4},{6,7},{7,6},{8,9},{9,8},{10,11... | collective-permute-start | bytes 3538952 | tf_op jit(solution)/shard_map/ppermute | solution.py:28
  532.1 22.4 %collective-permute-start.66 = (bf16[320,1536]{1,0:T(8,128)(2,1)S(1)}, bf16[320,1536]{1,0:T(8,128)(2,1)}, u32[]{:S(2)}, u32[]{:S(2)}) collective-permute-start(bf16[320,1536]{1,0:T(8,128)(2,1)S(1)} %copy-done.19), channel_id=1, source_target_pairs={{0,2},{2,0},{4,6},{6,4},{8,10},{10,8},{12,14},{14,12},{16,18},{18,... | collective-permute-start | bytes 2949128 | tf_op jit(solution)/shard_map/ppermute | solution.py:28
  532.1 22.4 %collective-permute-start.69 = (bf16[4,96,1152]{2,1,0:T(8,128)(2,1)}, bf16[4,96,1152]{2,1,0:T(8,128)(2,1)}, u32[]{:S(2)}, u32[]{:S(2)}) collective-permute-start(bf16[4,96,1152]{2,1,0:T(8,128)(2,1)} %get-tuple-element.545), channel_id=1, source_target_pairs={{0,4},{2,6},{4,0},{6,2},{8,12},{10,14},{12,8},{14,10},{16,20},{18,... | collective-permute-start | bytes 2654216 | tf_op jit(solution)/shard_map/ppermute | solution.py:28
  564.8 40.1 %collective-permute-start.75 = (bf16[4,96,1152]{2,1,0:T(8,128)(2,1)}, bf16[4,96,1152]{2,1,0:T(8,128)(2,1)}, u32[]{:S(2)}, u32[]{:S(2)}) collective-permute-start(bf16[4,96,1152]{2,1,0:T(8,128)(2,1)} %add_convert_fusion.7), channel_id=1, source_target_pairs={{0,16},{2,18},{4,20},{6,22},{8,24},{10,26},{12,28},{14,30},{16,0},... | collective-permute-start | bytes 2654216 | tf_op jit(solution)/shard_map/ppermute | solution.py:28
  566.7 38.2 %collective-permute-start.76 = (bf16[4,96,1152]{2,1,0:T(8,128)(2,1)}, bf16[4,96,1152]{2,1,0:T(8,128)(2,1)}, u32[]{:S(2)}, u32[]{:S(2)}) collective-permute-start(bf16[4,96,1152]{2,1,0:T(8,128)(2,1)} %get-tuple-element.564), channel_id=1, source_target_pairs={{0,4},{2,6},{4,0},{6,2},{8,12},{10,14},{12,8},{14,10},{16,20},{18,... | collective-permute-start | bytes 2654216 | tf_op jit(solution)/shard_map/ppermute | solution.py:28
  581.5 23.5 %collective-permute-start.73 = (bf16[2,2,2,96,384]{4,3,2,1,0:T(8,128)(2,1)}, bf16[2,2,2,96,384]{4,3,2,1,0:T(8,128)(2,1)}, u32[]{:S(2)}, u32[]{:S(2)}) collective-permute-start(bf16[2,2,2,96,384]{4,3,2,1,0:T(8,128)(2,1)} %get-tuple-element.625), channel_id=1, source_target_pairs={{0,4},{2,6},{4,0},{6,2},{8,12},{10,14},{12,8},{14,10},{16,20},{18,... | collective-permute-start | bytes 1769480 | tf_op jit(solution)/shard_map/ppermute | solution.py:28
  606.4 23.0 %collective-permute-start.85 = (bf16[2,96,768]{2,1,0:T(8,128)(2,1)S(1)}, bf16[2,96,768]{2,1,0:T(8,128)(2,1)S(1)}, u32[]{:S(2)}, u32[]{:S(2)}) collective-permute-start(bf16[2,96,768]{2,1,0:T(8,128)(2,1)S(1)} %get-tuple-element.641), channel_id=1, source_target_pairs={{0,8},{2,10},{4,12},{6,14},{8,0},{10,2},{12,4},{14,6},{16,24},{18,... | collective-permute-start | bytes 884744 | tf_op jit(solution)/shard_map/ppermute | solution.py:28
  (147 other events, 1906.7 us)

commit v3 on v2

v3 whole, which is shorter than its diff:
```python
import math

import jax
import jax.numpy as jnp
from jax import lax
from jax.experimental import pallas as pl
from jax.experimental.pallas import tpu as pltpu
from jax.sharding import PartitionSpec as P

HEADS = 12
KV = 2
HD = 128

CORE = 1
NEAR = 4
SIDE = 2
LANES = 128
STEP = 320
SCALE = 64
HEAD_STEP = 3
VMEM = 60 << 20

norm_eps = 1e-06
rope_base = 1000000.0


def swap(values, axis, bit):
    count = lax.axis_size(axis)
    return lax.ppermute(values, axis, [(i, i ^ bit) for i in range(count)])


def swap_both(values, evens, odds):
    fsdp, tp = lax.axis_size("fsdp"), lax.axis_size("tp")
    pairs = []
    for f in range(fsdp):
        for t in range(tp):
            axis, bit = odds if f % 2 else evens
            to = (f, t ^ bit) if axis == "tp" else (f ^ bit, t)
            pairs.append((f * tp + t, to[0] * tp + to[1]))
    return lax.ppermute(values, ("fsdp", "tp"), pairs)


def own_bit(axis, bit):
    return lax.rem(lax.div(lax.axis_index(axis), bit), 2)


def far_bits():
    count = lax.axis_size("fsdp")
    bits = []
    bit = count // 2
    while bit >= 8:
        bits.append(bit)
        bit //= 2
    return bits


def choose(flag, first, second):
    return jnp.where(flag == 0, first, second)


def rope_tables(position):
    half_width = HD // 2
    freqs = jnp.exp(jnp.arange(half_width, dtype=jnp.float32) * (-2.0 * math.log(rope_base) / HD))
    angles = position.astype(jnp.float32)[:, None] * freqs[None, :]
    cosine = jnp.cos(angles)
    sine = jnp.sin(angles)
    return (jnp.concatenate([cosine, cosine], 1), jnp.concatenate([sine, -sine], 1))


def unrotate(grads, cosine, sine):
    half_width = grads.shape[-1] // 2
    turned = jnp.concatenate([grads[..., half_width:], grads[..., :half_width]], -1)
    return grads * cosine[:, None, :] + turned * sine[:, None, :]


def root_scale(values):
    return lax.rsqrt(jnp.mean(values * values, axis=1, keepdims=True) + norm_eps)


def norm_back(grad_normed, gain, hat_rows, scale_rows):
    scaled = grad_normed * gain[None, :]
    return scale_rows * (scaled - hat_rows * jnp.mean(scaled * hat_rows, axis=1, keepdims=True))


def segment_of(rows, seq_lens):
    seq_ends = jnp.cumsum(seq_lens)
    seq_starts = seq_ends - seq_lens
    slot_ids = jnp.arange(seq_lens.shape[0], dtype=jnp.int32)
    segment = jnp.sum((rows[:, None] >= seq_ends[None, :]).astype(jnp.int32), axis=1)
    member = (segment[:, None] == slot_ids[None, :]).astype(jnp.int32)
    position = rows - jnp.sum(member * seq_starts[None, :], axis=1)
    return segment, position


def here():
    return jnp.stack([lax.axis_index("tp"), lax.axis_index("fsdp")]).astype(jnp.int32)


def place_blocks(arrays, moves, out_shapes):
    def kernel(place_ref, *refs):
        ins, outs, sems = refs[: len(arrays)], refs[len(arrays) : -1], refs[-1]
        copies = []
        for array, index, columns, number, part, block, there in moves:
            source, target = ins[array].at[index], outs[number]
            if isinstance(block, list):
                block = place_ref[1] ^ (block[0] + ((place_ref[1] & (CORE | NEAR)) ^ block[1]))
            if isinstance(block, tuple):
                odd = lax.rem(place_ref[1], 2)
                part = part[0] * (1 - odd) + part[1] * odd
                block = block[0] * (1 - odd) + block[1] * odd
            if part is not None:
                target = target.at[place_ref[0] ^ part]
            target = target.at[place_ref[1] ^ block]
            rows = target.shape[0]
            if columns is not None:
                source = source.at[pl.ds(0, rows), pl.ds(columns[0], columns[1])]
                target = target.at[:, pl.ds(there, columns[1])]
            copies.append(pltpu.make_async_copy(source, target, sems.at[len(copies)]))
        for copy in copies:
            copy.start()
        for copy in copies:
            copy.wait()

    size = sum(math.prod(shape) * 2 for shape in out_shapes)
    return pl.pallas_call(
        kernel,
        out_shape=[jax.ShapeDtypeStruct(shape, jnp.bfloat16) for shape in out_shapes],
        in_specs=[pl.BlockSpec(memory_space=pltpu.SMEM)]
        + [pl.BlockSpec(memory_space=pl.ANY)] * len(arrays),
        out_specs=[pl.BlockSpec(memory_space=pltpu.VMEM)] * len(out_shapes),
        scratch_shapes=[pltpu.SemaphoreType.DMA((len(moves),))],
        compiler_params=pltpu.CompilerParams(vmem_limit_bytes=VMEM),
        cost_estimate=pl.CostEstimate(flops=0, bytes_accessed=2 * size, transcendentals=0),
    )(here(), *arrays)


def bundle(arrays, moves, shape):
    block = shape[-2] // lax.axis_size("fsdp")
    if block % 16 == 0:
        return (arrays, moves, shape, block)
    split = shape[:-2] + (lax.axis_size("fsdp"), block, shape[-1])
    moves = [(move[0], move[1], move[2], 0) + move[3:] for move in moves]
    return ([place_blocks(arrays, moves, [split])[0].reshape(shape)], None, shape, block)


def bundle_copies(item, refs, place_ref, target, sems, first):
    _, moves, _, block = item
    if moves is None:
        return [pltpu.make_async_copy(refs[0], target, sems.at[first])]
    copies = []
    for array, index, columns, part, rel, there in moves:
        source = refs[array].at[index]
        if isinstance(rel, list):
            rel = place_ref[1] ^ (rel[0] + ((place_ref[1] & (CORE | NEAR)) ^ rel[1]))
        if isinstance(rel, tuple):
            odd = lax.rem(place_ref[1], 2)
            part = part[0] * (1 - odd) + part[1] * odd
            rel = rel[0] * (1 - odd) + rel[1] * odd
        row = pl.ds(pl.multiple_of((place_ref[1] ^ rel) * block, 16), block)
        there_part = target if part is None else target.at[place_ref[0] ^ part]
        if columns is None:
            there_part = there_part.at[row]
        else:
            source = source.at[:, pl.ds(columns[0], columns[1])]
            there_part = there_part.at[row, pl.ds(there, columns[1])]
        copies.append(pltpu.make_async_copy(source, there_part, sems.at[first + len(copies)]))
    return copies


def run_kernel(kernel, steps, operands, specs, bundles, outs, out_specs, flops, lazy=False):
    arrays = [array for item in bundles for array in item[0]]
    counts = [1 if item[1] is None else len(item[1]) for item in bundles]

    def wrapped(place_ref, *refs):
        ins, refs = refs[: len(operands)], refs[len(operands) :]
        parts, refs = refs[: len(arrays)], refs[len(arrays) :]
        results, refs = refs[: len(outs)], refs[len(outs) :]
        targets = refs[: len(bundles)]
        step = pl.program_id(0)
        copies, first, array = [], 0, 0
        for item, target, count in zip(bundles, targets, counts):
            own = parts[array : array + len(item[0])]
            copies.append(bundle_copies(item, own, place_ref, target, refs[-1], first))
            first += count
            array += len(item[0])

        def ready(number):
            @pl.when(step == 0)
            def _():
                for copy in copies[number]:
                    copy.wait()

        if bundles:

            @pl.when(step == 0)
            def _():
                for group in copies:
                    for copy in group:
                        copy.start()

        if lazy:
            kernel(step, ins, targets, results, ready)
        else:
            for number in range(len(bundles)):
                ready(number)
            kernel(step, ins, targets, results)

    scratch = [pltpu.VMEM(item[2], jnp.bfloat16) for item in bundles]
    if bundles:
        scratch.append(pltpu.SemaphoreType.DMA((sum(counts),)))
    size = sum(math.prod(v.shape) * v.dtype.itemsize for v in [*operands, *arrays, *outs])
    return pl.pallas_call(
        wrapped,
        out_shape=outs,
        grid=(steps,),
        in_specs=[pl.BlockSpec(memory_space=pltpu.SMEM)]
        + specs
        + [pl.BlockSpec(memory_space=pl.ANY)] * len(arrays),
        out_specs=out_specs,
        scratch_shapes=scratch,
        compiler_params=pltpu.CompilerParams(vmem_limit_bytes=VMEM),
        cost_estimate=pl.CostEstimate(
            flops=flops // SCALE, bytes_accessed=size // SCALE, transcendentals=0
        ),
    )(here(), *operands, *arrays)


def shaped(shape, dtype=jnp.bfloat16):
    return jax.ShapeDtypeStruct(shape, dtype)


def full_spec(value):
    return pl.BlockSpec(value.shape, lambda i: (0,) * len(value.shape))


def send_units(shards, quarter):
    units = shards[0].shape[1]
    core, near = own_bit("fsdp", CORE), own_bit("fsdp", NEAR)
    padded = jnp.stack([jnp.pad(shard, ((0, 0), (0, 4 * quarter - units))) for shard in shards])
    low, high = padded[..., : 2 * quarter], padded[..., 2 * quarter :]
    kept, got = choose(core, low, high), swap(choose(core, high, low), "fsdp", CORE)

    def halves(kept, got):
        pair = jnp.stack([kept, got], axis=1)
        low, high = pair[..., :quarter], pair[..., quarter:]
        return choose(near, low, high), choose(near, high, low)

    return kept, got, halves


INNER = [0, CORE, NEAR, NEAR | CORE]


def far_units(quad, low, high):
    pieces = far_gather(quad[low:high])
    return [(p, [rel | INNER[i] for i in range(low, high)]) for rel, p in pieces.items() if rel]


def side_units(pieces):
    arrays = jnp.concatenate([array for array, _ in pieces])
    places = [place | SIDE for _, marks in pieces for place in marks]
    return [(swap(arrays, "fsdp", SIDE), places)]


def part_of(pieces, low, high):
    return [(array[low:high], marks[low:high]) for array, marks in pieces]


def pick_units(piece, low, high):
    array, marks = piece
    return (array, marks, low, high)


def quad_groups(count):
    return [[i for i in range(count) if i & (CORE | NEAR) == inner] for inner in INNER]


def group_bundle(gathered):
    size, _, block, quarter = gathered.shape
    moves = [
        (0, 4 * k + i, None, None, [member, inner], None)
        for k, member in enumerate(quad_groups(4 * size)[0])
        for i, inner in enumerate(INNER)
    ]
    return bundle([gathered.reshape(4 * size, block, quarter)], moves, (4 * size * block, quarter))


def side_by_side(first, second):
    if first[1] is None:
        joined = jnp.concatenate([first[0][0], second[0][0]], axis=1)
        return ([joined], None, joined.shape, first[3])
    width = first[2][1]
    moves = [move[:2] + ((0, width),) + move[3:5] + (0,) for move in first[1]]
    moves += [
        (move[0] + len(first[0]), move[1], (0, second[2][1])) + move[3:5] + (width,)
        for move in second[1]
    ]
    return (first[0] + second[0], moves, (first[2][0], width + second[2][1]), first[3])


def unit_bundle(pieces):
    count = lax.axis_size("fsdp")
    _, block, quarter = pieces[0][0].shape
    moves = [
        (number, i, None, None, piece[1][i], None)
        for number, piece in enumerate(pieces)
        for i in range(*(piece[2:] or (0, len(piece[1]))))
    ]
    return bundle([piece[0] for piece in pieces], moves, (count * block, quarter))


def tie(*values):
    leaves, form = jax.tree.flatten(values)
    arrays = [i for i, leaf in enumerate(leaves) if isinstance(leaf, jax.Array)]
    for i, leaf in zip(arrays, lax.optimization_barrier([leaves[i] for i in arrays])):
        leaves[i] = leaf
    return jax.tree.unflatten(form, leaves)


def add_pair(own, got):
    return slim(wide(own) + wide(got))


def far_sums(pieces):
    for bit in far_bits():
        merged = {}
        for rel in [key for key in pieces if key & bit]:
            got = swap(pieces[rel], "fsdp", bit)
            other = rel ^ bit
            merged[other] = add_pair(pieces[other], got) if other in pieces else got
        pieces = merged
    return pieces[0]


def share_near(total):
    return total[:2], swap(total[2:], "fsdp", NEAR)


def share_cores(pairs, units):
    core, near = own_bit("fsdp", CORE), own_bit("fsdp", NEAR)
    keep, got = jnp.stack([keep for keep, _ in pairs]), jnp.stack([got for _, got in pairs])
    both = jnp.concatenate([choose(near, keep, got), choose(near, got, keep)], axis=3)
    keep, got = both[:, 0], swap(both[:, 1], "fsdp", CORE)
    both = jnp.concatenate([choose(core, keep, got), choose(core, got, keep)], axis=2)
    return [wide(both[i, :, :units]) for i in range(len(pairs))]


def links():
    return [("tp", 1), ("fsdp", SIDE), ("fsdp", NEAR)]


def thirds(width):
    tiles = width // LANES
    cuts = [(tiles + 2 - i) // 3 * LANES for i in range(3)]
    starts = [0, cuts[0], cuts[0] + cuts[1]]
    return list(zip(starts, cuts))


def step_all(parts, marks, step):
    for turn in range(3):
        axis, bit = links()[(turn + step) % 3]
        parts[turn] = jnp.concatenate([parts[turn], swap(parts[turn], axis, bit)])
        marks[turn] = marks[turn] + [
            (part | bit, rel) if axis == "tp" else (part, rel | bit) for part, rel in marks[turn]
        ]


def joint_moves(marks, widths):
    spans, start = [], 0
    for item in widths:
        spans.append((start, start + item))
        start += item
    moves = [[] for _ in widths]
    for turn, (first, size) in enumerate(thirds(start)):
        for other in range(2):
            for index, (part, rel) in enumerate(marks[turn]):
                for number, (low, high) in enumerate(spans):
                    begin, end = max(low, first), min(high, first + size)
                    if begin < end:
                        columns = (begin - first, end - begin)
                        rel_there = rel | CORE if other else rel
                        moves[number].append(
                            (turn + 3 * other, index, columns, part, rel_there, begin - low)
                        )
    return moves


def far_gather(values):
    pieces = {0: values}
    for bit in far_bits():
        pieces.update({rel | bit: swap(piece, "fsdp", bit) for rel, piece in list(pieces.items())})
    return pieces


def small_step(values, axis, bits):
    count = 2 ** len(bits)
    view = values.reshape(count, -1, values.shape[-1])
    own = 0
    for bit in bits:
        own = 2 * own + own_bit(axis, bit)
    total = lax.dynamic_index_in_dim(view, own, 0, keepdims=False)
    for rel in range(1, count):
        far = sum(bit for k, bit in enumerate(bits) if (rel >> (len(bits) - 1 - k)) & 1)
        sent = lax.dynamic_index_in_dim(view, own ^ rel, 0, keepdims=False)
        total = total + swap(sent, axis, far)
    return total


X, Z = ("tp", 1), ("fsdp", NEAR)


def spread_first(rows):
    return jnp.concatenate([rows, swap_both(rows, X, Z)])


def spread_second(rows):
    return swap_both(rows, Z, X)


def wide(values):
    return values.astype(jnp.float32)


def slim(values):
    return values.astype(jnp.bfloat16)


def dot(a, b):
    return jnp.dot(a, b, preferred_element_type=jnp.float32)


def dot_last(a, b):
    return lax.dot_general(a, b, (((1,), (1,)), ((), ())), preferred_element_type=jnp.float32)


def dot_first(a, b):
    return lax.dot_general(a, b, (((0,), (0,)), ((), ())), preferred_element_type=jnp.float32)


def project_keys(tokens, gain, bias, cosine, sine, weights):
    rows, depth = tokens.shape

    def kernel(step, ins, targets, outs):
        tokens_ref, gain_ref, bias_ref, cosine_ref, sine_ref = ins
        values = wide(tokens_ref[...])
        scale = lax.rsqrt(jnp.mean(values * values, axis=1, keepdims=True) + norm_eps)
        normed = slim(values * scale * gain_ref[...])
        outs[0][...] = normed
        for t in range(KV):
            total = dot(normed, targets[0][t]) + bias_ref[t : t + 1, :]
            part = total[:, :HD]
            part = part * cosine_ref[...] - pltpu.roll(part, HD // 2, 1) * sine_ref[...]
            outs[1][:, 2 * t * HD : (2 * t + 1) * HD] = slim(part)
            outs[1][:, (2 * t + 1) * HD : (2 * t + 2) * HD] = slim(total[:, HD:])

    operands = [tokens, gain, bias, cosine, sine]
    outs = [shaped((rows, depth)), shaped((rows, 2 * KV * HD))]
    return run_kernel(
        kernel, 1, operands, [full_spec(v) for v in operands], [weights], outs,
        [full_spec(v) for v in outs], 4 * rows * depth * KV * HD,
    )


def project_queries(normed, bias, cosine, sine, weights):
    rows, depth = normed.shape
    columns = weights[2][2]

    def kernel(step, ins, targets, outs):
        normed_ref, bias_ref, cosine_ref, sine_ref = ins
        cos, sin = cosine_ref[...], sine_ref[...]
        for t in range(KV):
            for c in range(0, columns, 2 * HD):
                span = slice(c, c + 2 * HD)
                total = dot(normed_ref[...], targets[0][t, :, span]) + bias_ref[t : t + 1, span]
                for j in range(2):
                    part = total[:, j * HD : (j + 1) * HD]
                    part = part * cos - pltpu.roll(part, HD // 2, 1) * sin
                    at = t * columns + c + j * HD
                    outs[0][:, at : at + HD] = slim(part)

    operands = [normed, bias, cosine, sine]
    outs = [shaped((rows, HEADS * HD))]
    return run_kernel(
        kernel, 1, operands, [full_spec(v) for v in operands], [weights], outs,
        [full_spec(v) for v in outs], 2 * rows * depth * HEADS * HD,
    )[0]


def softmax_rows(query, keys, mask):
    scores = dot_last(query, keys) * HD ** (-0.5) + mask
    expd = jnp.exp(scores - jnp.max(scores, axis=1, keepdims=True))
    return expd * (1.0 / jnp.sum(expd, axis=1, keepdims=True))


def head_specs(count, total):
    steps = HEADS // KV // HEAD_STEP
    return [
        pl.BlockSpec((count, HEAD_STEP * HD), lambda h: (0, h)),
        pl.BlockSpec((total, HD), lambda h: (0, h // steps * 2)),
        pl.BlockSpec((total, HD), lambda h: (0, h // steps * 2 + 1)),
        pl.BlockSpec((count, total), lambda h: (0, 0)),
    ]


def attend(queries, keys_values, mask):
    count, total = mask.shape

    def kernel(step, ins, targets, outs):
        for h in range(HEAD_STEP):
            span = slice(h * HD, (h + 1) * HD)
            probs = softmax_rows(ins[0][:, span], ins[1][...], ins[3][...])
            outs[0][:, span] = slim(dot(slim(probs), ins[2][...]))

    return run_kernel(
        kernel, HEADS // HEAD_STEP, [queries, keys_values, keys_values, mask],
        head_specs(count, total), [], [shaped(queries.shape)],
        [pl.BlockSpec((count, HEAD_STEP * HD), lambda h: (0, h))], 4 * HEADS * count * total * HD,
    )[0]


def attend_back(queries, keys_values, mask, grad_mixed, cosine, sine):
    count, total = mask.shape
    steps = HEADS // KV // HEAD_STEP

    def kernel(step, ins, targets, outs):
        keys, mask_rows = ins[1][...], ins[3][...]
        grad_keys, grad_values = None, None
        for h in range(HEAD_STEP):
            span = slice(h * HD, (h + 1) * HD)
            query, grad = ins[0][:, span], ins[4][:, span]
            probs = softmax_rows(query, keys, mask_rows)
            grad_probs = dot_last(grad, ins[2][...])
            inner = jnp.sum(probs * grad_probs, axis=1, keepdims=True)
            grad_scores = slim(probs * (grad_probs - inner))
            value_part = dot_first(slim(probs), grad)
            key_part = dot_first(grad_scores, query)
            grad_values = value_part if h == 0 else grad_values + value_part
            grad_keys = key_part if h == 0 else grad_keys + key_part
            part = dot(grad_scores, keys) * HD ** (-0.5)
            part = part * ins[5][...] + pltpu.roll(part, HD // 2, 1) * ins[6][...]
            outs[0][:, span] = slim(part)
        grad_keys = grad_keys * HD ** (-0.5)
        first = step % steps == 0

        @pl.when(first)
        def _():
            outs[1][...] = grad_keys
            outs[2][...] = grad_values

        @pl.when(jnp.logical_not(first))
        def _():
            outs[1][...] += grad_keys
            outs[2][...] += grad_values

    specs = head_specs(count, total) + [
        pl.BlockSpec((count, HEAD_STEP * HD), lambda h: (0, h)),
        full_spec(cosine),
        full_spec(sine),
    ]
    sums = shaped((total, KV * HD), jnp.float32)
    return run_kernel(
        kernel, HEADS // HEAD_STEP,
        [queries, keys_values, keys_values, mask, grad_mixed, cosine, sine], specs, [],
        [shaped(queries.shape), sums, sums],
        [
            pl.BlockSpec((count, HEAD_STEP * HD), lambda h: (0, h)),
            pl.BlockSpec((total, HD), lambda h: (0, h // steps)),
            pl.BlockSpec((total, HD), lambda h: (0, h // steps)),
        ],
        10 * HEADS * count * total * HD,
    )


def finish_keys(grad_keys, grad_values, other, grad_query, cosine, sine):
    rows = other.shape[0]

    def kernel(step, ins, targets, outs):
        for t in range(KV):
            span = slice(t * HD, (t + 1) * HD)
            keys = ins[0][:, span] + wide(ins[2][:, span])
            keys = keys * ins[4][...] + pltpu.roll(keys, HD // 2, 1) * ins[5][...]
            there = slice((KV + t) * HD, (KV + t + 1) * HD)
            values = ins[1][:, span] + wide(ins[2][:, there])
            outs[0][:, 2 * t * HD : (2 * t + 1) * HD] = slim(keys)
            outs[0][:, (2 * t + 1) * HD : (2 * t + 2) * HD] = slim(values)
        outs[1][...] = jnp.sum(wide(ins[3][...]), axis=0, keepdims=True)
        outs[2][...] = jnp.sum(wide(outs[0][...]), axis=0, keepdims=True)

    half = pl.BlockSpec((rows, KV * HD), lambda i: (0, 0))
    operands = [grad_keys, grad_values, other, grad_query, cosine, sine]
    outs = [
        shaped((rows, 2 * KV * HD)),
        shaped((1, HEADS * HD), jnp.float32),
        shaped((1, 2 * KV * HD), jnp.float32),
    ]
    return run_kernel(
        kernel, 1, operands, [half, half] + [full_spec(v) for v in operands[2:]], [], outs,
        [full_spec(v) for v in outs], 0,
    )


def project_out(mixed, tokens, gain, weights):
    def kernel(step, ins, targets, outs):
        columns = weights[2][2]
        hidden = wide(ins[1][...])
        for t in range(KV):
            hidden = hidden + dot_last(ins[0][:, t * columns : (t + 1) * columns], targets[0][t])
        outs[0][...] = hidden
        scale = lax.rsqrt(jnp.mean(hidden * hidden, axis=1, keepdims=True) + norm_eps)
        outs[1][...] = slim(hidden * scale * ins[2][...])

    operands = [mixed, tokens, gain]
    outs = [shaped(tokens.shape, jnp.float32), shaped(tokens.shape)]
    return run_kernel(
        kernel, 1, operands, [full_spec(v) for v in operands], [weights], outs,
        [full_spec(v) for v in outs], 2 * tokens.shape[0] * tokens.shape[1] * mixed.shape[1],
    )


def norm_parts(grad_normed, values, gain):
    scale = lax.rsqrt(jnp.mean(values * values, axis=1, keepdims=True) + norm_eps)
    hat = values * scale
    scaled = grad_normed * gain
    back = scale * (scaled - hat * jnp.mean(scaled * hat, axis=1, keepdims=True))
    return back, jnp.sum(grad_normed * hat, axis=0, keepdims=True)


def norm_back_out(grads, hidden, out_grad, gain, weights):
    rows, depth = hidden.shape
    columns = weights[2][2]

    def kernel(step, ins, targets, outs):
        total = wide(ins[0][...])
        for ref in ins[1 : len(grads)]:
            total = total + wide(ref[...])
        hidden_ref, out_grad_ref, gain_ref = ins[len(grads) :]
        back, outs[1][...] = norm_parts(total, hidden_ref[...], gain_ref[...])
        total = wide(out_grad_ref[...]) + back
        outs[0][...] = total
        branch = slim(total)
        outs[2][...] = branch
        for t in range(KV):
            outs[3][:, t * columns : (t + 1) * columns] = slim(dot(branch, targets[0][t]))

    operands = [*grads, hidden, out_grad, gain]
    outs = [
        shaped((rows, depth), jnp.float32),
        shaped((1, depth), jnp.float32),
        shaped((rows, depth)),
        shaped((rows, KV * columns)),
    ]
    specs = [pl.BlockSpec((rows, depth), lambda i: (0, 0))] * (len(grads) + 2) + [full_spec(gain)]
    return run_kernel(
        kernel, 1, operands, specs, [weights], outs, [full_spec(v) for v in outs],
        2 * rows * depth * KV * columns,
    )


def project_back(grad_query, grad_kv, tokens, grad_hidden, gain, query_weights, kv_weights):
    def kernel(step, ins, targets, outs):
        query, kv = HEADS // KV * HD, 2 * HD
        total = None
        for t in range(KV):
            part = dot_last(ins[0][:, t * query : (t + 1) * query], targets[0][t])
            part += dot_last(ins[1][:, t * kv : (t + 1) * kv], targets[1][t])
            total = part if total is None else total + part
        back, outs[1][...] = norm_parts(total, wide(ins[2][...]), ins[4][...])
        outs[0][...] = ins[3][...] + back

    operands = [grad_query, grad_kv, tokens, grad_hidden, gain]
    outs = [shaped(tokens.shape, jnp.float32), shaped((1, tokens.shape[1]), jnp.float32)]
    return run_kernel(
        kernel, 1, operands, [full_spec(v) for v in operands], [query_weights, kv_weights], outs,
        [full_spec(v) for v in outs], 4 * tokens.shape[0] * tokens.shape[1] * query_weights[2][2],
    )


def piece_specs(pieces):
    specs, start = [], 0
    for piece in pieces:
        steps = piece.shape[0] // STEP
        specs.append(
            pl.BlockSpec(
                (STEP, piece.shape[1]),
                lambda i, start=start, steps=steps: (jnp.clip(i - start, 0, steps - 1), 0),
            )
        )
        start += steps
    return specs, start


def pick_piece(step, refs, pieces):
    block, start = refs[0][...], 0
    for ref, piece in list(zip(refs, pieces))[1:]:
        start += piece.shape[0] // STEP
        block = jnp.where(step < start, block, ref[...])
        start = start
    return block


def sigma(values):
    return 0.5 * jnp.tanh(0.5 * values) + 0.5


def gated(pieces, weights, gates=None):
    specs, steps = piece_specs(pieces)
    depth, columns = weights[2]
    given = [] if gates is None else gates
    count = 1 if gates is None else 3

    def kernel(step, ins, targets, outs):
        value = dot(pick_piece(step, ins[: len(pieces)], pieces), targets[0][...])
        if gates is None:
            outs[0][...] = slim(value)
            return
        gate = wide(pick_piece(step, ins[len(pieces) :], gates))
        sig = sigma(gate)
        silu = gate * sig
        outs[0][...] = slim(value * (sig + silu * (1.0 - sig)))
        outs[1][...] = slim(silu)
        outs[2][...] = slim(silu * value)

    return run_kernel(
        kernel, steps, pieces + given, specs + piece_specs(given)[0], [weights],
        [shaped((steps * STEP, columns))] * count,
        [pl.BlockSpec((STEP, columns), lambda i: (i, 0))] * count, 2 * steps * STEP * depth * columns,
    )


def gated_back(pieces, slope, silu, first, w_gate_up, w_down, owned):
    specs, steps = piece_specs(pieces)
    depth, columns = w_down[2]
    part = pl.BlockSpec((STEP, 2 * columns), lambda i: (i, 0))
    later = pl.BlockSpec((STEP, columns), lambda i: (i + first // STEP, 0))
    sides = [shaped((sum(piece.shape[0] for piece in group), depth)) for group in (pieces[:owned], pieces[owned:])]

    def kernel(step, ins, targets, outs, ready):
        ready(0)
        act = dot(pick_piece(step, ins[: len(pieces)], pieces), targets[0][...])
        outs[0][:, :columns] = slim(act * wide(ins[-2][...]))
        outs[0][:, columns:] = slim(act * wide(ins[-1][...]))
        ready(1)
        store_piece(step, outs[1:], sides, slim(dot_last(outs[0][...], targets[1][...])))

    return run_kernel(
        kernel, steps, pieces + [slope, silu], specs + [later, later], [w_down, w_gate_up],
        [shaped((steps * STEP, 2 * columns))] + sides, [part] + piece_specs(sides)[0],
        6 * steps * STEP * depth * columns, True,
    )


def store_piece(step, refs, pieces, value):
    start = 0
    for ref, piece in zip(refs, pieces):
        end = start + piece.shape[0] // STEP

        @pl.when((step >= start) & (step < end))
        def _(ref=ref):
            ref[...] = value

        start = end


def down_rows(acts, w_down, pieces):
    specs, steps = piece_specs(acts)
    depth, columns = w_down[2]
    owner, starts, place = [], [0, 0], 0
    for number, piece in enumerate(pieces):
        owner += [number % 2] * (piece.shape[0] // STEP)
    index = [owner[:i].count(owner[i]) for i in range(steps)]
    outs = [shaped((owner.count(side) * STEP, depth)) for side in range(2)]

    def kernel(step, ins, targets, results):
        block = pick_piece(step, ins, acts)
        value = slim(dot_last(block, targets[0][...]))
        mine = step >= steps
        for i in range(steps):
            if owner[i] == 0:
                mine = mine | (step == i)

        @pl.when(mine)
        def _():
            results[0][...] = value

        @pl.when(jnp.logical_not(mine))
        def _():
            results[1][...] = value

    def spec(side):
        def place_of(i):
            reached = 0
            for k in range(steps):
                if owner[k] == side and index[k] > 0:
                    reached = jnp.where(i >= k, index[k], reached)
            return (reached, 0)

        return pl.BlockSpec((STEP, depth), place_of)

    return run_kernel(
        kernel, steps, acts, specs, [w_down], outs, [spec(0), spec(1)],
        2 * steps * STEP * depth * columns,
    )


def weight_grad(lefts, rights, columns, number_of=0, grouped=False):
    depth = lefts[0].shape[1]
    count = lax.axis_size("fsdp")
    block = depth // count
    rels = [0]
    for bit in far_bits() + [SIDE]:
        rels += [rel | bit for rel in rels]
    members = quad_groups(count)[0]
    direct = block % 16 == 0
    tile = 4 * block if direct else 2 * LANES
    steps = depth // tile
    total_rows = sum(left.shape[0] for left in lefts)

    def wrapped(place_ref, *refs):
        ins, refs = refs[: len(lefts) + len(rights)], refs[len(lefts) + len(rights) :]
        step = pl.program_id(0)
        total, number, row = None, len(lefts), 0
        for ref, left in zip(ins, lefts):
            part = dot_first(ref[...], ins[number][row : row + left.shape[0], :])
            total = part if total is None else total + part
            row += left.shape[0]
            if row == rights[number - len(lefts)].shape[0]:
                number, row = number + 1, 0
        if not direct:
            refs[0][...] = slim(total)
            return
        outs, held, sems = refs[:-2], refs[-2], refs[-1]
        held[step] = slim(total).reshape(4, block, columns)

        @pl.when(step == steps - 1)
        def _():
            copies = []
            for k, rel in enumerate(rels):
                out = outs[0].at[k] if grouped else outs[k]
                for i, inner in enumerate(INNER):
                    number = place_ref[1] ^ (rel | inner)
                    if grouped:
                        number = members[k] + ((place_ref[1] & (CORE | NEAR)) ^ inner)
                    source = held.at[lax.div(number, 4), lax.rem(number, 4)]
                    copies.append(pltpu.make_async_copy(source, out.at[i], sems.at[len(copies)]))
            for copy in copies:
                copy.start()
            for copy in copies:
                copy.wait()

    operands = [*lefts, *rights]
    specs = [pl.BlockSpec((left.shape[0], tile), lambda i: (0, i)) for left in lefts]
    specs += [pl.BlockSpec((right.shape[0], columns), lambda i: (0, number_of)) for right in rights]
    scratch = []
    if direct:
        outs = [shaped((4, block, columns)) for _ in rels]
        if grouped:
            outs = [shaped((len(rels), 4, block, columns))]
        out_specs = [pl.BlockSpec(memory_space=pl.ANY)] * len(outs)
        scratch = [
            pltpu.VMEM((steps, 4, block, columns), jnp.bfloat16),
            pltpu.SemaphoreType.DMA((4 * len(rels),)),
        ]
    else:
        outs = [shaped((depth, columns))]
        out_specs = [pl.BlockSpec((tile, columns), lambda i: (i, 0))]
    results = pl.pallas_call(
        wrapped,
        out_shape=outs,
        grid=(steps,),
        in_specs=[pl.BlockSpec(memory_space=pltpu.SMEM)] + specs,
        out_specs=out_specs,
        scratch_shapes=scratch,
        compiler_params=pltpu.CompilerParams(vmem_limit_bytes=VMEM),
        cost_estimate=pl.CostEstimate(
            flops=2 * total_rows * depth * columns // SCALE,
            bytes_accessed=depth * columns // SCALE,
            transcendentals=0,
        ),
    )(here(), *operands)
    if direct:
        return results[0] if grouped else dict(zip(rels, results))
    blocks = results[0].reshape(count, block, columns)
    if grouped:
        inner = (lax.axis_index("fsdp") & (CORE | NEAR)) ^ jnp.array(INNER)
        return blocks[jnp.array(members)[:, None] + inner[None, :]]
    places = lax.axis_index("fsdp") ^ jnp.array([rel | inner for rel in rels for inner in INNER])
    blocks = blocks[places].reshape(len(rels), 4, block, columns)
    return {rel: blocks[i] for i, rel in enumerate(rels)}


def split_places(late=False):
    fars = [0]
    for bit in far_bits():
        fars += [rel | bit for rel in fars]
    places = {}
    for a in range(2):
        for f, far in enumerate(fars):
            for b in range(2):
                for c in range(2):
                    even = (a, far | b * NEAR | c * SIDE)
                    odd = (b, far | c * NEAR | a * SIDE)
                    if late:
                        even, odd = (b, far | c * NEAR | a * SIDE), (c, far | a * NEAR | b * SIDE)
                    places[a, f, b, c] = (even, odd)
    return len(fars), places


OUT_LINKS = [(Z, Z), (X, ("fsdp", SIDE)), (("fsdp", SIDE), X)]


def split_moves(fars):
    marks = [0]
    for bit in far_bits():
        marks += [rel | bit for rel in marks]
    moves = []
    for other in range(2):
        for a in range(2):
            for f, far in enumerate(marks):
                for b in range(2):
                    for c in range(2):
                        near = far | a * NEAR | (CORE if other else 0)
                        even, odd = (c, near | b * SIDE), (b, near | c * SIDE)
                        labels = (odd, even) if other else (even, odd)
                        part, rel = (labels[0][0], labels[1][0]), (labels[0][1], labels[1][1])
                        moves.append((2 * other + b, c * 2 * fars + a * fars + f, None, part, rel, None))
    return moves


def joint_grad(lefts, rights, width, first, parts=None, late=False):
    depth = lefts[0].shape[1]
    count = lax.axis_size("fsdp")
    block = depth // count
    total = rights[0].shape[1]
    columns = total // 2
    direct = block % 16 == 0
    tile = 4 * block if direct else 2 * LANES
    steps = depth // tile
    far_count, places = split_places(late)
    shape = (far_count, 2, 2, block, width)
    given = [] if parts is None or not direct else list(parts)

    def wrapped(place_ref, *refs):
        ins, refs = refs[:4], refs[4 + len(given) :]
        step = pl.program_id(0)
        value = slim(dot_first(ins[0][...], ins[2][...]) + dot_first(ins[1][...], ins[3][...]))
        if not direct:
            refs[0][...] = value
            return
        outs, held, sems = refs[:2], refs[2], refs[3]
        held[step] = value.reshape(4, block, total)

        @pl.when(step == steps - 1)
        def _():
            copies = []
            odd = lax.rem(place_ref[1], 2)
            for (a, f, b, c), (even_place, odd_place) in places.items():
                part = place_ref[0] ^ (even_place[0] * (1 - odd) + odd_place[0] * odd)
                number = place_ref[1] ^ (even_place[1] * (1 - odd) + odd_place[1] * odd)
                source = held.at[lax.div(number, 4), lax.rem(number, 4)]
                source = source.at[:, pl.ds(pl.multiple_of(part * columns, LANES), columns)]
                target = outs[a].at[f, b, c, :, pl.ds(first, columns)]
                copies.append(pltpu.make_async_copy(source, target, sems.at[len(copies)]))
            for copy in copies:
                copy.start()
            for copy in copies:
                copy.wait()

    specs = [pl.BlockSpec(memory_space=pltpu.SMEM)]
    specs += [pl.BlockSpec((left.shape[0], tile), lambda i: (0, i)) for left in lefts]
    specs += [full_spec(right) for right in rights]
    specs += [pl.BlockSpec(memory_space=pl.ANY)] * len(given)
    scratch = []
    if direct:
        scratch = [
            pltpu.VMEM((steps, 4, block, total), jnp.bfloat16),
            pltpu.SemaphoreType.DMA((len(places),)),
        ]
    flops = 4 * lefts[0].shape[0] * depth * total
    results = pl.pallas_call(
        wrapped,
        out_shape=[shaped(shape)] * 2 if direct else [shaped((depth, total))],
        grid=(steps,),
        in_specs=specs,
        out_specs=[pl.BlockSpec(memory_space=pl.ANY)] * 2
        if direct
        else [pl.BlockSpec((tile, total), lambda i: (i, 0))],
        scratch_shapes=scratch,
        input_output_aliases={5: 0, 6: 1} if given else {},
        compiler_params=pltpu.CompilerParams(vmem_limit_bytes=VMEM),
        cost_estimate=pl.CostEstimate(flops=flops // SCALE, bytes_accessed=0, transcendentals=0),
    )(here(), *lefts, *rights, *given)
    if direct:
        return results
    order = jnp.array([[place[0] for place in pair] for pair in places.values()])
    blocks = jnp.array([[place[1] for place in pair] for pair in places.values()])
    odd = own_bit("fsdp", CORE)
    halves = results[0].reshape(count, block, 2, columns)
    value = halves[lax.axis_index("fsdp") ^ blocks[:, odd], :, lax.axis_index("tp") ^ order[:, odd]]
    value = value.reshape(2, far_count, 2, 2, block, columns)
    old = jnp.zeros((2,) + shape, jnp.bfloat16) if parts is None else jnp.stack(parts)
    value = lax.dynamic_update_slice_in_dim(old, value, first, 5)
    return [value[0], value[1]]


LINKS = [(X, ("fsdp", SIDE)), (("fsdp", SIDE), Z), (Z, X)]
LATE_LINKS = [LINKS[1], LINKS[2], LINKS[0]]


def split_step(keep, send, step, late=False):
    got = swap_both(send, *(LATE_LINKS if late else LINKS)[step])
    return keep, got


def split_next(keep, got, step):
    if step == 0:
        parts = (keep[:, :, 0], got[:, :, 0]), (keep[:, :, 1], got[:, :, 1])
    elif step == 1:
        parts = (keep[:, 0], got[:, 0]), (keep[:, 1], got[:, 1])
    else:
        return add_pair(keep, got)
    return [add_pair(*part) for part in parts]


def far_totals(piece):
    fars = [0]
    for bit in far_bits():
        fars += [rel | bit for rel in fars]
    pieces = {rel: piece[i] for i, rel in enumerate(fars)}
    for bit in far_bits():
        merged = {}
        for rel in [key for key in pieces if key & bit]:
            got = swap(slim(pieces[rel]), "fsdp", bit)
            merged[rel ^ bit] = wide(pieces[rel ^ bit]) + wide(got)
        pieces = merged
    return pieces[0]


def body(
    tokens, seq_lens, gain_attn, gain_mlp, w_qkv, b_qkv, w_out, w_gate, w_up, w_down, cotangent
):
    rows, width = tokens.shape
    count = lax.axis_size("fsdp")
    block = w_qkv.shape[0]
    units = w_gate.shape[1]
    quarter = -(-units // (4 * LANES)) * LANES
    query_end = HEADS // KV * HD
    place = lax.axis_index("tp")

    own_rows = place * rows + jnp.arange(rows, dtype=jnp.int32)
    other_rows = (1 - place) * rows + jnp.arange(rows, dtype=jnp.int32)
    segment, position = segment_of(own_rows, seq_lens[0])
    other_segment, _ = segment_of(other_rows, seq_lens[0])
    key_rows = jnp.concatenate([own_rows, other_rows])
    key_segment = jnp.concatenate([segment, other_segment])
    allowed = (segment[:, None] == key_segment[None, :]) & (key_rows[None, :] <= own_rows[:, None])
    mask = jnp.where(allowed, 0.0, -1e30).astype(jnp.float32)
    valid = segment < seq_lens.shape[1]
    out_grad = cotangent * valid[:, None].astype(jnp.bfloat16)
    cosine, sine = rope_tables(position)

    small = jnp.concatenate([gain_attn, gain_mlp, b_qkv[0]])
    used = -(-small.shape[0] // LANES)
    small = jnp.pad(small, (0, block * LANES - small.shape[0])).reshape(block, LANES)
    joint = jnp.concatenate([w_qkv, small], axis=1)
    widths = [query_end, w_qkv.shape[1] - query_end, LANES]
    kept, got, halves = send_units([w_gate, w_up, w_down.T], quarter)
    far = far_gather(joint)
    got, kept = tie(got, kept)
    kept, given = halves(kept, got)
    near_got = swap(given[0], *Z)
    near_got, far, mask, out_grad, cosine, sine, own_out = tie(
        near_got, far, mask, out_grad, cosine, sine, w_out.T
    )
    quads = [jnp.concatenate([kept[0], near_got])]
    labels = [(0, rel) for rel in far]
    far = jnp.stack(list(far.values()))
    parts = [far[:, :, start : start + size] for start, size in thirds(joint.shape[1])]
    marks = [labels] * 3

    far_gate, far_out = [], None
    for step in range(3):
        step_all(parts, marks, step)
        if step < 2:
            far_gate += far_units(quads[0], step, step + 1)
        else:
            far_out = far_gather(own_out)
        parts, far_gate, far_out, quads, given, out_grad, own_out = tie(
            parts, far_gate, far_out, quads, given, out_grad, own_out
        )

    own_gate = [(quads[0], INNER)]
    others = [swap(part, "fsdp", CORE) for part in parts]
    out_all = jnp.stack(list(far_out.values()))
    out_got = swap_both(out_all, *OUT_LINKS[0])
    parts, others, quads, out_grad, given, far_gate, out_got, out_all = tie(
        parts, others, quads, out_grad, given, far_gate, out_got, out_all
    )
    out_all = jnp.concatenate([out_all, out_got])

    moves = joint_moves(marks, widths)
    arrays = parts + others
    query_weights, kv_weights = [
        bundle(arrays, moves[i], (2, width, widths[i])) for i in range(2)
    ]
    tops = [array[:, : min(block, 16)] for array in (arrays[2], arrays[5])]
    small_moves = [
        (move[0] // 3, move[1], (move[2][0], LANES), 0, move[3], move[4], 0) for move in moves[2]
    ]
    small = place_blocks(tops, small_moves, [(2, count, min(block, 16), LANES)])[0]
    small = wide(small[:, :, :used].reshape(2, count, -1))
    gain_one = small[0, :, :block].reshape(1, width)
    gain_two = small[0, :, block : 2 * block].reshape(1, width)
    bias = small[:, :, 2 * block : 2 * block + b_qkv.shape[1]].reshape(KV, -1)
    out_got = swap_both(out_all, *OUT_LINKS[1])
    piece_gate = far_units(quads[0], 2, 3)
    all_gate = side_units(part_of(own_gate, 0, 1))
    normed_one, own = project_keys(tokens, gain_one, bias[:, query_end:], cosine, sine, kv_weights)
    own, normed_one, all_gate, given, quads, piece_gate, out_got, out_all = tie(
        own, normed_one, all_gate, given, quads, piece_gate, out_got, out_all
    )
    far_gate += piece_gate
    out_all = jnp.concatenate([out_all, out_got])

    other = swap(own, "tp", 1)
    near_got = swap(given[1], *Z)
    piece_gate = far_units(quads[0], 3, 4)
    all_gate += side_units(part_of(own_gate, 1, 3))
    out_core = swap(out_all, "fsdp", CORE)
    queries = project_queries(normed_one, bias[:, :query_end], cosine, sine, query_weights)
    queries, other, near_got, piece_gate, all_gate, given, quads, far_gate, out_core, out_all = tie(
        queries, other, near_got, piece_gate, all_gate, given, quads, far_gate, out_core, out_all
    )
    far_gate += piece_gate
    quads.append(jnp.concatenate([kept[1], near_got]))
    own_up = [(quads[1], INNER)]

    keys_values = jnp.concatenate([own, other])
    out_got = swap_both(out_all, *OUT_LINKS[2])
    near_got = swap(given[2], *Z)
    far_up = far_units(quads[1], 0, 1)
    mixed = attend(queries, keys_values, mask)
    mixed, near_got, far_up, quads, far_gate, out_got, out_grad = tie(
        mixed, near_got, far_up, quads, far_gate, out_got, out_grad
    )
    quads.append(jnp.concatenate([kept[2], near_got]))
    own_down = [(quads[2], INNER)]

    out_arrays = [out_all, out_got, out_core, swap(out_got, "fsdp", CORE)]
    out_arrays, mixed, quads, far_gate = tie(out_arrays, mixed, quads, far_gate)
    out_weights = bundle(out_arrays, split_moves(len(far_out)), (2, width, w_out.shape[0]))
    piece_up = far_units(quads[1], 1, 2)
    all_gate += side_units(part_of(own_gate, 3, 4) + far_gate[:2])
    grad_got = swap_both(out_grad, X, Z)
    hidden, normed_two = project_out(mixed, tokens, gain_two, out_weights)
    normed_two, piece_up, all_gate, quads, far_gate, grad_got = tie(
        normed_two, piece_up, all_gate, quads, far_gate, grad_got
    )
    far_up += piece_up

    normed_first = spread_first(normed_two)
    piece_up = far_units(quads[1], 2, 4)
    all_gate += side_units(far_gate[2:] + part_of(own_up, 0, 1))
    grad_first = jnp.concatenate([out_grad, grad_got])
    normed_first, piece_up, all_gate, quads, far_up, normed_one, grad_first = tie(
        normed_first, piece_up, all_gate, quads, far_up, normed_one, grad_first
    )
    far_up += piece_up

    normed_second = spread_second(normed_first)
    normed_core = [swap(normed_first, "fsdp", CORE)]
    normed_first, normed_core, quads = tie(normed_first, normed_core, quads)
    all_up = side_units(part_of(own_up, 1, 4) + far_up[:1])
    normed_got = swap(normed_one, "fsdp", CORE)
    gate_weights = unit_bundle(own_gate + far_gate + all_gate[:3] + [pick_units(all_gate[3], 0, 2)])
    normed_pieces = [[normed_first, normed_core[0]], None]
    gates = [gated(normed_pieces[0], gate_weights)[0]]
    normed_second, all_up, normed_got, gates, quads, far_up, grad_first, mixed = tie(
        normed_second, all_up, normed_got, gates, quads, far_up, grad_first, mixed
    )

    normed_pieces[1] = [normed_second, swap(normed_second, "fsdp", CORE)]
    normed_pieces, grad_first, far_up, quads = tie(normed_pieces, grad_first, far_up, quads)
    grad_second = [spread_second(grad_first[:rows])]
    far_down = far_units(quads[2], 0, 2)
    all_up += side_units(far_up[1:])
    gates += gated(normed_pieces[1], gate_weights)
    grad_first, grad_second, far_down, all_up, gates, quads, mixed = tie(
        grad_first, grad_second, far_down, all_up, gates, quads, mixed
    )

    grad_core = [swap(grad_first, "fsdp", CORE), swap(grad_second[0], "fsdp", CORE)]
    grad_second.append(spread_second(grad_first[rows:]))
    piece_down = far_units(quads[2], 2, 4)
    all_down = side_units(own_down)
    up_weights = unit_bundle(own_up + far_up + [pick_units(all_gate[3], 2, 3)] + all_up)
    slope, silu, act = gated(normed_pieces[0] + normed_pieces[1], up_weights, gates)
    act, grad_second, grad_core, piece_down, all_down, far_down, grad_first, quads, mixed = tie(
        act, grad_second, grad_core, piece_down, all_down, far_down, grad_first, quads, mixed
    )
    far_down += piece_down
    grad_core.append(swap(grad_second[1], "fsdp", CORE))
    grad_core, far_down, act, quads, mixed = tie(grad_core, far_down, act, quads, mixed)
    grad_pieces = [[grad_first, grad_core[0]], grad_second + grad_core[1:]]

    all_down += side_units(far_down)
    mixed_got = swap(mixed, "fsdp", CORE)
    grad_down = weight_grad(grad_pieces[0] + grad_pieces[1], [act], quarter)
    grad_down, grad_pieces, all_down, far_down, mixed_got = tie(
        grad_down, grad_pieces, all_down, far_down, mixed_got
    )
    down_weights = unit_bundle(own_down + far_down + all_down)

    codes = [rel for rel in grad_down if rel & SIDE == 0]
    far_codes = [rel for rel in codes if rel]
    down_got = {rel: swap(grad_down[rel | SIDE], "fsdp", SIDE) for rel in far_codes}
    both_weights = side_by_side(gate_weights, up_weights)
    grad_both_1, part_1, core_1 = gated_back(
        grad_pieces[1], slope, silu, 4 * rows, both_weights, down_weights, 2
    )
    down_got, part_1, core_1, act, grad_down = tie(down_got, part_1, core_1, act, grad_down)

    core_1 = swap(core_1, "fsdp", CORE)
    down_out = {rel: add_pair(grad_down[rel], got) for rel, got in down_got.items()}
    down_sum = [far_sums({rel: piece[:2] for rel, piece in down_out.items()})]
    down_got = swap(grad_down[SIDE], "fsdp", SIDE)
    out_own, out_other = down_rows([act], down_weights, normed_pieces[0] + normed_pieces[1])
    core_1, down_got, out_own, out_other, part_1, grad_pieces, down_sum, down_out = tie(
        core_1, down_got, out_own, out_other, part_1, grad_pieces, down_sum, down_out
    )

    got_1 = swap_both(add_pair(part_1, core_1), Z, X)
    out_core = swap(out_other, "fsdp", CORE)
    grad_both_0, part_0, core_0 = gated_back(
        grad_pieces[0], slope, silu, 0, both_weights, down_weights, 1
    )
    part_0, core_0, got_1, down_out, out_core, out_own, normed_sent = tie(
        part_0, core_0, got_1, down_out, out_core, out_own, normed_pieces
    )

    core_0 = swap(core_0, "fsdp", CORE)
    down_sum.append(far_sums({rel: piece[2:] for rel, piece in down_out.items()}))
    grad_gate = weight_grad(normed_sent[0] + normed_sent[1], [grad_both_0, grad_both_1], quarter, 0)
    core_0, down_sum, grad_gate, part_0, got_1, normed_sent = tie(
        core_0, down_sum, grad_gate, part_0, got_1, normed_sent
    )

    got_0 = swap_both(slim(wide(part_0[rows:]) + wide(core_0[rows:]) + wide(got_1[rows:])), X, Z)
    gate_got = {rel: swap(grad_gate[rel | SIDE], "fsdp", SIDE) for rel in far_codes}
    grad_up = weight_grad(normed_sent[0] + normed_sent[1], [grad_both_0, grad_both_1], quarter, 1)
    down_sum = add_pair(wide(grad_down[0]) + wide(down_got), jnp.concatenate(down_sum))
    got_0, gate_got, grad_up, part_0, core_0, got_1, down_sum, grad_gate = tie(
        got_0, gate_got, grad_up, part_0, core_0, got_1, down_sum, grad_gate
    )

    gate_out = {rel: add_pair(grad_gate[rel], got) for rel, got in gate_got.items()}
    gate_sum = [far_sums({rel: piece[:1] for rel, piece in gate_out.items()})]
    up_got = [{rel: swap(grad_up[rel | SIDE][:2], "fsdp", SIDE) for rel in far_codes}]
    down_share = share_near(down_sum)
    grads = [part_0, core_0, got_1, got_0]
    grad_hidden, grad_gain_two, branch, grad_mixed = norm_back_out(
        grads, hidden, out_grad, gain_two, out_weights
    )
    branch, grad_mixed, down_share, gate_sum, gate_out, up_got, grad_up, grad_gate = tie(
        branch, grad_mixed, down_share, gate_sum, gate_out, up_got, grad_up, grad_gate
    )
    branch_got = swap(branch, "fsdp", CORE)
    out_sum = add_pair(out_own[2 * rows :], out_core[2 * rows :])
    branch, branch_got, grad_gate, gate_out, out_sum, grad_up = tie(
        branch, branch_got, grad_gate, gate_out, out_sum, grad_up
    )

    gate_sum.append(far_sums({rel: piece[1:2] for rel, piece in gate_out.items()}))
    up_got.append({rel: swap(grad_up[rel | SIDE][2:], "fsdp", SIDE) for rel in far_codes})
    out_got = [swap_both(out_sum[:rows], Z, X)]
    out_piece = joint_grad([branch, branch_got], [mixed, mixed_got], query_end, 0, None, True)
    out_piece, gate_sum, up_got, out_got, out_sum, gate_out, grad_mixed, grad_gate, grad_up = tie(
        out_piece, gate_sum, up_got, out_got, out_sum, gate_out, grad_mixed, grad_gate, grad_up
    )

    out_got.append(swap_both(out_sum[rows:], Z, X))
    gate_sum.append(far_sums({rel: piece[2:] for rel, piece in gate_out.items()}))
    gate_got = swap(grad_gate[SIDE], "fsdp", SIDE)
    up_got = {rel: jnp.concatenate([got[rel] for got in up_got]) for rel in far_codes}
    up_out = {rel: add_pair(grad_up[rel], got) for rel, got in up_got.items()}
    grad_query, grad_keys, grad_values = attend_back(
        queries, keys_values, mask, grad_mixed, cosine, sine
    )
    grad_query, grad_keys, grad_values, out_got, gate_sum, gate_got, up_out, grad_up, out_piece = tie(
        grad_query, grad_keys, grad_values, out_got, gate_sum, gate_got, up_out, grad_up, out_piece
    )

    other = swap(slim(jnp.concatenate([grad_keys[rows:], grad_values[rows:]], 1)), "tp", 1)
    query_got = swap(grad_query, "fsdp", CORE)
    query_got, grad_query, out_piece, grad_up = tie(query_got, grad_query, out_piece, grad_up)
    out_pair = split_step(*out_piece, 0, True)
    up_sum = [far_sums({rel: piece[:1] for rel, piece in up_out.items()})]
    up_got = [swap(grad_up[SIDE][:2], "fsdp", SIDE)]
    size = w_qkv.shape[1]
    parts = joint_grad([normed_one, normed_got], [grad_query, query_got], size, 0)
    parts, other, out_pair, up_sum, up_got, up_out, grad_up, out_got = tie(
        parts, other, out_pair, up_sum, up_got, up_out, grad_up, out_got
    )

    grad_kv, query_sums, kv_sums = finish_keys(
        grad_keys, grad_values, other, grad_query, cosine, sine
    )
    grad_kv, out_got, gate_got, gate_sum = tie(grad_kv, out_got, gate_got, gate_sum)
    out_sums = [
        wide(out_own[at : at + rows]) + wide(out_core[at : at + rows]) + wide(got)
        for at, got in zip((0, rows), out_got)
    ]
    out_sent = slim(out_sums[1])
    out_pair = split_next(*out_pair, 0)
    kv_got = swap(grad_kv, "fsdp", CORE)
    kv_got, out_pair, out_sent, grad_up, up_out = tie(kv_got, out_pair, out_sent, grad_up, up_out)
    out_pair = split_step(*out_pair, 1, True)
    out_got = swap_both(out_sent, X, Z)
    up_got.append(swap(grad_up[SIDE][2:], "fsdp", SIDE))
    gate_sum = add_pair(wide(grad_gate[0]) + wide(gate_got), jnp.concatenate(gate_sum))
    kv_got, grad_kv, gate_sum = tie(kv_got, grad_kv, gate_sum)
    parts = joint_grad([normed_one, normed_got], [grad_kv, kv_got], size, query_end, parts)
    parts, gate_sum, up_out, up_sum, up_got, out_pair, out_got = tie(
        parts, gate_sum, up_out, up_sum, up_got, out_pair, out_got
    )

    parts, grad_hidden = tie(parts, grad_hidden)
    pair = split_step(*parts, 0)
    up_sum.append(far_sums({rel: piece[1:3] for rel, piece in up_out.items()}))
    gate_share = share_near(gate_sum)
    out_pair = split_step(*split_next(*out_pair, 1), 2, True)
    grad_inputs, grad_gain_one = project_back(
        grad_query, grad_kv, tokens, grad_hidden, gain_one, query_weights, kv_weights
    )
    share = block // 2
    query_sums = query_sums.reshape(KV, query_end)
    grad_bias = jnp.concatenate([query_sums, kv_sums.reshape(KV, 2 * HD)], axis=1)
    small = jnp.concatenate(
        [
            grad_gain_one.reshape(count, 2, share).swapaxes(0, 1),
            grad_gain_two.reshape(count, 2, share).swapaxes(0, 1),
            grad_bias.reshape(2, count, -1),
        ],
        axis=2,
    ).reshape(2 * count, -1)
    out_rows = slim(hidden + out_sums[0] + wide(out_got))
    pair, up_sum, gate_share, grad_inputs, small, out_pair, out_rows, up_out = tie(
        pair, up_sum, gate_share, grad_inputs, small, out_pair, out_rows, up_out
    )

    pair = split_step(*split_next(*pair, 0), 1)
    up_sum.append(far_sums({rel: piece[3:] for rel, piece in up_out.items()}))
    up_home = wide(grad_up[0]) + wide(jnp.concatenate(up_got))
    out_total = split_next(*out_pair, 2)
    small = small_step(small, "tp", [1])
    pair, up_sum, small, out_total = tie(pair, up_sum, small, out_total)
    up_sum = add_pair(up_home, jnp.concatenate(up_sum))

    pair = split_step(*split_next(*pair, 1), 2)
    small = small_step(small, "fsdp", far_bits() + [NEAR])
    up_share = share_near(up_sum)
    out_total = far_totals(out_total)
    pair, small, up_share, out_total = tie(pair, small, up_share, out_total)

    qkv_total = far_totals(split_next(*pair, 2))
    small_sum = small_step(small, "fsdp", [SIDE, CORE])[0]
    gate_sum, up_sum, down_sum = share_cores([gate_share, up_share, down_share], units)
    return (
        out_rows,
        grad_inputs,
        small_sum[:share],
        small_sum[share : 2 * share],
        qkv_total,
        small_sum[None, 2 * share :],
        out_total.T,
        gate_sum,
        up_sum,
        down_sum.T,
    )


def solution(mesh):
    placed = (
        P(("fsdp", "tp"), None),
        P("fsdp", None),
        P("fsdp"),
        P("fsdp"),
        P("fsdp", "tp"),
        P("tp", "fsdp"),
        P("tp", "fsdp"),
        P("fsdp", "tp"),
        P("fsdp", "tp"),
        P("tp", "fsdp"),
        P(("fsdp", "tp"), None),
    )
    return jax.shard_map(
        body,
        mesh=mesh,
        in_specs=placed,
        out_specs=(
            P(("fsdp", "tp"), None),
            P(("fsdp", "tp"), None),
            P(("fsdp", "tp")),
            P(("fsdp", "tp")),
            P("fsdp", "tp"),
            P("tp", "fsdp"),
            P("tp", "fsdp"),
            P("fsdp", "tp"),
            P("fsdp", "tp"),
            P("tp", "fsdp"),
        ),
        check_vma=False,
    )
```

time: 675 us -> 653 us (0.967)
  waiting for transfers between devices: 215 us -> 177 us
  local copies, waits for them, and re-layouts: 34.9 us -> 43.1 us
    ppermute x84 -> x81, waiting for transfers between devices: 192 us -> 146 us  [swap(): return lax.ppermute(values, axis, [(i, i ^ bit) for i in range(count)])]
    ppermute x9 -> x19, starting transfers between devices: 10.5 us -> 21.2 us  [swap_both(): return lax.ppermute(values, ('fsdp', 'tp'), pairs)]
    slice x3 -> x16, local copies, waits for them, and re-layouts: 1.44 us -> 10.6 us  [the longest x1 1.81 us: body(): up_got.append(swap(grad_up[SIDE][2:], 'fsdp', SIDE))]
    ppermute x9 -> x19, waiting for transfers between devices: 22.3 us -> 30.9 us  [swap_both(): return lax.ppermute(values, ('fsdp', 'tp'), pairs)]
    ppermute x84 -> x81, starting transfers between devices: 83.5 us -> 75.3 us  [swap(): return lax.ppermute(values, axis, [(i, i ^ bit) for i in range(count)])]
    squeeze x11 -> x5, local copies, waits for them, and re-layouts: 7.59 us -> 0.05 us  [the longest x2 0.03 us: far_totals(): pieces = {rel: piece[i] for i, rel in enumerate(fars)}]
    pallas_call x2 -> x3, Pallas kernels: 19.7 us -> 23.6 us  [joint_grad(): pl.pallas_call(wrapped, out_shape=[shaped(shape)] * 2 if direct else [sha...]
    pallas_call x12 -> x14, Pallas kernels: 179 us -> 177 us  [run_kernel(): pl.pallas_call(wrapped, out_shape=outs, grid=(steps,), in_specs=[pl.Block...]
  transfers between devices with their start and end apart: 93 -> 100, of which waited for: 38 -> 48; matrix products, arithmetic and copies ran while one was open for 9% -> 12% of each run, Pallas kernels for 39% -> 40%
where the time goes in v3:
time: 653 us; the launch traced here: 644 us
  Pallas kernels  260 us (40%)
  waiting for transfers between devices  177 us (27%)
  starting transfers between devices  96.5 us (15%)
  other arithmetic  64.6 us (10%)
  local copies, waits for them, and re-layouts  43.1 us (7%)
    pallas_call x14, Pallas kernels, run_kernel(): pl.pallas_call(wrapped, out_shape=outs, grid=(steps,), in_specs=[pl.Block...  177 us
    ppermute x81, waiting for transfers between devices, swap(): return lax.ppermute(values, axis, [(i, i ^ bit) for i in range(count)])  146 us
    ppermute x81, starting transfers between devices, swap(): return lax.ppermute(values, axis, [(i, i ^ bit) for i in range(count)])  75.3 us
    pallas_call x3, Pallas kernels, weight_grad(): pl.pallas_call(wrapped, out_shape=outs, grid=(steps,), in_specs=[pl.Block...  57.2 us
    convert_element_type x21, other arithmetic, slim(): return values.astype(jnp.bfloat16)  32 us
    ppermute x19, waiting for transfers between devices, swap_both(): return lax.ppermute(values, ('fsdp', 'tp'), pairs)  30.9 us
    pallas_call x3, Pallas kernels, joint_grad(): pl.pallas_call(wrapped, out_shape=[shaped(shape)] * 2 if direct else [sha...  23.6 us
    ppermute x19, starting transfers between devices, swap_both(): return lax.ppermute(values, ('fsdp', 'tp'), pairs)  21.2 us
  transfers between devices with their start and end apart: 100, of which 48 were waited for; matrix products, arithmetic and copies ran while one was open for 12% of the time, Pallas kernels for 40%

profile of v3, /device:TPU:0, one launch (start us, length us, event | category | flops | bytes accessed | tf_op | source)
XLA Modules:
  0.0 643.7 jit_solution(10570435002311368221)
XLA Ops:
  19.3 14.1 %collective-permute-done.1 = bf16[2,96,1152]{2,1,0:T(8,128)(2,1)S(1)} collective-permute-done((bf16[2,96,1152]{2,1,0:T(8,128)(2,1)S(1)}, bf16[2,96,1152]{2,1,0:T(8,128)(2,1)S(1)}, u32[]{:S(2)}, u32[]{:S(2)}) %collective-permute-start.1) | collective-permute-done | bytes 442400 | tf_op jit(solution)/shard_map/ppermute | solution.py:29
  48.7 5.9 collective-permute-done.8
  60.5 5.6 collective-permute-done.13
  74.3 7.1 %collective-permute-done.18 = bf16[2,96,768]{2,1,0:T(8,128)(2,1)S(1)} collective-permute-done((bf16[2,96,768]{2,1,0:T(8,128)(2,1)S(1)}, bf16[2,96,768]{2,1,0:T(8,128)(2,1)S(1)}, u32[]{:S(2)}, u32[]{:S(2)}) %collective-permute-start.18) | collective-permute-done | bytes 294944 | tf_op jit(solution)/shard_map/ppermute | solution.py:40
  112.1 7.1 %shard_map.188.refs_0_ = bf16[320,1536]{1,0:T(8,128)(2,1)} custom-call(s32[2]{0:T(128)} %pad_add_fusion.2.place_ref, bf16[320,1536]{1,0:T(8,128)(2,1)} %get-tuple-element.513.refs_0_, f32[2,768]{1,0:T(2,128)} %slice.417.refs_1_, f32[320,128]{1,0:T(8,128)} %get-tuple-element.445.refs_3_.refs_2_.refs_5_.refs_4_, ...), custom_call_target="tpu_custom_call" | custom-call | flops 23592960 | bytes 146528 | tf_op jit(solution)/shard_map/pallas_call | solution.py:212
  132.0 10.3 %shard_map.189.refs_0_.refs_2_ = bf16[320,1536]{1,0:T(8,128)(2,1)} custom-call(s32[2]{0:T(128)} %pad_add_fusion.2.place_ref, bf16[320,1536]{1,0:T(8,128)(2,1)} %shard_map.188.refs_0_, bf16[640,512]{1,0:T(8,128)(2,1)} %copy-done.14, bf16[640,512]{1,0:T(8,128)(2,1)} %copy-done.14, f32[320,640]{1,0:T(8,128)} %and_select_fusion.refs_3_), custom_call_target="tpu_custom_call" | custom-call | flops 19660800 | bytes 64000 | tf_op jit(solution)/shard_map/pallas_call | solution.py:212
  152.8 7.6 %shard_map.190 = (f32[320,1536]{1,0:T(8,128)}, bf16[320,1536]{1,0:T(8,128)(2,1)}) custom-call(s32[2]{0:T(128)} %pad_add_fusion.2.place_ref, bf16[320,1536]{1,0:T(8,128)(2,1)} %shard_map.189.refs_0_.refs_2_, bf16[320,1536]{1,0:T(8,128)(2,1)} %refs_2_.1, f32[1,1536]{1,0:T(1,128)} %reshape_squeeze.7.refs_2_.refs_6_, bf16[8,96,768]{2,1,0:T(8,128)(2,1)} %copy-done.22, ...), custom_call_target="tpu_custom_call" | custom-call | flops 23592960 | bytes 150624 | tf_op jit(solution)/shard_map/pallas_call | solution.py:212
  173.8 7.6 %collective-permute-done.34 = bf16[320,1536]{1,0:T(8,128)(2,1)S(1)} collective-permute-done((bf16[320,1536]{1,0:T(8,128)(2,1)}, bf16[320,1536]{1,0:T(8,128)(2,1)S(1)}, u32[]{:S(2)}, u32[]{:S(2)}) %collective-permute-start.34) | collective-permute-done | bytes 983072 | tf_op jit(solution)/shard_map/ppermute | solution.py:40
  181.6 10.5 %collective-permute-done.35.refs_9_.refs_23_.refs_21_ = bf16[2,96,1152]{2,1,0:T(8,128)(2,1)S(1)} collective-permute-done((bf16[2,96,1152]{2,1,0:T(8,128)(2,1)S(1)}, bf16[2,96,1152]{2,1,0:T(8,128)(2,1)S(1)}, u32[]{:S(2)}, u32[]{:S(2)}) %collective-permute-start.35) | collective-permute-done | bytes 442400 | tf_op jit(solution)/shard_map/ppermute | solution.py:29
  196.2 10.6 %shard_map.191.refs_4_ = bf16[1280,1152]{1,0:T(8,128)(2,1)} custom-call(s32[2]{0:T(128)} %pad_add_fusion.2.place_ref, bf16[640,1536]{1,0:T(8,128)(2,1)} %copy-done, bf16[640,1536]{1,0:T(8,128)(2,1)} %collective-permute-done.40.refs_1_, bf16[4,96,1152]{2,1,0:T(8,128)(2,1)} %copy-done.1, bf16[1,96,1152]{2,1,0:T(8,128)(2,1)} %copy-done.27, ...), custom_call_target="tpu_custom_call" | custom-call | flops 70778880 | bytes 166272 | tf_op jit(solution)/shard_map/pallas_call | solution.py:212
  206.9 9.4 %collective-permute-done.38.refs_11_.refs_25_.refs_23_ = bf16[4,96,1152]{2,1,0:T(8,128)(2,1)S(1)} collective-permute-done((bf16[4,96,1152]{2,1,0:T(8,128)(2,1)}, bf16[4,96,1152]{2,1,0:T(8,128)(2,1)S(1)}, u32[]{:S(2)}, u32[]{:S(2)}) %collective-permute-start.38) | collective-permute-done | bytes 884768 | tf_op jit(solution)/shard_map/ppermute | solution.py:29
  228.9 10.7 %shard_map.192.refs_5_ = bf16[1280,1152]{1,0:T(8,128)(2,1)} custom-call(s32[2]{0:T(128)} %pad_add_fusion.2.place_ref, bf16[640,1536]{1,0:T(8,128)(2,1)} %collective-permute-done.37.refs_0_.refs_2_, bf16[640,1536]{1,0:T(8,128)(2,1)} %copy-done.5, bf16[4,96,1152]{2,1,0:T(8,128)(2,1)} %copy-done.1, bf16[1,96,1152]{2,1,0:T(8,128)(2,1)} %copy-done.27, ...), custom_call_target="tpu_custom_call" | custom-call | flops 70778880 | bytes 166272 | tf_op jit(solution)/shard_map/pallas_call | solution.py:212
  239.6 10.3 %collective-permute-done.43.refs_7_.refs_2_.refs_5_ = bf16[2,96,1152]{2,1,0:T(8,128)(2,1)} collective-permute-done((bf16[2,96,1152]{2,1,0:T(8,128)(2,1)}, bf16[2,96,1152]{2,1,0:T(8,128)(2,1)}, u32[]{:S(2)}, u32[]{:S(2)}) %collective-permute-start.43) | collective-permute-done | bytes 442400 | tf_op jit(solution)/shard_map/ppermute | solution.py:29
  255.0 21.2 %shard_map.193 = (bf16[2560,1152]{1,0:T(8,128)(2,1)}, bf16[2560,1152]{1,0:T(8,128)(2,1)}, bf16[2560,1152]{1,0:T(8,128)(2,1)}) custom-call(s32[2]{0:T(128)} %pad_add_fusion.2.place_ref, bf16[640,1536]{1,0:T(8,128)(2,1)} %copy-done, bf16[640,1536]{1,0:T(8,128)(2,1)} %collective-permute-done.40.refs_1_, ...), custom_call_target="tpu_custom_call" | custom-call | flops 141557760 | bytes 553728 | tf_op jit(solution)/shard_map/pallas_call | solution.py:212
  282.7 20.6 %shard_map.194 = (bf16[4,96,1152]{2,1,0:T(8,128)(2,1)}, bf16[4,96,1152]{2,1,0:T(8,128)(2,1)}, bf16[4,96,1152]{2,1,0:T(8,128)(2,1)}, bf16[4,96,1152]{2,1,0:T(8,128)(2,1)}) custom-call(s32[2]{0:T(128)} %pad_add_fusion.2.place_ref, bf16[640,1536]{1,0:T(8,128)(2,1)} %pad_maximum_fusion.2.refs_0_, bf16[640,1536]{1,0:T(8,128)(2,1)} %collective-permute-done.46.refs_1_, ...), custom_call_target="tpu_custom_call" | custom-call | flops 141557760 | bytes 27648 | tf_op jit(solution)/shard_map/pallas_call | solution.py:866
  304.7 24.1 %shard_map.195 = (bf16[1280,2304]{1,0:T(8,128)(2,1)}, bf16[640,1536]{1,0:T(8,128)(2,1)}, bf16[640,1536]{1,0:T(8,128)(2,1)}) custom-call(s32[2]{0:T(128)} %pad_add_fusion.2.place_ref, bf16[320,1536]{1,0:T(8,128)(2,1)} %collective-permute-done.42.refs_2_.refs_0_, bf16[320,1536]{1,0:T(8,128)(2,1)} %collective-permute-done.45.refs_3_.refs_1_, ...), custom_call_target="tpu_custom_call" | custom-call | flops 212336640 | bytes 575616 | tf_op jit(solution)/shard_map/pallas_call | solution.py:212
  334.5 17.9 %shard_map.196 = (bf16[1280,1536]{1,0:T(8,128)(2,1)}, bf16[1280,1536]{1,0:T(8,128)(2,1)}) custom-call(s32[2]{0:T(128)} %pad_add_fusion.2.place_ref, bf16[2560,1152]{1,0:T(8,128)(2,1)} %get-tuple-element.597.refs_6_.refs_0_, bf16[4,96,1152]{2,1,0:T(8,128)(2,1)} %pad_maximum_fusion.12.refs_6_.refs_1_.refs_4_, ...), custom_call_target="tpu_custom_call" | custom-call | flops 141557760 | bytes 270336 | tf_op jit(solution)/shard_map/pallas_call | solution.py:212
  358.7 23.6 %shard_map.197 = (bf16[1280,2304]{1,0:T(8,128)(2,1)}, bf16[640,1536]{1,0:T(8,128)(2,1)}, bf16[640,1536]{1,0:T(8,128)(2,1)}) custom-call(s32[2]{0:T(128)} %pad_add_fusion.2.place_ref, bf16[640,1536]{1,0:T(8,128)(2,1)} %pad_maximum_fusion.2.refs_0_, bf16[640,1536]{1,0:T(8,128)(2,1)} %collective-permute-done.46.refs_1_, ...), custom_call_target="tpu_custom_call" | custom-call | flops 212336640 | bytes 575616 | tf_op jit(solution)/shard_map/pallas_call | solution.py:212
  386.1 18.4 %shard_map.198 = (bf16[4,96,1152]{2,1,0:T(8,128)(2,1)}, bf16[4,96,1152]{2,1,0:T(8,128)(2,1)}, bf16[4,96,1152]{2,1,0:T(8,128)(2,1)}, bf16[4,96,1152]{2,1,0:T(8,128)(2,1)}) custom-call(s32[2]{0:T(128)} %pad_add_fusion.2.place_ref, bf16[640,1536]{1,0:T(8,128)(2,1)} %copy-done, bf16[640,1536]{1,0:T(8,128)(2,1)} %collective-permute-done.40.refs_1_, ...), custom_call_target="tpu_custom_call" | custom-call | flops 141557760 | bytes 27648 | tf_op jit(solution)/shard_map/pallas_call | solution.py:866
  412.5 18.2 %shard_map.199 = (bf16[4,96,1152]{2,1,0:T(8,128)(2,1)}, bf16[4,96,1152]{2,1,0:T(8,128)(2,1)}, bf16[4,96,1152]{2,1,0:T(8,128)(2,1)}, bf16[4,96,1152]{2,1,0:T(8,128)(2,1)}) custom-call(s32[2]{0:T(128)} %pad_add_fusion.2.place_ref, bf16[640,1536]{1,0:T(8,128)(2,1)} %copy-done, bf16[640,1536]{1,0:T(8,128)(2,1)} %collective-permute-done.40.refs_1_, ...), custom_call_target="tpu_custom_call" | custom-call | flops 141557760 | bytes 27648 | tf_op jit(solution)/shard_map/pallas_call | solution.py:866
  437.8 9.6 %shard_map.200 = (f32[320,1536]{1,0:T(8,128)}, f32[1,1536]{1,0:T(1,128)}, bf16[320,1536]{1,0:T(8,128)(2,1)}, bf16[320,1536]{1,0:T(8,128)(2,1)}) custom-call(s32[2]{0:T(128)} %pad_add_fusion.2.place_ref, bf16[640,1536]{1,0:T(8,128)(2,1)} %get-tuple-element.648.refs_0_, bf16[640,1536]{1,0:T(8,128)(2,1)} %collective-permute-done.59.refs_1_, ...), custom_call_target="tpu_custom_call" | custom-call | flops 23592960 | bytes 288960 | tf_op jit(solution)/shard_map/pallas_call | solution.py:212
  458.4 9.1 %shard_map.201 = (bf16[2,2,2,96,768]{4,3,2,1,0:T(8,128)(2,1)}, bf16[2,2,2,96,768]{4,3,2,1,0:T(8,128)(2,1)}) custom-call(s32[2]{0:T(128)} %pad_add_fusion.2.place_ref, bf16[320,1536]{1,0:T(8,128)(2,1)} %get-tuple-element.674.refs_0_, bf16[320,1536]{1,0:T(8,128)(2,1)} %collective-permute-done.66.refs_1_, bf16[320,1536]{1,0:T(8,128)(2,1)} %shard_map.189.refs_0_.refs_2_, ...), custom_call_target="tpu_custom_call" | custom-call | flops 47185920 | tf_op jit(solution)/shard_map/pallas_call | solution.py:979
  467.5 5.3 collective-permute-done.67
  479.1 16.4 %shard_map.202 = (bf16[320,1536]{1,0:T(8,128)(2,1)}, f32[640,256]{1,0:T(8,128)}, f32[640,256]{1,0:T(8,128)}) custom-call(s32[2]{0:T(128)} %pad_add_fusion.2.place_ref, bf16[320,1536]{1,0:T(8,128)(2,1)} %shard_map.188.refs_0_, bf16[640,512]{1,0:T(8,128)(2,1)} %copy-done.14, bf16[640,512]{1,0:T(8,128)(2,1)} %copy-done.14, f32[320,640]{1,0:T(8,128)} %and_select_fusion.refs_3_, ...), custom_call_target="tpu_custom_call" | custom-call | flops 49152000 | bytes 104960 | tf_op jit(solution)/shard_map/pallas_call | solution.py:212
  509.2 9.0 %shard_map.203 = (bf16[2,2,2,96,1024]{4,3,2,1,0:T(8,128)(2,1)}, bf16[2,2,2,96,1024]{4,3,2,1,0:T(8,128)(2,1)}) custom-call(s32[2]{0:T(128)} %pad_add_fusion.2.place_ref, bf16[320,1536]{1,0:T(8,128)(2,1)} %get-tuple-element.513.refs_0_, bf16[320,1536]{1,0:T(8,128)(2,1)} %collective-permute-done.39.refs_1_, ...), custom_call_target="tpu_custom_call" | custom-call | flops 47185920 | tf_op jit(solution)/shard_map/pallas_call | solution.py:979
  518.2 7.7 %collective-permute-done.77 = bf16[2,96,1152]{2,1,0:T(8,128)(2,1)S(1)} collective-permute-done((bf16[2,96,1152]{2,1,0:T(8,128)(2,1)S(1)}, bf16[2,96,1152]{2,1,0:T(8,128)(2,1)S(1)}, u32[]{:S(2)}, u32[]{:S(2)}) %collective-permute-start.77) | collective-permute-done | bytes 442400 | tf_op jit(solution)/shard_map/ppermute | solution.py:29
  543.4 5.6 shard_map.205
  566.4 9.9 %shard_map.206 = (f32[320,1536]{1,0:T(8,128)}, f32[1,1536]{1,0:T(1,128)}) custom-call(s32[2]{0:T(128)} %pad_add_fusion.2.place_ref, bf16[320,1536]{1,0:T(8,128)(2,1)} %get-tuple-element.714.refs_2_.refs_3_.refs_0_, bf16[320,512]{1,0:T(8,128)(2,1)} %get-tuple-element.746.refs_2_.refs_1_, bf16[320,1536]{1,0:T(8,128)(2,1)} %refs_2_.1, ...), custom_call_target="tpu_custom_call" | custom-call | flops 23592960 | bytes 318656 | tf_op jit(solution)/shard_map/pallas_call | solution.py:212
  579.0 4.9 collective-permute-done.83
  590.1 8.4 %collective-permute-done.87 = bf16[1,96,1152]{2,1,0:T(8,128)(2,1)S(1)} collective-permute-done((bf16[1,96,1152]{2,1,0:T(8,128)(2,1)S(1)}, bf16[1,96,1152]{2,1,0:T(8,128)(2,1)S(1)}, u32[]{:S(2)}, u32[]{:S(2)}) %collective-permute-start.87) | collective-permute-done | bytes 221216 | tf_op jit(solution)/shard_map/ppermute | solution.py:29
  609.2 11.4 %collective-permute-done.89 = bf16[2,96,1024]{2,1,0:T(8,128)(2,1)S(1)} collective-permute-done((bf16[2,96,1024]{2,1,0:T(8,128)(2,1)S(1)}, bf16[2,96,1024]{2,1,0:T(8,128)(2,1)S(1)}, u32[]{:S(2)}, u32[]{:S(2)}) %collective-permute-start.89) | collective-permute-done | bytes 393248 | tf_op jit(solution)/shard_map/ppermute | solution.py:40
  629.6 8.8 %collective-permute-done.98 = bf16[96,1024]{1,0:T(8,128)(2,1)S(1)} collective-permute-done((bf16[96,1024]{1,0:T(8,128)(2,1)S(1)}, bf16[96,1024]{1,0:T(8,128)(2,1)S(1)}, u32[]{:S(2)}, u32[]{:S(2)}) %collective-permute-start.98) | collective-permute-done | bytes 196640 | tf_op jit(solution)/shard_map/ppermute | solution.py:29
  (533 shorter events, 274.2 us)
Async XLA Ops:
  16.8 24.0 %collective-permute-start.6 = (bf16[1,96,1152]{2,1,0:T(8,128)(2,1)S(1)}, bf16[1,96,1152]{2,1,0:T(8,128)(2,1)S(1)}, u32[]{:S(2)}, u32[]{:S(2)}) collective-permute-start(bf16[1,96,1152]{2,1,0:T(8,128)(2,1)S(1)} %get-tuple-element.826), channel_id=1, source_target_pairs={{0,16},{2,18},{4,20},{6,22},{8,24},{10,26},{12,28},{14,30},{16,0},... | collective-permute-start | bytes 663560 | tf_op jit(solution)/shard_map/ppermute | solution.py:29
  81.5 21.1 %collective-permute-start.21 = (bf16[4,96,768]{2,1,0:T(8,128)(2,1)S(1)}, bf16[4,96,768]{2,1,0:T(8,128)(2,1)}, u32[]{:S(2)}, u32[]{:S(2)}) collective-permute-start(bf16[4,96,768]{2,1,0:T(8,128)(2,1)S(1)} %constant_dynamic-update-slice_fusion), channel_id=1, source_target_pairs={{0,1},{1,0},{2,6},{3,7},{4,5},{5,4},{6,2},{7,3},{8,9},{9,8},{10,14... | collective-permute-start | bytes 1769480 | tf_op jit(solution)/shard_map/ppermute | solution.py:40
  168.7 23.4 %collective-permute-start.36 = (bf16[3,96,1152]{2,1,0:T(8,128)(2,1)S(1)}, bf16[3,96,1152]{2,1,0:T(8,128)(2,1)S(1)}, u32[]{:S(2)}, u32[]{:S(2)}) collective-permute-start(bf16[3,96,1152]{2,1,0:T(8,128)(2,1)S(1)} %pad_maximum_fusion.17), channel_id=1, source_target_pairs={{0,4},{2,6},{4,0},{6,2},{8,12},{10,14},{12,8},{14,10},{16,20},{18,... | collective-permute-start | bytes 1990664 | tf_op jit(solution)/shard_map/ppermute | solution.py:29
  169.9 22.1 %collective-permute-start.35 = (bf16[2,96,1152]{2,1,0:T(8,128)(2,1)S(1)}, bf16[2,96,1152]{2,1,0:T(8,128)(2,1)S(1)}, u32[]{:S(2)}, u32[]{:S(2)}) collective-permute-start(bf16[2,96,1152]{2,1,0:T(8,128)(2,1)S(1)} %slice.335), channel_id=1, source_target_pairs={{0,16},{2,18},{4,20},{6,22},{8,24},{10,26},{12,28},{14,30},{16,0},... | collective-permute-start | bytes 1327112 | tf_op jit(solution)/shard_map/ppermute | solution.py:29
  192.1 25.1 %collective-permute-start.37 = (bf16[640,1536]{1,0:T(8,128)(2,1)S(1)}, bf16[640,1536]{1,0:T(8,128)(2,1)}, u32[]{:S(2)}, u32[]{:S(2)}) collective-permute-start(bf16[640,1536]{1,0:T(8,128)(2,1)S(1)} %pad_maximum_fusion.1.refs_0_), channel_id=1, source_target_pairs={{0,8},{1,9},{2,3},{3,2},{4,12},{5,13},{6,7},{7,6},{8,0},{9,1},{10,... | collective-permute-start | bytes 5898248 | tf_op jit(solution)/shard_map/ppermute | solution.py:40
  192.3 24.0 %collective-permute-start.39 = (bf16[320,1536]{1,0:T(8,128)(2,1)}, bf16[320,1536]{1,0:T(8,128)(2,1)}, u32[]{:S(2)}, u32[]{:S(2)}) collective-permute-start(bf16[320,1536]{1,0:T(8,128)(2,1)} %get-tuple-element.513.refs_0_), channel_id=1, source_target_pairs={{0,2},{2,0},{4,6},{6,4},{8,10},{10,8},{12,14},{14,12},{16,18},{18,... | collective-permute-start | bytes 2949128 | tf_op jit(solution)/shard_map/ppermute | solution.py:29
  194.5 21.8 %collective-permute-start.38 = (bf16[4,96,1152]{2,1,0:T(8,128)(2,1)}, bf16[4,96,1152]{2,1,0:T(8,128)(2,1)S(1)}, u32[]{:S(2)}, u32[]{:S(2)}) collective-permute-start(bf16[4,96,1152]{2,1,0:T(8,128)(2,1)} %pad_maximum_fusion.13), channel_id=1, source_target_pairs={{0,4},{2,6},{4,0},{6,2},{8,12},{10,14},{12,8},{14,10},{16,20},{18,... | collective-permute-start | bytes 2654216 | tf_op jit(solution)/shard_map/ppermute | solution.py:29
  223.4 26.5 %collective-permute-start.42 = (bf16[320,1536]{1,0:T(8,128)(2,1)S(1)}, bf16[320,1536]{1,0:T(8,128)(2,1)}, u32[]{:S(2)}, u32[]{:S(2)}) collective-permute-start(bf16[320,1536]{1,0:T(8,128)(2,1)S(1)} %slice.337), channel_id=1, source_target_pairs={{0,8},{1,9},{2,3},{3,2},{4,12},{5,13},{6,7},{7,6},{8,0},{9,1},{10,... | collective-permute-start | bytes 2949128 | tf_op jit(solution)/shard_map/ppermute | solution.py:40
  225.8 24.1 %collective-permute-start.44 = (bf16[3,96,1152]{2,1,0:T(8,128)(2,1)}, bf16[3,96,1152]{2,1,0:T(8,128)(2,1)}, u32[]{:S(2)}, u32[]{:S(2)}) collective-permute-start(bf16[3,96,1152]{2,1,0:T(8,128)(2,1)} %pad_maximum_fusion.18), channel_id=1, source_target_pairs={{0,4},{2,6},{4,0},{6,2},{8,12},{10,14},{12,8},{14,10},{16,20},{18,... | collective-permute-start | bytes 1990664 | tf_op jit(solution)/shard_map/ppermute | solution.py:29
  227.9 22.0 %collective-permute-start.43 = (bf16[2,96,1152]{2,1,0:T(8,128)(2,1)}, bf16[2,96,1152]{2,1,0:T(8,128)(2,1)}, u32[]{:S(2)}, u32[]{:S(2)}) collective-permute-start(bf16[2,96,1152]{2,1,0:T(8,128)(2,1)} %slice.338), channel_id=1, source_target_pairs={{0,16},{2,18},{4,20},{6,22},{8,24},{10,26},{12,28},{14,30},{16,0},... | collective-permute-start | bytes 1327112 | tf_op jit(solution)/shard_map/ppermute | solution.py:29
  249.9 26.4 %collective-permute-start.46 = (bf16[640,1536]{1,0:T(8,128)(2,1)S(1)}, bf16[640,1536]{1,0:T(8,128)(2,1)}, u32[]{:S(2)}, u32[]{:S(2)}) collective-permute-start(bf16[640,1536]{1,0:T(8,128)(2,1)S(1)} %copy-done.4), channel_id=1, source_target_pairs={{0,2},{2,0},{4,6},{6,4},{8,10},{10,8},{12,14},{14,12},{16,18},{18,... | collective-permute-start | bytes 5898248 | tf_op jit(solution)/shard_map/ppermute | solution.py:29
  251.0 25.2 %collective-permute-start.45 = (bf16[320,1536]{1,0:T(8,128)(2,1)}, bf16[320,1536]{1,0:T(8,128)(2,1)}, u32[]{:S(2)}, u32[]{:S(2)}) collective-permute-start(bf16[320,1536]{1,0:T(8,128)(2,1)} %slice.339), channel_id=1, source_target_pairs={{0,8},{1,9},{2,3},{3,2},{4,12},{5,13},{6,7},{7,6},{8,0},{9,1},{10,... | collective-permute-start | bytes 2949128 | tf_op jit(solution)/shard_map/ppermute | solution.py:40
  251.0 25.3 %collective-permute-start.47 = (bf16[320,1536]{1,0:T(8,128)(2,1)}, bf16[320,1536]{1,0:T(8,128)(2,1)}, u32[]{:S(2)}, u32[]{:S(2)}) collective-permute-start(bf16[320,1536]{1,0:T(8,128)(2,1)} %collective-permute-done.42.refs_2_.refs_0_), channel_id=1, source_target_pairs={{0,2},{2,0},{4,6},{6,4},{8,10},{10,8},{12,14},{14,12},{16,18},{18,... | collective-permute-start | bytes 2949128 | tf_op jit(solution)/shard_map/ppermute | solution.py:29
  252.0 24.3 %collective-permute-start.49 = (bf16[4,96,1152]{2,1,0:T(8,128)(2,1)S(1)}, bf16[4,96,1152]{2,1,0:T(8,128)(2,1)}, u32[]{:S(2)}, u32[]{:S(2)}) collective-permute-start(bf16[4,96,1152]{2,1,0:T(8,128)(2,1)S(1)} %copy-done.9), channel_id=1, source_target_pairs={{0,4},{2,6},{4,0},{6,2},{8,12},{10,14},{12,8},{14,10},{16,20},{18,... | collective-permute-start | bytes 2654216 | tf_op jit(solution)/shard_map/ppermute | solution.py:29
  253.8 22.5 %collective-permute-start.48 = (bf16[2,96,1152]{2,1,0:T(8,128)(2,1)}, bf16[2,96,1152]{2,1,0:T(8,128)(2,1)}, u32[]{:S(2)}, u32[]{:S(2)}) collective-permute-start(bf16[2,96,1152]{2,1,0:T(8,128)(2,1)} %slice.340), channel_id=1, source_target_pairs={{0,16},{2,18},{4,20},{6,22},{8,24},{10,26},{12,28},{14,30},{16,0},... | collective-permute-start | bytes 1327112 | tf_op jit(solution)/shard_map/ppermute | solution.py:29
  279.2 24.4 %collective-permute-start.52 = (bf16[320,1536]{1,0:T(8,128)(2,1)S(1)}, bf16[320,1536]{1,0:T(8,128)(2,1)S(1)}, u32[]{:S(2)}, u32[]{:S(2)}) collective-permute-start(bf16[320,1536]{1,0:T(8,128)(2,1)S(1)} %copy-done.17), channel_id=1, source_target_pairs={{0,2},{2,0},{4,6},{6,4},{8,10},{10,8},{12,14},{14,12},{16,18},{18,... | collective-permute-start | bytes 2949128 | tf_op jit(solution)/shard_map/ppermute | solution.py:29
  281.7 21.9 %collective-permute-start.51 = (bf16[4,96,1152]{2,1,0:T(8,128)(2,1)}, bf16[4,96,1152]{2,1,0:T(8,128)(2,1)S(1)}, u32[]{:S(2)}, u32[]{:S(2)}) collective-permute-start(bf16[4,96,1152]{2,1,0:T(8,128)(2,1)} %pad_maximum_fusion.14), channel_id=1, source_target_pairs={{0,4},{2,6},{4,0},{6,2},{8,12},{10,14},{12,8},{14,10},{16,20},{18,... | collective-permute-start | bytes 2654216 | tf_op jit(solution)/shard_map/ppermute | solution.py:29
  303.6 25.2 %collective-permute-start.53 = (bf16[4,96,1152]{2,1,0:T(8,128)(2,1)}, bf16[4,96,1152]{2,1,0:T(8,128)(2,1)S(1)}, u32[]{:S(2)}, u32[]{:S(2)}) collective-permute-start(bf16[4,96,1152]{2,1,0:T(8,128)(2,1)} %get-tuple-element.579), channel_id=1, source_target_pairs={{0,4},{2,6},{4,0},{6,2},{8,12},{10,14},{12,8},{14,10},{16,20},{18,... | collective-permute-start | bytes 2654216 | tf_op jit(solution)/shard_map/ppermute | solution.py:29
  328.8 26.2 %collective-permute-start.54 = (bf16[640,1536]{1,0:T(8,128)(2,1)}, bf16[640,1536]{1,0:T(8,128)(2,1)}, u32[]{:S(2)}, u32[]{:S(2)}) collective-permute-start(bf16[640,1536]{1,0:T(8,128)(2,1)} %get-tuple-element.595), channel_id=1, source_target_pairs={{0,2},{2,0},{4,6},{6,4},{8,10},{10,8},{12,14},{14,12},{16,18},{18,... | collective-permute-start | bytes 5898248 | tf_op jit(solution)/shard_map/ppermute | solution.py:29
  329.8 25.3 %collective-permute-start.55 = (bf16[4,96,1152]{2,1,0:T(8,128)(2,1)}, bf16[4,96,1152]{2,1,0:T(8,128)(2,1)S(1)}, u32[]{:S(2)}, u32[]{:S(2)}) collective-permute-start(bf16[4,96,1152]{2,1,0:T(8,128)(2,1)} %get-tuple-element.596), channel_id=1, source_target_pairs={{0,4},{2,6},{4,0},{6,2},{8,12},{10,14},{12,8},{14,10},{16,20},{18,... | collective-permute-start | bytes 2654216 | tf_op jit(solution)/shard_map/ppermute | solution.py:29
  332.9 22.2 %collective-permute-start.56 = (bf16[2,96,1152]{2,1,0:T(8,128)(2,1)}, bf16[2,96,1152]{2,1,0:T(8,128)(2,1)}, u32[]{:S(2)}, u32[]{:S(2)}) collective-permute-start(bf16[2,96,1152]{2,1,0:T(8,128)(2,1)} %slice.424), channel_id=1, source_target_pairs={{0,16},{2,18},{4,20},{6,22},{8,24},{10,26},{12,28},{14,30},{16,0},... | collective-permute-start | bytes 1327112 | tf_op jit(solution)/shard_map/ppermute | solution.py:29
  355.1 28.5 %collective-permute-start.58 = (bf16[1280,1536]{1,0:T(8,128)(2,1)}, bf16[1280,1536]{1,0:T(8,128)(2,1)}, u32[]{:S(2)}, u32[]{:S(2)}) collective-permute-start(bf16[1280,1536]{1,0:T(8,128)(2,1)} %get-tuple-element.612), channel_id=1, source_target_pairs={{0,2},{2,0},{4,6},{6,4},{8,10},{10,8},{12,14},{14,12},{16,18},{18,... | collective-permute-start | bytes 11796488 | tf_op jit(solution)/shard_map/ppermute | solution.py:29
  358.7 24.8 %collective-permute-start.57 = (bf16[640,1536]{1,0:T(8,128)(2,1)}, bf16[640,1536]{1,0:T(8,128)(2,1)S(1)}, u32[]{:S(2)}, u32[]{:S(2)}) collective-permute-start(bf16[640,1536]{1,0:T(8,128)(2,1)} %add_convert_fusion.1), channel_id=1, source_target_pairs={{0,8},{1,9},{2,3},{3,2},{4,12},{5,13},{6,7},{7,6},{8,0},{9,1},{10,... | collective-permute-start | bytes 5898248 | tf_op jit(solution)/shard_map/ppermute | solution.py:40
  383.5 24.2 %collective-permute-start.59 = (bf16[640,1536]{1,0:T(8,128)(2,1)}, bf16[640,1536]{1,0:T(8,128)(2,1)}, u32[]{:S(2)}, u32[]{:S(2)}) collective-permute-start(bf16[640,1536]{1,0:T(8,128)(2,1)} %get-tuple-element.614), channel_id=1, source_target_pairs={{0,2},{2,0},{4,6},{6,4},{8,10},{10,8},{12,14},{14,12},{16,18},{18,... | collective-permute-start | bytes 5898248 | tf_op jit(solution)/shard_map/ppermute | solution.py:29
  384.5 23.2 %collective-permute-start.60 = (bf16[2,96,1152]{2,1,0:T(8,128)(2,1)}, bf16[2,96,1152]{2,1,0:T(8,128)(2,1)}, u32[]{:S(2)}, u32[]{:S(2)}) collective-permute-start(bf16[2,96,1152]{2,1,0:T(8,128)(2,1)} %slice.342), channel_id=1, source_target_pairs={{0,16},{2,18},{4,20},{6,22},{8,24},{10,26},{12,28},{14,30},{16,0},... | collective-permute-start | bytes 1327112 | tf_op jit(solution)/shard_map/ppermute | solution.py:29
  410.3 22.0 %collective-permute-start.61 = (bf16[320,1536]{1,0:T(8,128)(2,1)}, bf16[320,1536]{1,0:T(8,128)(2,1)S(1)}, u32[]{:S(2)}, u32[]{:S(2)}) collective-permute-start(bf16[320,1536]{1,0:T(8,128)(2,1)} %add_convert_fusion.4), channel_id=1, source_target_pairs={{0,1},{1,0},{2,10},{3,11},{4,5},{5,4},{6,14},{7,15},{8,9},{9,8},{1... | collective-permute-start | bytes 2949128 | tf_op jit(solution)/shard_map/ppermute | solution.py:40
  474.2 23.1 %collective-permute-start.70 = (bf16[320,1536]{1,0:T(8,128)(2,1)}, bf16[320,1536]{1,0:T(8,128)(2,1)S(1)}, u32[]{:S(2)}, u32[]{:S(2)}) collective-permute-start(bf16[320,1536]{1,0:T(8,128)(2,1)} %slice.355), channel_id=1, source_target_pairs={{0,8},{1,9},{2,3},{3,2},{4,12},{5,13},{6,7},{7,6},{8,0},{9,1},{10,... | collective-permute-start | bytes 2949128 | tf_op jit(solution)/shard_map/ppermute | solution.py:40
  500.1 25.9 %collective-permute-start.75 = (bf16[2,2,2,96,768]{4,3,2,1,0:T(8,128)(2,1)}, bf16[2,2,2,96,768]{4,3,2,1,0:T(8,128)(2,1)S(1)}, u32[]{:S(2)}, u32[]{:S(2)}) collective-permute-start(bf16[2,2,2,96,768]{4,3,2,1,0:T(8,128)(2,1)} %get-tuple-element.719), channel_id=1, source_target_pairs={{0,4},{1,5},{2,10},{3,11},{4,0},{5,1},{6,14},{7,15},{8,12},{9,13},... | collective-permute-start | bytes 3538952 | tf_op jit(solution)/shard_map/ppermute | solution.py:40
  503.1 22.9 %collective-permute-start.77 = (bf16[2,96,1152]{2,1,0:T(8,128)(2,1)S(1)}, bf16[2,96,1152]{2,1,0:T(8,128)(2,1)S(1)}, u32[]{:S(2)}, u32[]{:S(2)}) collective-permute-start(bf16[2,96,1152]{2,1,0:T(8,128)(2,1)S(1)} %slice.360), channel_id=1, source_target_pairs={{0,4},{2,6},{4,0},{6,2},{8,12},{10,14},{12,8},{14,10},{16,20},{18,... | collective-permute-start | bytes 1327112 | tf_op jit(solution)/shard_map/ppermute | solution.py:29
  555.0 29.0 %collective-permute-start.82 = (bf16[2,2,2,96,1024]{4,3,2,1,0:T(8,128)(2,1)}, bf16[2,2,2,96,1024]{4,3,2,1,0:T(8,128)(2,1)}, u32[]{:S(2)}, u32[]{:S(2)}) collective-permute-start(bf16[2,2,2,96,1024]{4,3,2,1,0:T(8,128)(2,1)} %get-tuple-element.764), channel_id=1, source_target_pairs={{0,1},{1,0},{2,6},{3,7},{4,5},{5,4},{6,2},{7,3},{8,9},{9,8},{10,14... | collective-permute-start | bytes 4718600 | tf_op jit(solution)/shard_map/ppermute | solution.py:40
  557.6 21.2 %collective-permute-start.85 = (bf16[2,96,768]{2,1,0:T(8,128)(2,1)}, bf16[2,96,768]{2,1,0:T(8,128)(2,1)}, u32[]{:S(2)}, u32[]{:S(2)}) collective-permute-start(bf16[2,96,768]{2,1,0:T(8,128)(2,1)} %fusion.17), channel_id=1, source_target_pairs={{0,1},{1,0},{2,6},{3,7},{4,5},{5,4},{6,2},{7,3},{8,9},{9,8},{10,14... | collective-permute-start | bytes 884744 | tf_op jit(solution)/shard_map/ppermute | solution.py:40
  562.6 21.3 %collective-permute-start.83 = (bf16[2,96,1152]{2,1,0:T(8,128)(2,1)}, bf16[2,96,1152]{2,1,0:T(8,128)(2,1)}, u32[]{:S(2)}, u32[]{:S(2)}) collective-permute-start(bf16[2,96,1152]{2,1,0:T(8,128)(2,1)} %slice.368), channel_id=1, source_target_pairs={{0,16},{2,18},{4,20},{6,22},{8,24},{10,26},{12,28},{14,30},{16,0},... | collective-permute-start | bytes 1327112 | tf_op jit(solution)/shard_map/ppermute | solution.py:29
  (165 other events, 1864.1 us)

commit v4 on v3

--- a/solution.py
+++ b/solution.py
@@ -691,10 +691,9 @@
 
 def pick_piece(step, refs, pieces):
     block, start = refs[0][...], 0
-    for ref, piece in list(zip(refs, pieces))[1:]:
-        start += piece.shape[0] // STEP
-        block = jnp.where(step < start, block, ref[...])
-        start = start
+    for i in range(1, len(pieces)):
+        start += pieces[i - 1].shape[0] // STEP
+        block = jnp.where(step < start, block, refs[i][...])
     return block
 
 
@@ -727,12 +726,12 @@
     )
 
 
-def gated_back(pieces, slope, silu, first, w_gate_up, w_down, owned):
+def gated_back(pieces, slope, silu, first, w_gate_up, w_down, owners):
     specs, steps = piece_specs(pieces)
     depth, columns = w_down[2]
     part = pl.BlockSpec((STEP, 2 * columns), lambda i: (i, 0))
     later = pl.BlockSpec((STEP, columns), lambda i: (i + first // STEP, 0))
-    sides = [shaped((sum(piece.shape[0] for piece in group), depth)) for group in (pieces[:owned], pieces[owned:])]
+    sides, side_specs, store = owner_sides(pieces, owners, depth)
 
     def kernel(step, ins, targets, outs, ready):
         ready(0)
@@ -740,64 +739,59 @@
         outs[0][:, :columns] = slim(act * wide(ins[-2][...]))
         outs[0][:, columns:] = slim(act * wide(ins[-1][...]))
         ready(1)
-        store_piece(step, outs[1:], sides, slim(dot_last(outs[0][...], targets[1][...])))
+        store(step, outs[1:], slim(dot_last(outs[0][...], targets[1][...])))
 
     return run_kernel(
         kernel, steps, pieces + [slope, silu], specs + [later, later], [w_down, w_gate_up],
-        [shaped((steps * STEP, 2 * columns))] + sides, [part] + piece_specs(sides)[0],
+        [shaped((steps * STEP, 2 * columns))] + sides, [part] + side_specs,
         6 * steps * STEP * depth * columns, True,
     )
 
 
-def store_piece(step, refs, pieces, value):
-    start = 0
-    for ref, piece in zip(refs, pieces):
-        end = start + piece.shape[0] // STEP
-
-        @pl.when((step >= start) & (step < end))
-        def _(ref=ref):
-            ref[...] = value
-
-        start = end
-
-
-def down_rows(acts, w_down, pieces):
-    specs, steps = piece_specs(acts)
-    depth, columns = w_down[2]
-    owner, starts, place = [], [0, 0], 0
-    for number, piece in enumerate(pieces):
-        owner += [number % 2] * (piece.shape[0] // STEP)
-    index = [owner[:i].count(owner[i]) for i in range(steps)]
-    outs = [shaped((owner.count(side) * STEP, depth)) for side in range(2)]
-
-    def kernel(step, ins, targets, results):
-        block = pick_piece(step, ins, acts)
-        value = slim(dot_last(block, targets[0][...]))
-        mine = step >= steps
-        for i in range(steps):
-            if owner[i] == 0:
-                mine = mine | (step == i)
-
-        @pl.when(mine)
-        def _():
-            results[0][...] = value
-
-        @pl.when(jnp.logical_not(mine))
-        def _():
-            results[1][...] = value
+def owner_sides(pieces, owners, depth):
+    owner = []
+    for piece, one in zip(pieces, owners):
+        owner += [one] * (piece.shape[0] // STEP)
+    index = [owner[:i].count(owner[i]) for i in range(len(owner))]
 
     def spec(side):
         def place_of(i):
             reached = 0
-            for k in range(steps):
+            for k in range(len(owner)):
                 if owner[k] == side and index[k] > 0:
                     reached = jnp.where(i >= k, index[k], reached)
             return (reached, 0)
 
         return pl.BlockSpec((STEP, depth), place_of)
 
+    def store(step, refs, value):
+        mine = step >= len(owner)
+        for i in range(len(owner)):
+            if owner[i] == 0:
+                mine = mine | (step == i)
+
+        @pl.when(mine)
+        def _():
+            refs[0][...] = value
+
+        @pl.when(jnp.logical_not(mine))
+        def _():
+            refs[1][...] = value
+
+    shapes = [shaped((owner.count(side) * STEP, depth)) for side in range(2)]
+    return shapes, [spec(0), spec(1)], store
+
+
+def down_rows(act, w_down, pieces):
+    steps = act.shape[0] // STEP
+    depth, columns = w_down[2]
+    outs, out_specs, store = owner_sides(pieces, [i % 2 for i in range(len(pieces))], depth)
+
+    def kernel(step, ins, targets, results):
+        store(step, results, slim(dot_last(ins[0][...], targets[0][...])))
+
     return run_kernel(
-        kernel, steps, acts, specs, [w_down], outs, [spec(0), spec(1)],
+        kernel, steps, [act], [pl.BlockSpec((STEP, columns), lambda i: (i, 0))], [w_down], outs, out_specs,
         2 * steps * STEP * depth * columns,
     )
 
@@ -818,13 +812,16 @@
     def wrapped(place_ref, *refs):
         ins, refs = refs[: len(lefts) + len(rights)], refs[len(lefts) + len(rights) :]
         step = pl.program_id(0)
-        total, number, row = None, len(lefts), 0
+        gathered, refs = refs[-1], refs[:-1]
+        row = 0
         for ref, left in zip(ins, lefts):
-            part = dot_first(ref[...], ins[number][row : row + left.shape[0], :])
+            gathered[row : row + left.shape[0], :] = ref[...]
+            row += left.shape[0]
+        total, row = None, 0
+        for ref, right in zip(ins[len(lefts) :], rights):
+            part = dot_first(gathered[row : row + right.shape[0], :], ref[...])
             total = part if total is None else total + part
-            row += left.shape[0]
-            if row == rights[number - len(lefts)].shape[0]:
-                number, row = number + 1, 0
+            row += right.shape[0]
         if not direct:
             refs[0][...] = slim(total)
             return
@@ -863,6 +860,7 @@
     else:
         outs = [shaped((depth, columns))]
         out_specs = [pl.BlockSpec((tile, columns), lambda i: (i, 0))]
+    scratch.append(pltpu.VMEM((total_rows, tile), jnp.bfloat16))
     results = pl.pallas_call(
         wrapped,
         out_shape=outs,
@@ -1160,9 +1158,9 @@
     normed_first = spread_first(normed_two)
     piece_up = far_units(quads[1], 2, 4)
     all_gate += side_units(far_gate[2:] + part_of(own_up, 0, 1))
-    grad_first = jnp.concatenate([out_grad, grad_got])
-    normed_first, piece_up, all_gate, quads, far_up, normed_one, grad_first = tie(
-        normed_first, piece_up, all_gate, quads, far_up, normed_one, grad_first
+    grad_core = [swap(out_grad, "fsdp", CORE)]
+    normed_first, piece_up, all_gate, quads, far_up, normed_one, grad_got, grad_core = tie(
+        normed_first, piece_up, all_gate, quads, far_up, normed_one, grad_got, grad_core
     )
     far_up += piece_up
 
@@ -1174,33 +1172,36 @@
     gate_weights = unit_bundle(own_gate + far_gate + all_gate[:3] + [pick_units(all_gate[3], 0, 2)])
     normed_pieces = [[normed_first, normed_core[0]], None]
     gates = [gated(normed_pieces[0], gate_weights)[0]]
-    normed_second, all_up, normed_got, gates, quads, far_up, grad_first, mixed = tie(
-        normed_second, all_up, normed_got, gates, quads, far_up, grad_first, mixed
+    normed_second, all_up, normed_got, gates, quads, far_up, grad_got, mixed = tie(
+        normed_second, all_up, normed_got, gates, quads, far_up, grad_got, mixed
     )
 
     normed_pieces[1] = [normed_second, swap(normed_second, "fsdp", CORE)]
-    normed_pieces, grad_first, far_up, quads = tie(normed_pieces, grad_first, far_up, quads)
-    grad_second = [spread_second(grad_first[:rows])]
+    normed_pieces, grad_got, far_up, quads, out_grad = tie(
+        normed_pieces, grad_got, far_up, quads, out_grad
+    )
+    grad_second = [swap_both(out_grad, Z, X)]
+    grad_core.append(swap(grad_got, "fsdp", CORE))
     far_down = far_units(quads[2], 0, 2)
     all_up += side_units(far_up[1:])
     gates += gated(normed_pieces[1], gate_weights)
-    grad_first, grad_second, far_down, all_up, gates, quads, mixed = tie(
-        grad_first, grad_second, far_down, all_up, gates, quads, mixed
-    )
-
-    grad_core = [swap(grad_first, "fsdp", CORE), swap(grad_second[0], "fsdp", CORE)]
-    grad_second.append(spread_second(grad_first[rows:]))
+    grad_got, grad_core, grad_second, far_down, all_up, gates, quads, mixed = tie(
+        grad_got, grad_core, grad_second, far_down, all_up, gates, quads, mixed
+    )
+
+    grad_core.append(swap(grad_second[0], "fsdp", CORE))
+    grad_second.append(swap_both(grad_got, Z, X))
     piece_down = far_units(quads[2], 2, 4)
     all_down = side_units(own_down)
     up_weights = unit_bundle(own_up + far_up + [pick_units(all_gate[3], 2, 3)] + all_up)
     slope, silu, act = gated(normed_pieces[0] + normed_pieces[1], up_weights, gates)
-    act, grad_second, grad_core, piece_down, all_down, far_down, grad_first, quads, mixed = tie(
-        act, grad_second, grad_core, piece_down, all_down, far_down, grad_first, quads, mixed
+    act, grad_second, grad_core, piece_down, all_down, far_down, quads, mixed = tie(
+        act, grad_second, grad_core, piece_down, all_down, far_down, quads, mixed
     )
     far_down += piece_down
     grad_core.append(swap(grad_second[1], "fsdp", CORE))
     grad_core, far_down, act, quads, mixed = tie(grad_core, far_down, act, quads, mixed)
-    grad_pieces = [[grad_first, grad_core[0]], grad_second + grad_core[1:]]
+    grad_pieces = [[out_grad, grad_got] + grad_core[:2], grad_second + grad_core[2:]]
 
     all_down += side_units(far_down)
     mixed_got = swap(mixed, "fsdp", CORE)
@@ -1215,7 +1216,7 @@
     down_got = {rel: swap(grad_down[rel | SIDE], "fsdp", SIDE) for rel in far_codes}
     both_weights = side_by_side(gate_weights, up_weights)
     grad_both_1, part_1, core_1 = gated_back(
-        grad_pieces[1], slope, silu, 4 * rows, both_weights, down_weights, 2
+        grad_pieces[1], slope, silu, 4 * rows, both_weights, down_weights, [0, 0, 1, 1]
     )
     down_got, part_1, core_1, act, grad_down = tie(down_got, part_1, core_1, act, grad_down)
 
@@ -1223,7 +1224,7 @@
     down_out = {rel: add_pair(grad_down[rel], got) for rel, got in down_got.items()}
     down_sum = [far_sums({rel: piece[:2] for rel, piece in down_out.items()})]
     down_got = swap(grad_down[SIDE], "fsdp", SIDE)
-    out_own, out_other = down_rows([act], down_weights, normed_pieces[0] + normed_pieces[1])
+    out_own, out_other = down_rows(act, down_weights, normed_pieces[0] + normed_pieces[1])
     core_1, down_got, out_own, out_other, part_1, grad_pieces, down_sum, down_out = tie(
         core_1, down_got, out_own, out_other, part_1, grad_pieces, down_sum, down_out
     )
@@ -1231,7 +1232,7 @@
     got_1 = swap_both(add_pair(part_1, core_1), Z, X)
     out_core = swap(out_other, "fsdp", CORE)
     grad_both_0, part_0, core_0 = gated_back(
-        grad_pieces[0], slope, silu, 0, both_weights, down_weights, 1
+        grad_pieces[0], slope, silu, 0, both_weights, down_weights, [0, 0, 1, 1]
     )
     part_0, core_0, got_1, down_out, out_core, out_own, normed_sent = tie(
         part_0, core_0, got_1, down_out, out_core, out_own, normed_pieces
@@ -1294,11 +1295,10 @@
     query_got, grad_query, out_piece, grad_up = tie(query_got, grad_query, out_piece, grad_up)
     out_pair = split_step(*out_piece, 0, True)
     up_sum = [far_sums({rel: piece[:1] for rel, piece in up_out.items()})]
-    up_got = [swap(grad_up[SIDE][:2], "fsdp", SIDE)]
     size = w_qkv.shape[1]
     parts = joint_grad([normed_one, normed_got], [grad_query, query_got], size, 0)
-    parts, other, out_pair, up_sum, up_got, up_out, grad_up, out_got = tie(
-        parts, other, out_pair, up_sum, up_got, up_out, grad_up, out_got
+    parts, other, out_pair, up_sum, up_out, grad_up, out_got = tie(
+        parts, other, out_pair, up_sum, up_out, grad_up, out_got
     )
 
     grad_kv, query_sums, kv_sums = finish_keys(
@@ -1315,7 +1315,8 @@
     kv_got, out_pair, out_sent, grad_up, up_out = tie(kv_got, out_pair, out_sent, grad_up, up_out)
     out_pair = split_step(*out_pair, 1, True)
     out_got = swap_both(out_sent, X, Z)
-    up_got.append(swap(grad_up[SIDE][2:], "fsdp", SIDE))
+    up_got = [swap(grad_up[SIDE], "fsdp", SIDE)]
+    up_sum.append(far_sums({rel: piece[1:3] for rel, piece in up_out.items()}))
     gate_sum = add_pair(wide(grad_gate[0]) + wide(gate_got), jnp.concatenate(gate_sum))
     kv_got, grad_kv, gate_sum = tie(kv_got, grad_kv, gate_sum)
     parts = joint_grad([normed_one, normed_got], [grad_kv, kv_got], size, query_end, parts)
@@ -1325,9 +1326,8 @@
 
     parts, grad_hidden = tie(parts, grad_hidden)
     pair = split_step(*parts, 0)
-    up_sum.append(far_sums({rel: piece[1:3] for rel, piece in up_out.items()}))
+    up_sum.append(far_sums({rel: piece[3:] for rel, piece in up_out.items()}))
     gate_share = share_near(gate_sum)
-    out_pair = split_step(*split_next(*out_pair, 1), 2, True)
     grad_inputs, grad_gain_one = project_back(
         grad_query, grad_kv, tokens, grad_hidden, gain_one, query_weights, kv_weights
     )
@@ -1348,17 +1348,16 @@
     )
 
     pair = split_step(*split_next(*pair, 0), 1)
-    up_sum.append(far_sums({rel: piece[3:] for rel, piece in up_out.items()}))
     up_home = wide(grad_up[0]) + wide(jnp.concatenate(up_got))
-    out_total = split_next(*out_pair, 2)
+    out_pair = split_step(*split_next(*out_pair, 1), 2, True)
     small = small_step(small, "tp", [1])
-    pair, up_sum, small, out_total = tie(pair, up_sum, small, out_total)
+    pair, up_sum, small, out_pair = tie(pair, up_sum, small, out_pair)
     up_sum = add_pair(up_home, jnp.concatenate(up_sum))
 
     pair = split_step(*split_next(*pair, 1), 2)
     small = small_step(small, "fsdp", far_bits() + [NEAR])
     up_share = share_near(up_sum)
-    out_total = far_totals(out_total)
+    out_total = far_totals(split_next(*out_pair, 2))
     pair, small, up_share, out_total = tie(pair, small, up_share, out_total)
 
     qkv_total = far_totals(split_next(*pair, 2))

time: 653 us -> 650 us (level)
  starting transfers between devices: 96.5 us -> 106 us
  other arithmetic: 64.6 us -> 57.1 us
    ppermute x81, starting transfers between devices: 75.3 us -> 84.3 us  [swap(): return lax.ppermute(values, axis, [(i, i ^ bit) for i in range(count)])]
    ppermute x19, waiting for transfers between devices: 30.9 us -> 38.3 us  [swap_both(): return lax.ppermute(values, ('fsdp', 'tp'), pairs)]
  transfers between devices with their start and end apart: 100 -> 100, of which waited for: 48 -> 48; matrix products, arithmetic and copies ran while one was open for 12% -> 10% of each run, Pallas kernels for 40% -> 39%
where the time goes in v4:
time: 650 us; the launch traced here: 641 us
  Pallas kernels  254 us (39%)
  waiting for transfers between devices  183 us (28%)
  starting transfers between devices  106 us (16%)
  other arithmetic  57.1 us (9%)
  local copies, waits for them, and re-layouts  38.1 us (6%)
    pallas_call x14, Pallas kernels, run_kernel(): pl.pallas_call(wrapped, out_shape=outs, grid=(steps,), in_specs=[pl.Block...  177 us
    ppermute x81, waiting for transfers between devices, swap(): return lax.ppermute(values, axis, [(i, i ^ bit) for i in range(count)])  145 us
    ppermute x81, starting transfers between devices, swap(): return lax.ppermute(values, axis, [(i, i ^ bit) for i in range(count)])  84.3 us
    pallas_call x3, Pallas kernels, weight_grad(): pl.pallas_call(wrapped, out_shape=outs, grid=(steps,), in_specs=[pl.Block...  50.9 us
    ppermute x19, waiting for transfers between devices, swap_both(): return lax.ppermute(values, ('fsdp', 'tp'), pairs)  38.3 us
    convert_element_type x21, other arithmetic, slim(): return values.astype(jnp.bfloat16)  30.1 us
    pallas_call x3, Pallas kernels, joint_grad(): pl.pallas_call(wrapped, out_shape=[shaped(shape)] * 2 if direct else [sha...  23.6 us
    ppermute x19, starting transfers between devices, swap_both(): return lax.ppermute(values, ('fsdp', 'tp'), pairs)  22.1 us
  transfers between devices with their start and end apart: 100, of which 48 were waited for; matrix products, arithmetic and copies ran while one was open for 10% of the time, Pallas kernels for 39%

profile of v4, /device:TPU:0, one launch (start us, length us, event | category | flops | bytes accessed | tf_op | source)
XLA Modules:
  0.0 641.1 jit_solution(4236994322871078730)
XLA Ops:
  19.3 14.1 %collective-permute-done.1 = bf16[2,96,1152]{2,1,0:T(8,128)(2,1)S(1)} collective-permute-done((bf16[2,96,1152]{2,1,0:T(8,128)(2,1)S(1)}, bf16[2,96,1152]{2,1,0:T(8,128)(2,1)S(1)}, u32[]{:S(2)}, u32[]{:S(2)}) %collective-permute-start.1) | collective-permute-done | bytes 442400 | tf_op jit(solution)/shard_map/ppermute | solution.py:29
  48.7 5.9 collective-permute-done.8
  60.6 5.5 collective-permute-done.13
  74.3 7.1 %collective-permute-done.18 = bf16[2,96,768]{2,1,0:T(8,128)(2,1)S(1)} collective-permute-done((bf16[2,96,768]{2,1,0:T(8,128)(2,1)S(1)}, bf16[2,96,768]{2,1,0:T(8,128)(2,1)S(1)}, u32[]{:S(2)}, u32[]{:S(2)}) %collective-permute-start.18) | collective-permute-done | bytes 294944 | tf_op jit(solution)/shard_map/ppermute | solution.py:40
  114.2 7.1 %shard_map.188.refs_0_ = bf16[320,1536]{1,0:T(8,128)(2,1)} custom-call(s32[2]{0:T(128)} %pad_add_fusion.2.place_ref, bf16[320,1536]{1,0:T(8,128)(2,1)} %get-tuple-element.522.refs_0_, f32[2,768]{1,0:T(2,128)} %slice.401.refs_1_, f32[320,128]{1,0:T(8,128)} %get-tuple-element.454.refs_3_.refs_2_.refs_5_.refs_4_, ...), custom_call_target="tpu_custom_call" | custom-call | flops 23592960 | bytes 146528 | tf_op jit(solution)/shard_map/pallas_call | solution.py:212
  132.6 10.2 %shard_map.189.refs_0_.refs_2_ = bf16[320,1536]{1,0:T(8,128)(2,1)} custom-call(s32[2]{0:T(128)} %pad_add_fusion.2.place_ref, bf16[320,1536]{1,0:T(8,128)(2,1)} %shard_map.188.refs_0_, bf16[640,512]{1,0:T(8,128)(2,1)} %copy-done.12, bf16[640,512]{1,0:T(8,128)(2,1)} %copy-done.12, f32[320,640]{1,0:T(8,128)} %and_select_fusion.refs_3_), custom_call_target="tpu_custom_call" | custom-call | flops 19660800 | bytes 64000 | tf_op jit(solution)/shard_map/pallas_call | solution.py:212
  152.2 7.6 %shard_map.190 = (f32[320,1536]{1,0:T(8,128)}, bf16[320,1536]{1,0:T(8,128)(2,1)}) custom-call(s32[2]{0:T(128)} %pad_add_fusion.2.place_ref, bf16[320,1536]{1,0:T(8,128)(2,1)} %shard_map.189.refs_0_.refs_2_, bf16[320,1536]{1,0:T(8,128)(2,1)} %refs_2_.1, f32[1,1536]{1,0:T(1,128)} %reshape_squeeze.7.refs_2_.refs_6_, bf16[8,96,768]{2,1,0:T(8,128)(2,1)} %copy-done.19, ...), custom_call_target="tpu_custom_call" | custom-call | flops 23592960 | bytes 150624 | tf_op jit(solution)/shard_map/pallas_call | solution.py:212
  161.4 5.2 collective-permute-done.32.refs_9_.refs_18_
  171.1 9.8 %collective-permute-done.34 = bf16[320,1536]{1,0:T(8,128)(2,1)S(1)} collective-permute-done((bf16[320,1536]{1,0:T(8,128)(2,1)}, bf16[320,1536]{1,0:T(8,128)(2,1)S(1)}, u32[]{:S(2)}, u32[]{:S(2)}) %collective-permute-start.34) | collective-permute-done | bytes 983072 | tf_op jit(solution)/shard_map/ppermute | solution.py:40
  181.1 11.5 %collective-permute-done.35.refs_9_.refs_23_ = bf16[2,96,1152]{2,1,0:T(8,128)(2,1)S(1)} collective-permute-done((bf16[2,96,1152]{2,1,0:T(8,128)(2,1)S(1)}, bf16[2,96,1152]{2,1,0:T(8,128)(2,1)S(1)}, u32[]{:S(2)}, u32[]{:S(2)}) %collective-permute-start.35) | collective-permute-done | bytes 442400 | tf_op jit(solution)/shard_map/ppermute | solution.py:29
  196.8 10.6 %shard_map.191.refs_4_ = bf16[1280,1152]{1,0:T(8,128)(2,1)} custom-call(s32[2]{0:T(128)} %pad_add_fusion.2.place_ref, bf16[640,1536]{1,0:T(8,128)(2,1)} %copy-done, bf16[640,1536]{1,0:T(8,128)(2,1)} %collective-permute-done.41.refs_1_, bf16[4,96,1152]{2,1,0:T(8,128)(2,1)} %copy-done.1, bf16[1,96,1152]{2,1,0:T(8,128)(2,1)} %copy-done.26, ...), custom_call_target="tpu_custom_call" | custom-call | flops 70778880 | bytes 166272 | tf_op jit(solution)/shard_map/pallas_call | solution.py:212
  207.4 9.7 %collective-permute-done.39.refs_11_.refs_25_ = bf16[4,96,1152]{2,1,0:T(8,128)(2,1)} collective-permute-done((bf16[4,96,1152]{2,1,0:T(8,128)(2,1)}, bf16[4,96,1152]{2,1,0:T(8,128)(2,1)}, u32[]{:S(2)}, u32[]{:S(2)}) %collective-permute-start.39) | collective-permute-done | bytes 884768 | tf_op jit(solution)/shard_map/ppermute | solution.py:29
  229.0 10.7 %shard_map.192.refs_5_ = bf16[1280,1152]{1,0:T(8,128)(2,1)} custom-call(s32[2]{0:T(128)} %pad_add_fusion.2.place_ref, bf16[640,1536]{1,0:T(8,128)(2,1)} %collective-permute-done.38.refs_0_.refs_2_, bf16[640,1536]{1,0:T(8,128)(2,1)} %copy-done.4, bf16[4,96,1152]{2,1,0:T(8,128)(2,1)} %copy-done.1, bf16[1,96,1152]{2,1,0:T(8,128)(2,1)} %copy-done.26, ...), custom_call_target="tpu_custom_call" | custom-call | flops 70778880 | bytes 166272 | tf_op jit(solution)/shard_map/pallas_call | solution.py:212
  239.7 9.3 %collective-permute-done.45.refs_7_.refs_2_ = bf16[2,96,1152]{2,1,0:T(8,128)(2,1)S(1)} collective-permute-done((bf16[2,96,1152]{2,1,0:T(8,128)(2,1)}, bf16[2,96,1152]{2,1,0:T(8,128)(2,1)S(1)}, u32[]{:S(2)}, u32[]{:S(2)}) %collective-permute-start.45) | collective-permute-done | bytes 442400 | tf_op jit(solution)/shard_map/ppermute | solution.py:29
  253.8 21.2 %shard_map.193 = (bf16[2560,1152]{1,0:T(8,128)(2,1)}, bf16[2560,1152]{1,0:T(8,128)(2,1)}, bf16[2560,1152]{1,0:T(8,128)(2,1)}) custom-call(s32[2]{0:T(128)} %pad_add_fusion.2.place_ref, bf16[640,1536]{1,0:T(8,128)(2,1)} %copy-done, bf16[640,1536]{1,0:T(8,128)(2,1)} %collective-permute-done.41.refs_1_, ...), custom_call_target="tpu_custom_call" | custom-call | flops 141557760 | bytes 553728 | tf_op jit(solution)/shard_map/pallas_call | solution.py:212
  281.6 17.1 %shard_map.194 = (bf16[4,96,1152]{2,1,0:T(8,128)(2,1)}, bf16[4,96,1152]{2,1,0:T(8,128)(2,1)}, bf16[4,96,1152]{2,1,0:T(8,128)(2,1)}, bf16[4,96,1152]{2,1,0:T(8,128)(2,1)}) custom-call(s32[2]{0:T(128)} %pad_add_fusion.2.place_ref, bf16[320,1536]{1,0:T(8,128)(2,1)} %broadcast_multiply_fusion.refs_0_.refs_5_, bf16[320,1536]{1,0:T(8,128)(2,1)} %collective-permute-done.33.refs_1_, ...), custom_call_target="tpu_custom_call" | custom-call | flops 141557760 | bytes 27648 | tf_op jit(solution)/shard_map/pallas_call | solution.py:864
  303.6 24.1 %shard_map.195 = (bf16[1280,2304]{1,0:T(8,128)(2,1)}, bf16[640,1536]{1,0:T(8,128)(2,1)}, bf16[640,1536]{1,0:T(8,128)(2,1)}) custom-call(s32[2]{0:T(128)} %pad_add_fusion.2.place_ref, bf16[320,1536]{1,0:T(8,128)(2,1)} %collective-permute-done.44.refs_4_.refs_0_, bf16[320,1536]{1,0:T(8,128)(2,1)} %collective-permute-done.47.refs_5_.refs_1_, ...), custom_call_target="tpu_custom_call" | custom-call | flops 212336640 | bytes 575616 | tf_op jit(solution)/shard_map/pallas_call | solution.py:212
  330.0 18.0 %shard_map.196 = (bf16[1280,1536]{1,0:T(8,128)(2,1)}, bf16[1280,1536]{1,0:T(8,128)(2,1)}) custom-call(s32[2]{0:T(128)} %pad_add_fusion.2.place_ref, bf16[2560,1152]{1,0:T(8,128)(2,1)} %get-tuple-element.611.refs_8_.refs_0_, bf16[4,96,1152]{2,1,0:T(8,128)(2,1)} %copy-done.7, bf16[2,96,1152]{2,1,0:T(8,128)(2,1)} %copy-done.20, ...), custom_call_target="tpu_custom_call" | custom-call | flops 141557760 | bytes 270336 | tf_op jit(solution)/shard_map/pallas_call | solution.py:212
  356.0 23.9 %shard_map.197 = (bf16[1280,2304]{1,0:T(8,128)(2,1)}, bf16[640,1536]{1,0:T(8,128)(2,1)}, bf16[640,1536]{1,0:T(8,128)(2,1)}) custom-call(s32[2]{0:T(128)} %pad_add_fusion.2.place_ref, bf16[320,1536]{1,0:T(8,128)(2,1)} %broadcast_multiply_fusion.refs_0_.refs_5_, bf16[320,1536]{1,0:T(8,128)(2,1)} %collective-permute-done.33.refs_1_, ...), custom_call_target="tpu_custom_call" | custom-call | flops 212336640 | bytes 575616 | tf_op jit(solution)/shard_map/pallas_call | solution.py:212
  383.1 17.0 %shard_map.198 = (bf16[4,96,1152]{2,1,0:T(8,128)(2,1)}, bf16[4,96,1152]{2,1,0:T(8,128)(2,1)}, bf16[4,96,1152]{2,1,0:T(8,128)(2,1)}, bf16[4,96,1152]{2,1,0:T(8,128)(2,1)}) custom-call(s32[2]{0:T(128)} %pad_add_fusion.2.place_ref, bf16[640,1536]{1,0:T(8,128)(2,1)} %copy-done, bf16[640,1536]{1,0:T(8,128)(2,1)} %collective-permute-done.41.refs_1_, ...), custom_call_target="tpu_custom_call" | custom-call | flops 141557760 | bytes 27648 | tf_op jit(solution)/shard_map/pallas_call | solution.py:864
  400.0 5.1 collective-permute-done.61
  409.7 16.8 %shard_map.199 = (bf16[4,96,1152]{2,1,0:T(8,128)(2,1)}, bf16[4,96,1152]{2,1,0:T(8,128)(2,1)}, bf16[4,96,1152]{2,1,0:T(8,128)(2,1)}, bf16[4,96,1152]{2,1,0:T(8,128)(2,1)}) custom-call(s32[2]{0:T(128)} %pad_add_fusion.2.place_ref, bf16[640,1536]{1,0:T(8,128)(2,1)} %copy-done, bf16[640,1536]{1,0:T(8,128)(2,1)} %collective-permute-done.41.refs_1_, ...), custom_call_target="tpu_custom_call" | custom-call | flops 141557760 | bytes 27648 | tf_op jit(solution)/shard_map/pallas_call | solution.py:864
  434.5 9.6 %shard_map.200 = (f32[320,1536]{1,0:T(8,128)}, f32[1,1536]{1,0:T(1,128)}, bf16[320,1536]{1,0:T(8,128)(2,1)}, bf16[320,1536]{1,0:T(8,128)(2,1)}) custom-call(s32[2]{0:T(128)} %pad_add_fusion.2.place_ref, bf16[640,1536]{1,0:T(8,128)(2,1)} %get-tuple-element.666.refs_0_, bf16[640,1536]{1,0:T(8,128)(2,1)} %collective-permute-done.60.refs_1_, ...), custom_call_target="tpu_custom_call" | custom-call | flops 23592960 | bytes 288960 | tf_op jit(solution)/shard_map/pallas_call | solution.py:212
  457.0 9.0 %shard_map.201 = (bf16[2,2,2,96,768]{4,3,2,1,0:T(8,128)(2,1)}, bf16[2,2,2,96,768]{4,3,2,1,0:T(8,128)(2,1)}) custom-call(s32[2]{0:T(128)} %pad_add_fusion.2.place_ref, bf16[320,1536]{1,0:T(8,128)(2,1)} %get-tuple-element.692.refs_0_, bf16[320,1536]{1,0:T(8,128)(2,1)} %copy-done.57, bf16[320,1536]{1,0:T(8,128)(2,1)} %shard_map.189.refs_0_.refs_2_, ...), custom_call_target="tpu_custom_call" | custom-call | flops 47185920 | tf_op jit(solution)/shard_map/pallas_call | solution.py:977
  477.3 16.4 %shard_map.202 = (bf16[320,1536]{1,0:T(8,128)(2,1)}, f32[640,256]{1,0:T(8,128)}, f32[640,256]{1,0:T(8,128)}) custom-call(s32[2]{0:T(128)} %pad_add_fusion.2.place_ref, bf16[320,1536]{1,0:T(8,128)(2,1)} %shard_map.188.refs_0_, bf16[640,512]{1,0:T(8,128)(2,1)} %copy-done.12, bf16[640,512]{1,0:T(8,128)(2,1)} %copy-done.12, f32[320,640]{1,0:T(8,128)} %and_select_fusion.refs_3_, ...), custom_call_target="tpu_custom_call" | custom-call | flops 49152000 | bytes 104960 | tf_op jit(solution)/shard_map/pallas_call | solution.py:212
  505.2 9.0 %shard_map.203 = (bf16[2,2,2,96,1024]{4,3,2,1,0:T(8,128)(2,1)}, bf16[2,2,2,96,1024]{4,3,2,1,0:T(8,128)(2,1)}) custom-call(s32[2]{0:T(128)} %pad_add_fusion.2.place_ref, bf16[320,1536]{1,0:T(8,128)(2,1)} %get-tuple-element.522.refs_0_, bf16[320,1536]{1,0:T(8,128)(2,1)} %collective-permute-done.40.refs_1_, ...), custom_call_target="tpu_custom_call" | custom-call | flops 47185920 | tf_op jit(solution)/shard_map/pallas_call | solution.py:977
  535.3 5.6 shard_map.205
  540.9 14.8 %collective-permute-done.79 = bf16[2,96,1152]{2,1,0:T(8,128)(2,1)} collective-permute-done((bf16[2,96,1152]{2,1,0:T(8,128)(2,1)S(1)}, bf16[2,96,1152]{2,1,0:T(8,128)(2,1)}, u32[]{:S(2)}, u32[]{:S(2)}) %collective-permute-start.79) | collective-permute-done | bytes 442400 | tf_op jit(solution)/shard_map/ppermute | solution.py:29
  567.6 9.9 %shard_map.206 = (f32[320,1536]{1,0:T(8,128)}, f32[1,1536]{1,0:T(1,128)}) custom-call(s32[2]{0:T(128)} %pad_add_fusion.2.place_ref, bf16[320,1536]{1,0:T(8,128)(2,1)} %get-tuple-element.732.refs_2_.refs_3_.refs_0_, bf16[320,512]{1,0:T(8,128)(2,1)} %get-tuple-element.764.refs_2_.refs_1_, bf16[320,1536]{1,0:T(8,128)(2,1)} %refs_2_.1, ...), custom_call_target="tpu_custom_call" | custom-call | flops 23592960 | bytes 318656 | tf_op jit(solution)/shard_map/pallas_call | solution.py:212
  587.9 7.2 %collective-permute-done.86 = bf16[2,2,96,1024]{3,2,1,0:T(8,128)(2,1)S(1)} collective-permute-done((bf16[2,2,96,1024]{3,2,1,0:T(8,128)(2,1)S(1)}, bf16[2,2,96,1024]{3,2,1,0:T(8,128)(2,1)S(1)}, u32[]{:S(2)}, u32[]{:S(2)}) %collective-permute-start.86) | collective-permute-done | bytes 786464 | tf_op jit(solution)/shard_map/ppermute | solution.py:40
  607.6 11.0 %collective-permute-done.89 = bf16[2,96,1024]{2,1,0:T(8,128)(2,1)S(1)} collective-permute-done((bf16[2,96,1024]{2,1,0:T(8,128)(2,1)S(1)}, bf16[2,96,1024]{2,1,0:T(8,128)(2,1)S(1)}, u32[]{:S(2)}, u32[]{:S(2)}) %collective-permute-start.89) | collective-permute-done | bytes 393248 | tf_op jit(solution)/shard_map/ppermute | solution.py:40
  627.0 8.9 %collective-permute-done.98 = bf16[96,1024]{1,0:T(8,128)(2,1)S(1)} collective-permute-done((bf16[96,1024]{1,0:T(8,128)(2,1)S(1)}, bf16[96,1024]{1,0:T(8,128)(2,1)S(1)}, u32[]{:S(2)}, u32[]{:S(2)}) %collective-permute-start.98) | collective-permute-done | bytes 196640 | tf_op jit(solution)/shard_map/ppermute | solution.py:29
  (524 shorter events, 269.5 us)
Async XLA Ops:
  16.8 23.9 %collective-permute-start.6 = (bf16[1,96,1152]{2,1,0:T(8,128)(2,1)S(1)}, bf16[1,96,1152]{2,1,0:T(8,128)(2,1)S(1)}, u32[]{:S(2)}, u32[]{:S(2)}) collective-permute-start(bf16[1,96,1152]{2,1,0:T(8,128)(2,1)S(1)} %get-tuple-element.844), channel_id=1, source_target_pairs={{0,16},{2,18},{4,20},{6,22},{8,24},{10,26},{12,28},{14,30},{16,0},... | collective-permute-start | bytes 663560 | tf_op jit(solution)/shard_map/ppermute | solution.py:29
  168.5 24.1 %collective-permute-start.36 = (bf16[3,96,1152]{2,1,0:T(8,128)(2,1)S(1)}, bf16[3,96,1152]{2,1,0:T(8,128)(2,1)S(1)}, u32[]{:S(2)}, u32[]{:S(2)}) collective-permute-start(bf16[3,96,1152]{2,1,0:T(8,128)(2,1)S(1)} %pad_maximum_fusion.16), channel_id=1, source_target_pairs={{0,4},{2,6},{4,0},{6,2},{8,12},{10,14},{12,8},{14,10},{16,20},{18,... | collective-permute-start | bytes 1990664 | tf_op jit(solution)/shard_map/ppermute | solution.py:29
  169.9 22.7 %collective-permute-start.35 = (bf16[2,96,1152]{2,1,0:T(8,128)(2,1)S(1)}, bf16[2,96,1152]{2,1,0:T(8,128)(2,1)S(1)}, u32[]{:S(2)}, u32[]{:S(2)}) collective-permute-start(bf16[2,96,1152]{2,1,0:T(8,128)(2,1)S(1)} %slice.323), channel_id=1, source_target_pairs={{0,16},{2,18},{4,20},{6,22},{8,24},{10,26},{12,28},{14,30},{16,0},... | collective-permute-start | bytes 1327112 | tf_op jit(solution)/shard_map/ppermute | solution.py:29
  192.7 24.8 %collective-permute-start.38 = (bf16[640,1536]{1,0:T(8,128)(2,1)S(1)}, bf16[640,1536]{1,0:T(8,128)(2,1)}, u32[]{:S(2)}, u32[]{:S(2)}) collective-permute-start(bf16[640,1536]{1,0:T(8,128)(2,1)S(1)} %pad_maximum_fusion.1.refs_0_), channel_id=1, source_target_pairs={{0,8},{1,9},{2,3},{3,2},{4,12},{5,13},{6,7},{7,6},{8,0},{9,1},{10,... | collective-permute-start | bytes 5898248 | tf_op jit(solution)/shard_map/ppermute | solution.py:40
  192.9 24.3 %collective-permute-start.40 = (bf16[320,1536]{1,0:T(8,128)(2,1)}, bf16[320,1536]{1,0:T(8,128)(2,1)}, u32[]{:S(2)}, u32[]{:S(2)}) collective-permute-start(bf16[320,1536]{1,0:T(8,128)(2,1)} %get-tuple-element.522.refs_0_), channel_id=1, source_target_pairs={{0,2},{2,0},{4,6},{6,4},{8,10},{10,8},{12,14},{14,12},{16,18},{18,... | collective-permute-start | bytes 2949128 | tf_op jit(solution)/shard_map/ppermute | solution.py:29
  195.3 21.9 %collective-permute-start.39 = (bf16[4,96,1152]{2,1,0:T(8,128)(2,1)}, bf16[4,96,1152]{2,1,0:T(8,128)(2,1)}, u32[]{:S(2)}, u32[]{:S(2)}) collective-permute-start(bf16[4,96,1152]{2,1,0:T(8,128)(2,1)} %pad_maximum_fusion.12), channel_id=1, source_target_pairs={{0,4},{2,6},{4,0},{6,2},{8,12},{10,14},{12,8},{14,10},{16,20},{18,... | collective-permute-start | bytes 2654216 | tf_op jit(solution)/shard_map/ppermute | solution.py:29
  221.7 27.3 %collective-permute-start.43 = (bf16[320,1536]{1,0:T(8,128)(2,1)}, bf16[320,1536]{1,0:T(8,128)(2,1)}, u32[]{:S(2)}, u32[]{:S(2)}) collective-permute-start(bf16[320,1536]{1,0:T(8,128)(2,1)} %collective-permute-done.33.refs_1_), channel_id=1, source_target_pairs={{0,2},{2,0},{4,6},{6,4},{8,10},{10,8},{12,14},{14,12},{16,18},{18,... | collective-permute-start | bytes 2949128 | tf_op jit(solution)/shard_map/ppermute | solution.py:29
  221.8 27.2 %collective-permute-start.44 = (bf16[320,1536]{1,0:T(8,128)(2,1)}, bf16[320,1536]{1,0:T(8,128)(2,1)}, u32[]{:S(2)}, u32[]{:S(2)}) collective-permute-start(bf16[320,1536]{1,0:T(8,128)(2,1)} %broadcast_multiply_fusion.refs_0_.refs_5_), channel_id=1, source_target_pairs={{0,8},{1,9},{2,3},{3,2},{4,12},{5,13},{6,7},{7,6},{8,0},{9,1},{10,... | collective-permute-start | bytes 2949128 | tf_op jit(solution)/shard_map/ppermute | solution.py:40
  224.5 24.5 %collective-permute-start.46 = (bf16[3,96,1152]{2,1,0:T(8,128)(2,1)}, bf16[3,96,1152]{2,1,0:T(8,128)(2,1)S(1)}, u32[]{:S(2)}, u32[]{:S(2)}) collective-permute-start(bf16[3,96,1152]{2,1,0:T(8,128)(2,1)} %pad_maximum_fusion.17), channel_id=1, source_target_pairs={{0,4},{2,6},{4,0},{6,2},{8,12},{10,14},{12,8},{14,10},{16,20},{18,... | collective-permute-start | bytes 1990664 | tf_op jit(solution)/shard_map/ppermute | solution.py:29
  225.7 23.3 %collective-permute-start.45 = (bf16[2,96,1152]{2,1,0:T(8,128)(2,1)}, bf16[2,96,1152]{2,1,0:T(8,128)(2,1)S(1)}, u32[]{:S(2)}, u32[]{:S(2)}) collective-permute-start(bf16[2,96,1152]{2,1,0:T(8,128)(2,1)} %slice.325), channel_id=1, source_target_pairs={{0,16},{2,18},{4,20},{6,22},{8,24},{10,26},{12,28},{14,30},{16,0},... | collective-permute-start | bytes 1327112 | tf_op jit(solution)/shard_map/ppermute | solution.py:29
  249.0 26.1 %collective-permute-start.47 = (bf16[320,1536]{1,0:T(8,128)(2,1)}, bf16[320,1536]{1,0:T(8,128)(2,1)}, u32[]{:S(2)}, u32[]{:S(2)}) collective-permute-start(bf16[320,1536]{1,0:T(8,128)(2,1)} %collective-permute-done.33.refs_1_), channel_id=1, source_target_pairs={{0,8},{1,9},{2,3},{3,2},{4,12},{5,13},{6,7},{7,6},{8,0},{9,1},{10,... | collective-permute-start | bytes 2949128 | tf_op jit(solution)/shard_map/ppermute | solution.py:40
  249.4 25.7 %collective-permute-start.48 = (bf16[320,1536]{1,0:T(8,128)(2,1)}, bf16[320,1536]{1,0:T(8,128)(2,1)}, u32[]{:S(2)}, u32[]{:S(2)}) collective-permute-start(bf16[320,1536]{1,0:T(8,128)(2,1)} %collective-permute-done.44.refs_4_.refs_0_), channel_id=1, source_target_pairs={{0,2},{2,0},{4,6},{6,4},{8,10},{10,8},{12,14},{14,12},{16,18},{18,... | collective-permute-start | bytes 2949128 | tf_op jit(solution)/shard_map/ppermute | solution.py:29
  249.4 25.6 %collective-permute-start.50 = (bf16[4,96,1152]{2,1,0:T(8,128)(2,1)S(1)}, bf16[4,96,1152]{2,1,0:T(8,128)(2,1)S(1)}, u32[]{:S(2)}, u32[]{:S(2)}) collective-permute-start(bf16[4,96,1152]{2,1,0:T(8,128)(2,1)S(1)} %pad_maximum_fusion.11.refs_6_.refs_1_), channel_id=1, source_target_pairs={{0,4},{2,6},{4,0},{6,2},{8,12},{10,14},{12,8},{14,10},{16,20},{18,... | collective-permute-start | bytes 2654216 | tf_op jit(solution)/shard_map/ppermute | solution.py:29
  251.2 23.8 %collective-permute-start.49 = (bf16[2,96,1152]{2,1,0:T(8,128)(2,1)}, bf16[2,96,1152]{2,1,0:T(8,128)(2,1)S(1)}, u32[]{:S(2)}, u32[]{:S(2)}) collective-permute-start(bf16[2,96,1152]{2,1,0:T(8,128)(2,1)} %slice.326), channel_id=1, source_target_pairs={{0,16},{2,18},{4,20},{6,22},{8,24},{10,26},{12,28},{14,30},{16,0},... | collective-permute-start | bytes 1327112 | tf_op jit(solution)/shard_map/ppermute | solution.py:29
  277.9 23.9 %collective-permute-start.53 = (bf16[320,1536]{1,0:T(8,128)(2,1)S(1)}, bf16[320,1536]{1,0:T(8,128)(2,1)}, u32[]{:S(2)}, u32[]{:S(2)}) collective-permute-start(bf16[320,1536]{1,0:T(8,128)(2,1)S(1)} %copy-done.15), channel_id=1, source_target_pairs={{0,2},{2,0},{4,6},{6,4},{8,10},{10,8},{12,14},{14,12},{16,18},{18,... | collective-permute-start | bytes 2949128 | tf_op jit(solution)/shard_map/ppermute | solution.py:29
  279.9 21.9 %collective-permute-start.52 = (bf16[4,96,1152]{2,1,0:T(8,128)(2,1)}, bf16[4,96,1152]{2,1,0:T(8,128)(2,1)S(1)}, u32[]{:S(2)}, u32[]{:S(2)}) collective-permute-start(bf16[4,96,1152]{2,1,0:T(8,128)(2,1)} %pad_maximum_fusion.13), channel_id=1, source_target_pairs={{0,4},{2,6},{4,0},{6,2},{8,12},{10,14},{12,8},{14,10},{16,20},{18,... | collective-permute-start | bytes 2654216 | tf_op jit(solution)/shard_map/ppermute | solution.py:29
  301.8 25.8 %collective-permute-start.54 = (bf16[4,96,1152]{2,1,0:T(8,128)(2,1)}, bf16[4,96,1152]{2,1,0:T(8,128)(2,1)S(1)}, u32[]{:S(2)}, u32[]{:S(2)}) collective-permute-start(bf16[4,96,1152]{2,1,0:T(8,128)(2,1)} %get-tuple-element.593), channel_id=1, source_target_pairs={{0,4},{2,6},{4,0},{6,2},{8,12},{10,14},{12,8},{14,10},{16,20},{18,... | collective-permute-start | bytes 2654216 | tf_op jit(solution)/shard_map/ppermute | solution.py:29
  327.6 24.6 %collective-permute-start.55 = (bf16[640,1536]{1,0:T(8,128)(2,1)}, bf16[640,1536]{1,0:T(8,128)(2,1)}, u32[]{:S(2)}, u32[]{:S(2)}) collective-permute-start(bf16[640,1536]{1,0:T(8,128)(2,1)} %get-tuple-element.609), channel_id=1, source_target_pairs={{0,2},{2,0},{4,6},{6,4},{8,10},{10,8},{12,14},{14,12},{16,18},{18,... | collective-permute-start | bytes 5898248 | tf_op jit(solution)/shard_map/ppermute | solution.py:29
  327.7 24.6 %collective-permute-start.56 = (bf16[4,96,1152]{2,1,0:T(8,128)(2,1)}, bf16[4,96,1152]{2,1,0:T(8,128)(2,1)S(1)}, u32[]{:S(2)}, u32[]{:S(2)}) collective-permute-start(bf16[4,96,1152]{2,1,0:T(8,128)(2,1)} %get-tuple-element.610), channel_id=1, source_target_pairs={{0,4},{2,6},{4,0},{6,2},{8,12},{10,14},{12,8},{14,10},{16,20},{18,... | collective-permute-start | bytes 2654216 | tf_op jit(solution)/shard_map/ppermute | solution.py:29
  329.8 22.5 %collective-permute-start.57 = (bf16[2,96,1152]{2,1,0:T(8,128)(2,1)}, bf16[2,96,1152]{2,1,0:T(8,128)(2,1)}, u32[]{:S(2)}, u32[]{:S(2)}) collective-permute-start(bf16[2,96,1152]{2,1,0:T(8,128)(2,1)} %slice.408), channel_id=1, source_target_pairs={{0,16},{2,18},{4,20},{6,22},{8,24},{10,26},{12,28},{14,30},{16,0},... | collective-permute-start | bytes 1327112 | tf_op jit(solution)/shard_map/ppermute | solution.py:29
  352.3 28.5 %collective-permute-start.59 = (bf16[1280,1536]{1,0:T(8,128)(2,1)}, bf16[1280,1536]{1,0:T(8,128)(2,1)}, u32[]{:S(2)}, u32[]{:S(2)}) collective-permute-start(bf16[1280,1536]{1,0:T(8,128)(2,1)} %get-tuple-element.630), channel_id=1, source_target_pairs={{0,2},{2,0},{4,6},{6,4},{8,10},{10,8},{12,14},{14,12},{16,18},{18,... | collective-permute-start | bytes 11796488 | tf_op jit(solution)/shard_map/ppermute | solution.py:29
  356.0 24.8 %collective-permute-start.58 = (bf16[640,1536]{1,0:T(8,128)(2,1)}, bf16[640,1536]{1,0:T(8,128)(2,1)S(1)}, u32[]{:S(2)}, u32[]{:S(2)}) collective-permute-start(bf16[640,1536]{1,0:T(8,128)(2,1)} %add_convert_fusion.1), channel_id=1, source_target_pairs={{0,8},{1,9},{2,3},{3,2},{4,12},{5,13},{6,7},{7,6},{8,0},{9,1},{10,... | collective-permute-start | bytes 5898248 | tf_op jit(solution)/shard_map/ppermute | solution.py:40
  380.8 24.3 %collective-permute-start.60 = (bf16[640,1536]{1,0:T(8,128)(2,1)}, bf16[640,1536]{1,0:T(8,128)(2,1)}, u32[]{:S(2)}, u32[]{:S(2)}) collective-permute-start(bf16[640,1536]{1,0:T(8,128)(2,1)} %get-tuple-element.632), channel_id=1, source_target_pairs={{0,2},{2,0},{4,6},{6,4},{8,10},{10,8},{12,14},{14,12},{16,18},{18,... | collective-permute-start | bytes 5898248 | tf_op jit(solution)/shard_map/ppermute | solution.py:29
  382.0 23.1 %collective-permute-start.61 = (bf16[2,96,1152]{2,1,0:T(8,128)(2,1)}, bf16[2,96,1152]{2,1,0:T(8,128)(2,1)}, u32[]{:S(2)}, u32[]{:S(2)}) collective-permute-start(bf16[2,96,1152]{2,1,0:T(8,128)(2,1)} %slice.328), channel_id=1, source_target_pairs={{0,16},{2,18},{4,20},{6,22},{8,24},{10,26},{12,28},{14,30},{16,0},... | collective-permute-start | bytes 1327112 | tf_op jit(solution)/shard_map/ppermute | solution.py:29
  407.7 21.5 %collective-permute-start.62 = (bf16[320,1536]{1,0:T(8,128)(2,1)}, bf16[320,1536]{1,0:T(8,128)(2,1)S(1)}, u32[]{:S(2)}, u32[]{:S(2)}) collective-permute-start(bf16[320,1536]{1,0:T(8,128)(2,1)} %add_convert_fusion.4), channel_id=1, source_target_pairs={{0,1},{1,0},{2,10},{3,11},{4,5},{5,4},{6,14},{7,15},{8,9},{9,8},{1... | collective-permute-start | bytes 2949128 | tf_op jit(solution)/shard_map/ppermute | solution.py:40
  472.5 22.9 %collective-permute-start.71 = (bf16[320,1536]{1,0:T(8,128)(2,1)}, bf16[320,1536]{1,0:T(8,128)(2,1)}, u32[]{:S(2)}, u32[]{:S(2)}) collective-permute-start(bf16[320,1536]{1,0:T(8,128)(2,1)} %slice.341), channel_id=1, source_target_pairs={{0,8},{1,9},{2,3},{3,2},{4,12},{5,13},{6,7},{7,6},{8,0},{9,1},{10,... | collective-permute-start | bytes 2949128 | tf_op jit(solution)/shard_map/ppermute | solution.py:40
  474.6 20.8 %collective-permute-start.73 = (bf16[4,96,1152]{2,1,0:T(8,128)(2,1)}, bf16[4,96,1152]{2,1,0:T(8,128)(2,1)}, u32[]{:S(2)}, u32[]{:S(2)}) collective-permute-start(bf16[4,96,1152]{2,1,0:T(8,128)(2,1)} %get-tuple-element.717), channel_id=1, source_target_pairs={{0,4},{2,6},{4,0},{6,2},{8,12},{10,14},{12,8},{14,10},{16,20},{18,... | collective-permute-start | bytes 2654216 | tf_op jit(solution)/shard_map/ppermute | solution.py:29
  528.2 28.4 %collective-permute-start.82 = (bf16[320,1536]{1,0:T(8,128)(2,1)}, bf16[320,1536]{1,0:T(8,128)(2,1)}, u32[]{:S(2)}, u32[]{:S(2)}) collective-permute-start(bf16[320,1536]{1,0:T(8,128)(2,1)} %add_convert_fusion.3), channel_id=1, source_target_pairs={{0,1},{1,0},{2,10},{3,11},{4,5},{5,4},{6,14},{7,15},{8,9},{9,8},{1... | collective-permute-start | bytes 2949128 | tf_op jit(solution)/shard_map/ppermute | solution.py:40
  529.5 27.1 %collective-permute-start.80 = (bf16[4,96,1152]{2,1,0:T(8,128)(2,1)}, bf16[4,96,1152]{2,1,0:T(8,128)(2,1)}, u32[]{:S(2)}, u32[]{:S(2)}) collective-permute-start(bf16[4,96,1152]{2,1,0:T(8,128)(2,1)} %get-tuple-element.773), channel_id=1, source_target_pairs={{0,4},{2,6},{4,0},{6,2},{8,12},{10,14},{12,8},{14,10},{16,20},{18,... | collective-permute-start | bytes 2654216 | tf_op jit(solution)/shard_map/ppermute | solution.py:29
  530.5 26.1 %collective-permute-start.81 = (bf16[2,2,96,768]{3,2,1,0:T(8,128)(2,1)}, bf16[2,2,96,768]{3,2,1,0:T(8,128)(2,1)}, u32[]{:S(2)}, u32[]{:S(2)}) collective-permute-start(bf16[2,2,96,768]{3,2,1,0:T(8,128)(2,1)} %fusion.12), channel_id=1, source_target_pairs={{0,8},{1,9},{2,3},{3,2},{4,12},{5,13},{6,7},{7,6},{8,0},{9,1},{10,... | collective-permute-start | bytes 1769480 | tf_op jit(solution)/shard_map/ppermute | solution.py:40
  532.3 23.4 %collective-permute-start.79 = (bf16[2,96,1152]{2,1,0:T(8,128)(2,1)S(1)}, bf16[2,96,1152]{2,1,0:T(8,128)(2,1)}, u32[]{:S(2)}, u32[]{:S(2)}) collective-permute-start(bf16[2,96,1152]{2,1,0:T(8,128)(2,1)S(1)} %slice.352), channel_id=1, source_target_pairs={{0,16},{2,18},{4,20},{6,22},{8,24},{10,26},{12,28},{14,30},{16,0},... | collective-permute-start | bytes 1327112 | tf_op jit(solution)/shard_map/ppermute | solution.py:29
  556.6 22.2 %collective-permute-start.83 = (bf16[2,2,2,96,1024]{4,3,2,1,0:T(8,128)(2,1)}, bf16[2,2,2,96,1024]{4,3,2,1,0:T(8,128)(2,1)}, u32[]{:S(2)}, u32[]{:S(2)}) collective-permute-start(bf16[2,2,2,96,1024]{4,3,2,1,0:T(8,128)(2,1)} %get-tuple-element.781), channel_id=1, source_target_pairs={{0,1},{1,0},{2,6},{3,7},{4,5},{5,4},{6,2},{7,3},{8,9},{9,8},{10,14... | collective-permute-start | bytes 4718600 | tf_op jit(solution)/shard_map/ppermute | solution.py:40
  (163 other events, 2036.2 us)
